TPU v7x, 32 devices: a whole 2x2x4 slice. The times are simulated.
32 devices in a mesh: rows: 16 (over z, x, core), cols: 2 (over y).
Axes of the slice: x: 2, y: 2, z: 4, core: 2. Of those that a mesh axis runs over, the one named last changes fastest.
Arguments:
- tokens: bfloat16 [2, 128, 128, 768], P(None, 'rows', 'cols'), may hold values from -6 to 6
- region_sizes: int32 [2, 2], replicated, may hold values from 64 to 128, as said below
- region_starts: int32 [2], replicated, may hold values from 0 to 127
- entry_gain: float32 [768], replicated, may hold values from 0.1 to 1.9
- entry_shift: float32 [768], replicated, may hold values from -1.75 to 1.75
- spectral_kernel: bfloat16 [2, 8, 96, 96], replicated, may hold values from -0.4375 to 0.4375
- spectral_bias: float32 [2, 8, 96], replicated, may hold values from -3 to 3
- spectral_mixer: bfloat16 [2, 8, 96, 96], replicated, may hold values from -0.4375 to 0.4375
- spectral_offset: float32 [2, 8, 96], replicated, may hold values from -1.75 to 1.75
- exit_scale: float32 [768], replicated, may hold values from 0.1 to 1.9
- exit_center: float32 [768], replicated, may hold values from -1.75 to 1.75
- dense_expand: bfloat16 [768, 3072], replicated, may hold values from -0.21875 to 0.21875
- dense_lift: float32 [3072], replicated, may hold values from -1.75 to 1.75
- dense_project: bfloat16 [3072, 768], replicated, may hold values from -0.15625 to 0.15625
- dense_return: float32 [768], replicated, may hold values from -1.75 to 1.75
- cotangent: bfloat16 [2, 128, 128, 768], P(None, 'rows', 'cols'), may hold values from -6 to 6
Outputs:
- output: bfloat16 [2, 128, 128, 768], P(None, 'rows', 'cols')
- gradient_tokens: float32 [2, 128, 128, 768], P(None, 'rows', 'cols')
- gradient_gain: float32 [768], replicated
- gradient_shift: float32 [768], replicated
- gradient_kernel: float32 [2, 8, 96, 96], replicated
- gradient_bias: float32 [2, 8, 96], replicated
- gradient_mixer: float32 [2, 8, 96, 96], replicated
- gradient_offset: float32 [2, 8, 96], replicated
- gradient_scale: float32 [768], replicated
- gradient_center: float32 [768], replicated
- gradient_expand: float32 [768, 3072], replicated
- gradient_lift: float32 [3072], replicated
- gradient_project: float32 [3072, 768], replicated
- gradient_return: float32 [768], replicated
Inputs may be any that keep to these rules, and one draw needn't show every extreme that they name: `region_sizes`: each region's valid rows number 128 // 2 to 128 and its valid columns 64 to 128; in every draw one region is the whole grid, 128 rows by 128 columns, and another has exactly 64 valid rows.
All inputs are finite; a program needn't handle non-finite values.
Results may differ from a plain program's by a relative error of at most 0.018.
The roundings to bfloat16 on the way count: a program that leaves them out, or rounds other values in their place, can miss the bound.
Values may be sent and summed in bfloat16 or wider, within the bound.
A program may use at most 192 MiB of HBM per device.

v0:
```python
import math

import jax
import jax.numpy as jnp
from jax import lax
from jax.sharding import PartitionSpec as P

shrink_width = 0.01
norm_eps = 1e-06
highest = lax.Precision.HIGHEST


def tables(height, width, modes):
    column = jnp.arange(width, dtype=jnp.int32)
    frequency = jnp.arange(modes, dtype=jnp.int32)
    turns = column[:, None] * frequency[None, :] % width
    angle = turns.astype(jnp.float32) * (2.0 * math.pi / width)
    cosine = jnp.cos(angle)
    sine = jnp.sin(angle)
    scale = 1.0 / math.sqrt(width)
    forward_zonal = jnp.stack([cosine, -sine], 1) * scale
    factor = jnp.where(frequency == 0, 1.0, 2.0).astype(jnp.float32)
    inverse_zonal = jnp.stack([cosine.T * factor[:, None], -sine.T * factor[:, None]], 0) * scale
    latitude = jnp.arange(height, dtype=jnp.int32)
    meridian_turns = latitude[:, None] * latitude[None, :] % height
    meridian_angle = meridian_turns.astype(jnp.float32) * (2.0 * math.pi / height)
    meridian_cos = jnp.cos(meridian_angle) / math.sqrt(height)
    meridian_sin = jnp.sin(meridian_angle) / math.sqrt(height)
    meridian_table = jnp.stack(
        [jnp.stack([meridian_cos, meridian_sin], -1), jnp.stack([-meridian_sin, meridian_cos], -1)],
        1,
    )
    forward_low = forward_zonal.astype(jnp.bfloat16)
    inverse_low = inverse_zonal.astype(jnp.bfloat16)
    meridian_low = meridian_table.astype(jnp.bfloat16)
    meridian_wide = meridian_low.astype(jnp.float32)
    return (forward_low, inverse_low, meridian_low, meridian_wide)


def layer_norm(value, gain, shift):
    centre = jnp.mean(value, -1, keepdims=True)
    centred = value - centre
    spread = jnp.mean(centred * centred, -1, keepdims=True)
    return centred * lax.rsqrt(spread + norm_eps) * gain + shift


def gelu_exact(value):
    return jax.nn.gelu(value, approximate=False)


def shrink(value):
    return value - shrink_width * jnp.tanh(value / shrink_width)


def block_layout(spectrum, blocks, block_size):
    leading = spectrum.shape[:3]
    parts = spectrum.reshape(leading + (2, blocks, block_size))
    parts = jnp.moveaxis(parts, 3, 4)
    return parts.reshape((-1, blocks, 2 * block_size))


def spectral_layout(modes_flat, leading, blocks, block_size):
    parts = modes_flat.reshape(leading + (blocks, 2, block_size))
    parts = jnp.moveaxis(parts, 4, 3)
    return parts.reshape(leading + (2, blocks * block_size))


def complex_matrix(weight):
    real = weight[0]
    imaginary = weight[1]
    upper = jnp.concatenate([real, imaginary], 2)
    lower = jnp.concatenate([-imaginary, real], 2)
    return jnp.concatenate([upper, lower], 1)


def matrix_gradient(whole, block_size):
    upper = whole[:, :block_size]
    lower = whole[:, block_size:]
    real = upper[:, :, :block_size] + lower[:, :, block_size:]
    imaginary = upper[:, :, block_size:] - lower[:, :, :block_size]
    return jnp.stack([real, imaginary], 0)


def bias_rows(bias):
    return jnp.moveaxis(bias, 0, 1).reshape(bias.shape[1], 2 * bias.shape[2])


def bias_gradient(summed, block_size):
    return jnp.moveaxis(summed.reshape(summed.shape[0], 2, block_size), 1, 0)


def advance(tokens, mask, weights, grids, layout):
    (
        entry_gain,
        entry_shift,
        spectral_kernel,
        spectral_bias,
        spectral_mixer,
        spectral_offset,
        exit_scale,
        exit_center,
        dense_expand,
        dense_lift,
        dense_project,
        dense_return,
    ) = weights
    forward_zonal, inverse_zonal, meridian_table, meridian_wide = grids
    blocks, block_size, first_block = layout
    residual = tokens.astype(jnp.float32)
    normed = layer_norm(residual, entry_gain, entry_shift)
    sent = (mask * normed).astype(jnp.bfloat16)
    by_channel = lax.all_to_all(sent, "cols", split_axis=3, concat_axis=2, tiled=True)
    zonal = jnp.einsum(
        "rhwc,wpk->rhkpc", by_channel, forward_zonal, preferred_element_type=jnp.float32
    )
    by_mode = lax.all_to_all(
        zonal.astype(jnp.bfloat16), "rows", split_axis=2, concat_axis=1, tiled=True
    )
    spectrum = jnp.einsum(
        "kphq,rhmqc->rkmpc", meridian_table, by_mode, preferred_element_type=jnp.float32
    ).astype(jnp.bfloat16)
    leading = spectrum.shape[:3]
    modes_flat = block_layout(spectrum, blocks, block_size)
    kernel_matrix = complex_matrix(
        lax.dynamic_slice_in_dim(spectral_kernel, first_block, blocks, 1)
    )
    mixer_matrix = complex_matrix(lax.dynamic_slice_in_dim(spectral_mixer, first_block, blocks, 1))
    kernel_bias = bias_rows(lax.dynamic_slice_in_dim(spectral_bias, first_block, blocks, 1))
    mixer_bias = bias_rows(lax.dynamic_slice_in_dim(spectral_offset, first_block, blocks, 1))
    first_pre = (
        jnp.einsum("nbx,bxy->nby", modes_flat, kernel_matrix, preferred_element_type=jnp.float32)
        + kernel_bias
    )
    first_act = gelu_exact(first_pre).astype(jnp.bfloat16)
    second_pre = (
        jnp.einsum("nbx,bxy->nby", first_act, mixer_matrix, preferred_element_type=jnp.float32)
        + mixer_bias
    )
    shrunk = spectral_layout(shrink(second_pre), leading, blocks, block_size)
    back_meridian = jnp.einsum(
        "kphq,rkmpc->rhmqc", meridian_wide, shrunk, precision=highest
    ).astype(jnp.bfloat16)
    by_row = lax.all_to_all(back_meridian, "rows", split_axis=1, concat_axis=2, tiled=True)
    filtered = jnp.einsum(
        "rhkpc,pkw->rhwc", by_row, inverse_zonal, preferred_element_type=jnp.float32
    ).astype(jnp.bfloat16)
    by_token = lax.all_to_all(filtered, "cols", split_axis=2, concat_axis=3, tiled=True)
    mixed = residual + mask * by_token.astype(jnp.float32) + normed
    features = mixed.shape[-1]
    second_norm = (
        layer_norm(mixed, exit_scale, exit_center).astype(jnp.bfloat16).reshape(-1, features)
    )
    hidden_pre = jnp.dot(second_norm, dense_expand, preferred_element_type=jnp.float32) + dense_lift
    hidden = gelu_exact(hidden_pre).astype(jnp.bfloat16)
    output = mixed + (
        jnp.dot(hidden, dense_project, preferred_element_type=jnp.float32) + dense_return
    ).reshape(mixed.shape)
    kept = (
        residual,
        modes_flat,
        first_pre,
        first_act,
        second_pre,
        mixed,
        second_norm,
        hidden_pre,
        hidden,
        kernel_matrix,
        mixer_matrix,
        leading,
    )
    return (output, kept)


def retreat(cotangent, mask, kept, weights, grids, layout):
    (
        entry_gain,
        entry_shift,
        spectral_kernel,
        spectral_bias,
        spectral_mixer,
        spectral_offset,
        exit_scale,
        exit_center,
        dense_expand,
        dense_lift,
        dense_project,
        dense_return,
    ) = weights
    forward_zonal, inverse_zonal, meridian_table, meridian_wide = grids
    blocks, block_size, first_block = layout
    (
        residual,
        modes_flat,
        first_pre,
        first_act,
        second_pre,
        mixed,
        second_norm,
        hidden_pre,
        hidden,
        kernel_matrix,
        mixer_matrix,
        leading,
    ) = kept
    features = mixed.shape[-1]
    upstream = cotangent.reshape(-1, features)
    gradient_project = jnp.einsum("tf,tc->fc", hidden, upstream, preferred_element_type=jnp.float32)
    gradient_return = jnp.sum(upstream.astype(jnp.float32), 0)
    outer = (gradient_project, gradient_return)
    hidden_back = jnp.einsum(
        "tc,fc->tf", upstream, dense_project, preferred_element_type=jnp.float32
    )
    hidden_pull = jax.vjp(gelu_exact, hidden_pre)[1]
    pre_back = hidden_pull(hidden_back)[0].astype(jnp.bfloat16)
    gradient_expand = jnp.einsum(
        "tc,tf->cf", second_norm, pre_back, preferred_element_type=jnp.float32
    )
    gradient_lift = jnp.sum(pre_back.astype(jnp.float32), 0)
    norm_back = jnp.einsum(
        "tf,cf->tc", pre_back, dense_expand, preferred_element_type=jnp.float32
    ).reshape(mixed.shape)
    exit_pull = jax.vjp(layer_norm, mixed, exit_scale, exit_center)[1]
    mixed_part, gradient_scale, gradient_center = exit_pull(norm_back)
    inner = (gradient_expand, gradient_lift, gradient_scale, gradient_center)
    mixed_back = cotangent.astype(jnp.float32) + mixed_part
    filter_back = (mask * mixed_back).astype(jnp.bfloat16)
    channel_back = lax.all_to_all(filter_back, "cols", split_axis=3, concat_axis=2, tiled=True)
    zonal_back = jnp.einsum(
        "rhwc,pkw->rhkpc", channel_back, inverse_zonal, preferred_element_type=jnp.float32
    ).astype(jnp.bfloat16)
    meridian_back = lax.all_to_all(zonal_back, "rows", split_axis=2, concat_axis=1, tiled=True)
    shrunk_back = jnp.einsum(
        "kphq,rhmqc->rkmpc", meridian_table, meridian_back, preferred_element_type=jnp.float32
    )
    shrink_pull = jax.vjp(shrink, second_pre)[1]
    second_back = shrink_pull(block_layout(shrunk_back, blocks, block_size))[0].astype(jnp.bfloat16)
    mixer_whole = jnp.einsum(
        "nbx,nby->bxy", first_act, second_back, preferred_element_type=jnp.float32
    )
    offset_rows = jnp.sum(second_back.astype(jnp.float32), 0)
    activation_back = jnp.einsum(
        "nby,bxy->nbx", second_back, mixer_matrix, preferred_element_type=jnp.float32
    )
    first_pull = jax.vjp(gelu_exact, first_pre)[1]
    first_back = first_pull(activation_back)[0].astype(jnp.bfloat16)
    kernel_whole = jnp.einsum(
        "nbx,nby->bxy", modes_flat, first_back, preferred_element_type=jnp.float32
    )
    kernel_rows = jnp.sum(first_back.astype(jnp.float32), 0)
    spectrum_back = spectral_layout(
        jnp.einsum("nby,bxy->nbx", first_back, kernel_matrix, preferred_element_type=jnp.float32),
        leading,
        blocks,
        block_size,
    )
    modes_back = jnp.einsum(
        "kphq,rkmpc->rhmqc", meridian_wide, spectrum_back, precision=highest
    ).astype(jnp.bfloat16)
    row_back = lax.all_to_all(modes_back, "rows", split_axis=1, concat_axis=2, tiled=True)
    sent_back = jnp.einsum(
        "rhkpc,wpk->rhwc", row_back, forward_zonal, preferred_element_type=jnp.float32
    ).astype(jnp.bfloat16)
    token_back = lax.all_to_all(sent_back, "cols", split_axis=2, concat_axis=3, tiled=True)
    normed_back = mixed_back + mask * token_back.astype(jnp.float32)
    entry_pull = jax.vjp(layer_norm, residual, entry_gain, entry_shift)[1]
    residual_part, gradient_gain, gradient_shift = entry_pull(normed_back)
    gradient_tokens = mixed_back + residual_part
    shared = (
        gradient_gain,
        gradient_shift,
        inner[2],
        inner[3],
        inner[0],
        inner[1],
        outer[0],
        outer[1],
    )
    local_blocks = (
        matrix_gradient(kernel_whole, block_size),
        bias_gradient(kernel_rows, block_size),
        matrix_gradient(mixer_whole, block_size),
        bias_gradient(offset_rows, block_size),
    )
    return (gradient_tokens, shared, local_blocks)


def shards(
    tokens,
    region_sizes,
    region_starts,
    entry_gain,
    entry_shift,
    spectral_kernel,
    spectral_bias,
    spectral_mixer,
    spectral_offset,
    exit_scale,
    exit_center,
    dense_expand,
    dense_lift,
    dense_project,
    dense_return,
    cotangent,
):
    rows_here = tokens.shape[1]
    cols_here = tokens.shape[2]
    height = rows_here * lax.axis_size("rows")
    width = cols_here * lax.axis_size("cols")
    grids = tables(height, width, width // 2)
    latitude = lax.axis_index("rows") * rows_here + jnp.arange(rows_here, dtype=jnp.int32)
    longitude = lax.axis_index("cols") * cols_here + jnp.arange(cols_here, dtype=jnp.int32)
    inside_rows = latitude[None, :, None] < region_sizes[:, 0][:, None, None]
    offset = (longitude[None, None, :] - region_starts[:, None, None]) % width
    inside_cols = offset < region_sizes[:, 1][:, None, None]
    mask = jnp.where(inside_rows & inside_cols, 1.0, 0.0).astype(jnp.float32)[..., None]
    block_size = spectral_kernel.shape[2]
    total_blocks = spectral_kernel.shape[1]
    blocks = tokens.shape[3] // lax.axis_size("cols") // block_size
    first_block = lax.axis_index("cols") * blocks
    layout = (blocks, block_size, first_block)
    weights = (
        entry_gain,
        entry_shift,
        spectral_kernel,
        spectral_bias,
        spectral_mixer,
        spectral_offset,
        exit_scale,
        exit_center,
        dense_expand,
        dense_lift,
        dense_project,
        dense_return,
    )
    output, kept = advance(tokens, mask, weights, grids, layout)
    replay, settled = lax.optimization_barrier((tokens, output))
    output = settled
    unused, kept = advance(replay, mask, weights, grids, layout)
    gradient_tokens, shared, local_blocks = retreat(cotangent, mask, kept, weights, grids, layout)
    (
        gain_part,
        shift_part,
        scale_part,
        center_part,
        expand_part,
        lift_part,
        project_part,
        return_part,
    ) = shared
    summed = lax.psum(
        (
            gain_part,
            shift_part,
            scale_part,
            center_part,
            expand_part,
            lift_part,
            project_part,
            return_part,
        ),
        ("rows", "cols"),
    )
    kernel_local, bias_local, mixer_local, offset_local = local_blocks
    kernel_full = lax.dynamic_update_slice_in_dim(
        jnp.zeros((2, total_blocks, block_size, block_size), jnp.float32),
        kernel_local,
        first_block,
        1,
    )
    bias_full = lax.dynamic_update_slice_in_dim(
        jnp.zeros((2, total_blocks, block_size), jnp.float32), bias_local, first_block, 1
    )
    mixer_full = lax.dynamic_update_slice_in_dim(
        jnp.zeros((2, total_blocks, block_size, block_size), jnp.float32),
        mixer_local,
        first_block,
        1,
    )
    offset_full = lax.dynamic_update_slice_in_dim(
        jnp.zeros((2, total_blocks, block_size), jnp.float32), offset_local, first_block, 1
    )
    block_totals = lax.psum((kernel_full, bias_full, mixer_full, offset_full), ("rows", "cols"))
    return (
        output.astype(jnp.bfloat16),
        gradient_tokens,
        summed[0],
        summed[1],
        block_totals[0],
        block_totals[1],
        block_totals[2],
        block_totals[3],
        summed[2],
        summed[3],
        summed[4],
        summed[5],
        summed[6],
        summed[7],
    )


def solution(mesh):
    placed = (
        P(None, "rows", "cols", None),
        P(),
        P(),
        P(),
        P(),
        P(),
        P(),
        P(),
        P(),
        P(),
        P(),
        P(),
        P(),
        P(),
        P(),
        P(None, "rows", "cols", None),
    )
    return jax.shard_map(
        shards,
        mesh=mesh,
        in_specs=placed,
        out_specs=(
            P(None, "rows", "cols", None),
            P(None, "rows", "cols", None),
            P(),
            P(),
            P(),
            P(),
            P(),
            P(),
            P(),
            P(),
            P(),
            P(),
            P(),
            P(),
        ),
        check_vma=False,
    )
```

profile of v0, /device:TPU:0, one launch (start us, length us, event | category | flops | bytes accessed | tf_op | source)
XLA Modules:
  0.0 1066.9 jit_solution(2714158382939266430)
XLA Ops:
  26.8 20.0 %all-to-all-done = bf16[2,2,196608]{2,1,0:T(2,128)(2,1)S(1)} async-done(((bf16[2,2,196608]{2,1,0:T(2,128)(2,1)}), bf16[2,2,196608]{2,1,0:T(2,128)(2,1)S(1)}, u32[]{:S(2)}, u32[]{:S(2)}) %all-to-all-start) | async-done | bytes 1572896 | tf_op jit(solution)/shard_map/all_to_all | solution.py:112
  70.6 24.5 %all-to-all-done.1 = bf16[2,8,64,2,384]{4,1,0,3,2:T(8,128)(2,1)S(1)} async-done(((bf16[2,8,64,2,384]{4,1,0,3,2:T(8,128)(2,1)}), bf16[2,8,64,2,384]{4,1,0,3,2:T(8,128)(2,1)S(1)}, u32[]{:S(2)}, u32[]{:S(2)}) %all-to-all-start.1) | async-done | bytes 1572896 | tf_op jit(solution)/shard_map/all_to_all | solution.py:116
  107.4 10.9 %bitcast_subtract_fusion.1 = f32[1024,4,192]{0,2,1:T(8,128)} fusion(f32[4,192]{1,0:T(4,128)S(1)} %add.308, bf16[1024,4,192]{2,0,1:T(8,128)(2,1)} %reshape.571, f32[4,192]{1,0:T(4,128)S(1)} %add.305, bf16[4,96,96]{1,2,0:T(8,128)(2,1)S(1)} %bitcast.520, bf16[4,96,96]{1,2,0:T(8,128)(2,1)S(1)} %copy-done.50, bf16[4,96,96]{1,2,0:T(8,128)(2,1)S(1)} %bitcast.514, ...), kind=kOutput, calls=%fused_computation.105 | convolution fusion | flops 661389312 | bytes 5167104 | tf_op jit(solution)/shard_map/nbx,bxy->nby/dot_general | solution.py:136
  142.5 9.6 all-to-all-start.2
  152.2 31.8 %all-to-all-done.2 = bf16[2,128,4,2,384]{4,3,2,0,1:T(2,128)(2,1)S(1)} async-done(((bf16[2,128,4,2,384]{4,3,2,0,1:T(2,128)(2,1)}), bf16[2,128,4,2,384]{4,3,2,0,1:T(2,128)(2,1)S(1)}, u32[]{:S(2)}, u32[]{:S(2)}) %all-to-all-start.2) | async-done | bytes 1572896 | tf_op jit(solution)/shard_map/all_to_all | solution.py:143
  191.0 22.9 %all_to_all.189 = bf16[2,8,128,384]{3,1,0,2:T(8,128)(2,1)S(1)} all-to-all(bf16[2,8,128,384]{3,1,0,2:T(8,128)(2,1)S(1)} %copy.213), channel_id=1, replica_groups=mesh['rows'=16,'cols'=2] {'cols'}, dimensions={2} | all-to-all | bytes 3145728 | tf_op jit(solution)/shard_map/all_to_all | solution.py:147
  229.3 39.3 %fusion.87 = f32[1024,768]{1,0:T(8,128)} fusion(bf16[3072,768]{1,0:T(8,128)(2,1)} %param.29, f32[3072]{0:T(1024)S(1)} %copy-done.75, bf16[1024,768]{1,0:T(8,128)(2,1)S(1)} %bitcast.510, bf16[768,3072]{1,0:T(8,128)(2,1)} %param.27, f32[768]{0:T(1024)S(1)} %copy-done.76), kind=kOutput, calls=%fused_computation.159 | convolution fusion | flops 9872080896 | bytes 14171136 | tf_op jit(solution)/shard_map/dot_general | solution.py:156
  283.9 22.9 %all_to_all.190 = bf16[2,2,196608]{2,1,0:T(2,128)(2,1)} all-to-all(bf16[2,2,196608]{2,1,0:T(2,128)(2,1)S(1)} %reshape.623), channel_id=1, replica_groups=mesh['rows'=16,'cols'=2] {'cols'}, dimensions={0} | all-to-all | bytes 3145728 | tf_op jit(solution)/shard_map/all_to_all | solution.py:112
  317.1 44.3 %all_to_all.191 = bf16[2,8,64,2,384]{4,1,0,3,2:T(8,128)(2,1)S(1)} all-to-all(bf16[2,8,64,2,384]{4,1,0,3,2:T(8,128)(2,1)S(1)} %copy.217), channel_id=1, replica_groups=mesh['rows'=16,'cols'=2] {'rows'}, dimensions={2} | all-to-all | bytes 3145728 | tf_op jit(solution)/shard_map/all_to_all | solution.py:116
  370.1 10.3 fusion.57
  412.1 40.9 %all_to_all.192 = bf16[2,128,4,2,384]{4,3,2,0,1:T(2,128)(2,1)S(1)} all-to-all(bf16[2,128,4,2,384]{4,3,2,0,1:T(2,128)(2,1)S(1)} %copy.226), channel_id=1, replica_groups=mesh['rows'=16,'cols'=2] {'rows'}, dimensions={1} | all-to-all | bytes 3145728 | tf_op jit(solution)/shard_map/all_to_all | solution.py:143
  463.7 20.4 %all-to-all-done.7 = bf16[2,8,128,384]{3,1,0,2:T(8,128)(2,1)S(1)} async-done(((bf16[2,8,128,384]{3,1,0,2:T(8,128)(2,1)}), bf16[2,8,128,384]{3,1,0,2:T(8,128)(2,1)S(1)}, u32[]{:S(2)}, u32[]{:S(2)}) %all-to-all-start.7) | async-done | bytes 1572896 | tf_op jit(solution)/shard_map/all_to_all | solution.py:147
  497.9 31.7 %fusion.3 = (f32[1024,3072]{1,0:T(8,128)}, f32[1024,3072]{1,0:T(8,128)}) fusion(f32[3072]{0:T(1024)S(1)} %copy-done.75, bf16[1024,768]{1,0:T(8,128)(2,1)S(1)} %bitcast.508, bf16[768,3072]{1,0:T(8,128)(2,1)S(1)} %bitcast.526), kind=kOutput, calls=%fused_computation.5 | convolution fusion | flops 5030019072 | bytes 31469568 | tf_op jit(solution)/shard_map/dot_general | solution.py:153
  529.6 16.7 %convert_reduce_fusion = (f32[3072]{0:T(1024)S(1)}, bf16[1024,3072]{1,0:T(8,128)(2,1)}) fusion(f32[1024,3072]{1,0:T(8,128)} %get-tuple-element.75, bf16[1024,768]{1,0:T(8,128)(2,1)S(1)} %bitcast.474, bf16[3072,768]{1,0:T(8,128)(2,1)} %param.29, f32[1024,3072]{1,0:T(8,128)} %get-tuple-element.76, f32[3072]{0:T(1024)S(1)} %copy-done.75), kind=kOutput, calls=%fused_computation.7 | convolution fusion | flops 4885312512 | bytes 37773312 | tf_op jit(solution)/shard_map/tc,fc->tf/dot_general | solution.py:211
  546.4 8.8 fusion.218
  572.6 22.9 %all_to_all.193 = bf16[2,2,196608]{2,1,0:T(2,128)(2,1)} all-to-all(bf16[2,2,196608]{2,1,0:T(2,128)(2,1)S(1)} %reshape.625), channel_id=1, replica_groups=mesh['rows'=16,'cols'=2] {'cols'}, dimensions={0} | all-to-all | bytes 3145728 | tf_op jit(solution)/shard_map/all_to_all | solution.py:228
  613.4 10.0 fusion.221
  623.5 20.6 %fusion.16 = f32[3072,768]{1,0:T(8,128)} fusion(bf16[1024,768]{1,0:T(8,128)(2,1)S(1)} %bitcast.475, f32[1024,3072]{1,0:T(8,128)} %get-tuple-element.75, f32[1024,3072]{1,0:T(8,128)} %get-tuple-element.76, f32[3072]{0:T(1024)S(1)} %copy-done.75), kind=kOutput, calls=%fused_computation.37 | convolution fusion | flops 4844421120 | bytes 36188160 | tf_op jit(solution)/shard_map/tf,tc->fc/dot_general | solution.py:208
  695.2 7.0 copy.243
  712.6 65.2 %all_to_all.194 = bf16[2,128,4,2,384]{4,3,2,0,1:T(2,128)(2,1)S(1)} all-to-all(bf16[2,128,4,2,384]{4,3,2,0,1:T(2,128)(2,1)S(1)} %copy.245), channel_id=1, replica_groups=mesh['rows'=16,'cols'=2] {'rows'}, dimensions={1} | all-to-all | bytes 3145728 | tf_op jit(solution)/shard_map/all_to_all | solution.py:260
  789.9 23.4 %all-to-all-done.11 = bf16[2,8,128,384]{3,1,0,2:T(8,128)(2,1)S(1)} async-done(((bf16[2,8,128,384]{3,1,0,2:T(8,128)(2,1)}), bf16[2,8,128,384]{3,1,0,2:T(8,128)(2,1)S(1)}, u32[]{:S(2)}, u32[]{:S(2)}) %all-to-all-start.11) | async-done | bytes 1572896 | tf_op jit(solution)/shard_map/all_to_all | solution.py:264
  829.7 42.9 %all-reduce = (f32[768]{0:T(1024)}, f32[768]{0:T(1024)}, f32[2,8,96]{2,1,0:T(8,128)}, f32[2,8,96]{2,1,0:T(8,128)}, f32[768]{0:T(1024)}, /*index=5*/f32[768]{0:T(1024)}, f32[3072]{0:T(1024)}, f32[768]{0:T(1024)}) all-reduce(f32[768]{0:T(1024)S(1)} %get-tuple-element.32, ...), channel_id=1, replica_groups=mesh['rows'=16,'cols'=2] {'rows','cols'}, use_global_device_ids=true, to_apply=%region_13.14 | all-reduce | flops 9984 | bytes 79872 | tf_op jit(solution)/shard_map/psum | solution.py:351
  878.7 164.1 %all-reduce.4.cloned.1.call-done = (f32[2,8,96,96]{3,2,1,0:T(8,128)}, f32[2,8,96,96]{3,2,1,0:T(8,128)}, f32[768,3072]{1,0:T(8,128)}, f32[3072,768]{1,0:T(8,128)}) async-done(((f32[2,8,96,96]{3,2,1,0:T(8,128)}, f32[2,8,96,96]{3,2,1,0:T(8,128)}, f32[768,3072]{1,0:T(8,128)}, f32[3072,768]{1,0:T(8,128)}), (f32[2,8,96,96]{3,2,1,0:T(8,128)}, f32[2,8,96,96]{3,2,1,0:T(8,128)}, f32[768,3072]{1,0:T(8,128)}, ...) | async-done | bytes 20054032 | tf_op jit(solution)/shard_map/psum | solution.py:383
  1047.1 8.8 copy.339
  (317 shorter events, 331.1 us)
Async XLA Ops:
  11.5 481.6 %copy-start.21 = (f32[2,8,64]{2,1,0:T(8,128)}, f32[2,8,64]{2,1,0:T(8,128)S(1)}, u32[]{:S(2)}) copy-start(f32[2,8,64]{2,1,0:T(8,128)S(1)} %get-tuple-element.88) | copy-start | bytes 12292
  22.4 24.4 %all-to-all-start = ((bf16[2,2,196608]{2,1,0:T(2,128)(2,1)}), bf16[2,2,196608]{2,1,0:T(2,128)(2,1)S(1)}, u32[]{:S(2)}, u32[]{:S(2)}) async-start(bf16[2,2,196608]{2,1,0:T(2,128)(2,1)} %reshape.621), calls=%async_computation | async-start | bytes 3145728 | tf_op jit(solution)/shard_map/all_to_all | solution.py:112
  26.8 27.3 %copy-start.23 = (f32[128,1,64]{0,2,1:T(8,128)}, f32[128,1,64]{0,2,1:T(8,128)S(1)}, u32[]{:S(2)}) copy-start(f32[128,1,64]{0,2,1:T(8,128)S(1)} %get-tuple-element.89) | copy-start | bytes 98308
  26.8 27.3 %copy-start.26 = (f32[128,1,64]{0,2,1:T(8,128)}, f32[128,1,64]{0,2,1:T(8,128)S(1)}, u32[]{:S(2)}) copy-start(f32[128,1,64]{0,2,1:T(8,128)S(1)} %get-tuple-element.90) | copy-start | bytes 98308
  56.7 38.5 %all-to-all-start.1 = ((bf16[2,8,64,2,384]{4,1,0,3,2:T(8,128)(2,1)}), bf16[2,8,64,2,384]{4,1,0,3,2:T(8,128)(2,1)S(1)}, u32[]{:S(2)}, u32[]{:S(2)}) async-start(bf16[2,8,64,2,384]{4,1,0,3,2:T(8,128)(2,1)} %copy.199), calls=%async_computation.1 | async-start | bytes 3145728 | tf_op jit(solution)/shard_map/all_to_all | solution.py:116
  65.0 305.0 %copy-start.19 = (bf16[1,4,96,96]{2,3,1,0:T(8,128)(2,1)}, bf16[1,4,96,96]{2,3,1,0:T(8,128)(2,1)S(1)}, u32[]{:S(2)}) copy-start(bf16[1,4,96,96]{2,3,1,0:T(8,128)(2,1)S(1)} %copy.301) | copy-start | bytes 221188
  66.1 41.3 %copy-start.16 = (bf16[1,4,96,96]{2,3,1,0:T(8,128)(2,1)}, bf16[1,4,96,96]{2,3,1,0:T(8,128)(2,1)S(1)}, u32[]{:S(2)}) copy-start(bf16[1,4,96,96]{2,3,1,0:T(8,128)(2,1)S(1)} %copy.298) | copy-start | bytes 221188
  68.6 301.5 %copy-start.70 = (f32[4,192]{1,0:T(4,128)}, f32[4,192]{1,0:T(4,128)S(1)}, u32[]{:S(2)}) copy-start(f32[4,192]{1,0:T(4,128)S(1)} %add.305) | copy-start | bytes 9220
  68.7 38.7 %copy-start.64 = (f32[4,192]{1,0:T(4,128)}, f32[4,192]{1,0:T(4,128)S(1)}, u32[]{:S(2)}) copy-start(f32[4,192]{1,0:T(4,128)S(1)} %add.308) | copy-start | bytes 9220
  69.3 332.7 %copy-start.11 = (bf16[128,1,128,2]{2,0,3,1:T(8,128)(2,1)}, bf16[128,1,128,2]{2,0,3,1:T(8,128)(2,1)S(1)}, u32[]{:S(2)}) copy-start(bf16[128,1,128,2]{2,0,3,1:T(8,128)(2,1)S(1)} %get-tuple-element.68) | copy-start | bytes 196612
  69.3 332.6 %copy-start.13 = (bf16[128,1,128,2]{2,0,3,1:T(8,128)(2,1)}, bf16[128,1,128,2]{2,0,3,1:T(8,128)(2,1)S(1)}, u32[]{:S(2)}) copy-start(bf16[128,1,128,2]{2,0,3,1:T(8,128)(2,1)S(1)} %get-tuple-element.69) | copy-start | bytes 196612
  142.5 41.5 %all-to-all-start.2 = ((bf16[2,128,4,2,384]{4,3,2,0,1:T(2,128)(2,1)}), bf16[2,128,4,2,384]{4,3,2,0,1:T(2,128)(2,1)S(1)}, u32[]{:S(2)}, u32[]{:S(2)}) async-start(bf16[2,128,4,2,384]{4,3,2,0,1:T(2,128)(2,1)} %copy.210), calls=%async_computation.2 | async-start | bytes 3145728 | tf_op jit(solution)/shard_map/all_to_all | solution.py:143
  152.2 37.3 %copy-start.29 = (f32[1,64,128]{2,1,0:T(8,128)}, f32[1,64,128]{2,1,0:T(8,128)S(1)}, u32[]{:S(2)}) copy-start(f32[1,64,128]{2,1,0:T(8,128)S(1)} %get-tuple-element.70) | copy-start | bytes 98308
  152.2 37.3 %copy-start.32 = (f32[1,64,128]{2,1,0:T(8,128)}, f32[1,64,128]{2,1,0:T(8,128)S(1)}, u32[]{:S(2)}) copy-start(f32[1,64,128]{2,1,0:T(8,128)S(1)} %get-tuple-element.71) | copy-start | bytes 98308
  273.2 219.8 %copy-start.37 = (f32[2,8,64]{2,1,0:T(8,128)}, f32[2,8,64]{2,1,0:T(8,128)S(1)}, u32[]{:S(2)}) copy-start(f32[2,8,64]{2,1,0:T(8,128)S(1)} %broadcast_multiply_fusion.1) | copy-start | bytes 12292
  273.8 219.2 %copy-start.54 = (f32[2,8,64]{2,1,0:T(8,128)}, f32[2,8,64]{2,1,0:T(8,128)S(1)}, u32[]{:S(2)}) copy-start(f32[2,8,64]{2,1,0:T(8,128)S(1)} %fusion.139) | copy-start | bytes 12292
  460.0 24.1 %all-to-all-start.7 = ((bf16[2,8,128,384]{3,1,0,2:T(8,128)(2,1)}), bf16[2,8,128,384]{3,1,0,2:T(8,128)(2,1)S(1)}, u32[]{:S(2)}, u32[]{:S(2)}) async-start(bf16[2,8,128,384]{3,1,0,2:T(8,128)(2,1)} %copy.229), calls=%async_computation.7 | async-start | bytes 3145728 | tf_op jit(solution)/shard_map/all_to_all | solution.py:147
  497.3 32.4 %copy-start.52 = (f32[2,8,64]{2,1,0:T(8,128)}, f32[2,8,64]{2,1,0:T(8,128)S(1)}, u32[]{:S(2)}) copy-start(f32[2,8,64]{2,1,0:T(8,128)S(1)} %fusion.140) | copy-start | bytes 12292
  497.9 31.8 %copy-start.15 = (bf16[2,8,64,768]{3,2,1,0:T(8,128)(2,1)}, bf16[2,8,64,768]{3,2,1,0:T(8,128)(2,1)S(1)}, u32[]{:S(2)}) copy-start(bf16[2,8,64,768]{3,2,1,0:T(8,128)(2,1)S(1)} %add_convert_fusion.2) | copy-start | bytes 4718596
  497.9 31.7 %copy-start.7 = (bf16[2,8,64,768]{3,2,1,0:T(8,128)(2,1)S(1)}, bf16[2,8,64,768]{3,2,1,0:T(8,128)(2,1)}, u32[]{:S(2)}) copy-start(bf16[2,8,64,768]{3,2,1,0:T(8,128)(2,1)} %param.31) | copy-start | bytes 4718596
  609.3 36.1 %all-to-all-start.9 = ((bf16[2,8,64,2,384]{4,1,0,3,2:T(8,128)(2,1)}), bf16[2,8,64,2,384]{4,1,0,3,2:T(8,128)(2,1)S(1)}, u32[]{:S(2)}, u32[]{:S(2)}) async-start(bf16[2,8,64,2,384]{4,1,0,3,2:T(8,128)(2,1)} %copy.233), calls=%async_computation.9 | async-start | bytes 3145728 | tf_op jit(solution)/shard_map/all_to_all | solution.py:232
  613.4 429.4 %all-reduce.4.cloned.1.call-start = ((), (), s32[]{:S(2)}) async-start(), calls=%async_computation.12 | async-start | bytes 40894464 | tf_op jit(solution)/shard_map/psum | solution.py:383
  623.5 21.9 %copy-start.14 = (bf16[128,1,128,2]{2,0,3,1:T(8,128)(2,1)S(1)}, bf16[128,1,128,2]{2,0,3,1:T(8,128)(2,1)}, u32[]{:S(2)}) copy-start(bf16[128,1,128,2]{2,0,3,1:T(8,128)(2,1)} %copy-done.13) | copy-start | bytes 196612
  786.0 27.3 %all-to-all-start.11 = ((bf16[2,8,128,384]{3,1,0,2:T(8,128)(2,1)}), bf16[2,8,128,384]{3,1,0,2:T(8,128)(2,1)S(1)}, u32[]{:S(2)}, u32[]{:S(2)}) async-start(bf16[2,8,128,384]{3,1,0,2:T(8,128)(2,1)} %copy.248), calls=%async_computation.11 | async-start | bytes 3145728 | tf_op jit(solution)/shard_map/all_to_all | solution.py:264
  (67 other events, 348.1 us)
Sparse Core Ops, SparseCore 0:
  679.7 363.0 all-reduce.3
where the time goes:
time: 1080 us; the launch traced here: 1070 us
  waiting for transfers between devices  285 us (26%)
  blocking collectives  262 us (24%)
  local copies, waits for them, and re-layouts  232 us (21%)
  matrix products  186 us (17%)
  other arithmetic  53.6 us (5%)
  starting transfers between devices  31.8 us (3%)
  between operations  15.8 us (1%)
    psum x1, waiting for transfers between devices, shards(): lax.psum((kernel_full, bias_full, mixer_full, offset_full), ('rows', 'col...  164 us
    all_to_all x1, blocking collectives, retreat(): lax.all_to_all(modes_back, 'rows', split_axis=1, concat_axis=2, tiled=True)  65.2 us
    unnamed x182, local copies, waits for them, and re-layouts  50 us
    all_to_all x1, blocking collectives, advance(): lax.all_to_all(zonal.astype(jnp.bfloat16), 'rows', split_axis=2, concat_a...  44.3 us
    psum x1, blocking collectives, shards(): lax.psum((gain_part, shift_part, scale_part, center_part, expand_part, li...  42.9 us
    all_to_all x1, blocking collectives, advance(): lax.all_to_all(back_meridian, 'rows', split_axis=1, concat_axis=2, tiled=...  40.9 us
    dot_general x1, matrix products, advance(): jnp.dot(hidden, dense_project, preferred_element_type=jnp.float32)  39.3 us
    all_to_all x1, waiting for transfers between devices, advance(): lax.all_to_all(back_meridian, 'rows', split_axis=1, concat_axis=2, tiled=...  31.8 us
  transfers between devices with their start and end apart: 7, of which 7 were waited for; matrix products, arithmetic and copies ran while one was open for 9% of the time, Pallas kernels for 0%

commit v1 on v0

--- a/solution.py
+++ b/solution.py
@@ -334,9 +334,6 @@
         dense_return,
     )
     output, kept = advance(tokens, mask, weights, grids, layout)
-    replay, settled = lax.optimization_barrier((tokens, output))
-    output = settled
-    unused, kept = advance(replay, mask, weights, grids, layout)
     gradient_tokens, shared, local_blocks = retreat(cotangent, mask, kept, weights, grids, layout)
     (
         gain_part,
@@ -348,19 +345,16 @@
         project_part,
         return_part,
     ) = shared
-    summed = lax.psum(
-        (
-            gain_part,
-            shift_part,
-            scale_part,
-            center_part,
-            expand_part,
-            lift_part,
-            project_part,
-            return_part,
-        ),
-        ("rows", "cols"),
-    )
+    everywhere = ("rows", "cols")
+    project_sum = lax.psum(project_part.astype(jnp.bfloat16), everywhere).astype(jnp.float32)
+    expand_sum = lax.psum(expand_part.astype(jnp.bfloat16), everywhere).astype(jnp.float32)
+    vectors = (gain_part, shift_part, scale_part, center_part, lift_part, return_part)
+    sums = lax.psum(jnp.concatenate(vectors), everywhere)
+    ends = [0]
+    for vector in vectors:
+        ends.append(ends[-1] + vector.shape[0])
+    parts = [sums[low:high] for low, high in zip(ends[:-1], ends[1:])]
+    summed = (*parts[:4], expand_sum, parts[4], project_sum, parts[5])
     kernel_local, bias_local, mixer_local, offset_local = local_blocks
     kernel_full = lax.dynamic_update_slice_in_dim(
         jnp.zeros((2, total_blocks, block_size, block_size), jnp.float32),

time: 1080 us -> 764 us (0.71)
  blocking collectives: 262 us -> 65.7 us
  local copies, waits for them, and re-layouts: 232 us -> 168 us
  matrix products: 186 us -> 129 us
  starting transfers between devices: 31.8 us -> 53.2 us
  waiting for transfers between devices: 285 us -> 270 us
    all_to_all x5 -> x0, blocking collectives: 196 us -> none  [the longest x1 65.2 us: retreat(): lax.all_to_all(modes_back, 'rows', split_axis=1, concat_axis=2, tiled=True)]
    psum x1, waiting for transfers between devices: 164 us -> 63.5 us  [shards(): lax.psum((kernel_full, bias_full, mixer_full, offset_full), ('rows', 'col...]
    psum x0 -> x1, waiting for transfers between devices: none -> 62.8 us  [shards(): lax.psum(expand_part.astype(jnp.bfloat16), everywhere).astype(jnp.float32)]
    dot_general x1, matrix products: 39.3 us -> 5.04 us  [advance(): jnp.dot(hidden, dense_project, preferred_element_type=jnp.float32)]
    all_to_all x0 -> x1, waiting for transfers between devices: none -> 32.7 us  [retreat(): lax.all_to_all(modes_back, 'rows', split_axis=1, concat_axis=2, tiled=True)]
    all_to_all x1, waiting for transfers between devices: 23.4 us -> 0.01 us  [retreat(): lax.all_to_all(sent_back, 'cols', split_axis=2, concat_axis=3, tiled=True)]
    unnamed x182 -> x163, local copies, waits for them, and re-layouts: 50 us -> 31.2 us
    all_to_all x0 -> x1, starting transfers between devices: none -> 16.5 us  [retreat(): lax.all_to_all(modes_back, 'rows', split_axis=1, concat_axis=2, tiled=True)]
  transfers between devices with their start and end apart: 7 -> 9, of which waited for: 7 -> 8; matrix products, arithmetic and copies ran while one was open for 9% -> 19% of each run, Pallas kernels for 0% -> 0%
where the time goes in v1:
time: 764 us; the launch traced here: 750 us
  waiting for transfers between devices  270 us (35%)
  local copies, waits for them, and re-layouts  168 us (22%)
  matrix products  129 us (17%)
  blocking collectives  65.7 us (9%)
  starting transfers between devices  53.2 us (7%)
  other arithmetic  48.8 us (6%)
  between operations  15.3 us (2%)
    psum x1, waiting for transfers between devices, shards(): lax.psum((kernel_full, bias_full, mixer_full, offset_full), ('rows', 'col...  63.5 us
    psum x1, waiting for transfers between devices, shards(): lax.psum(expand_part.astype(jnp.bfloat16), everywhere).astype(jnp.float32)  62.8 us
    psum x1, blocking collectives, shards(): sums = lax.psum(jnp.concatenate(vectors), everywhere)  40.9 us
    dot_general x1, matrix products, advance(): jnp.dot(second_norm, dense_expand, preferred_element_type=jnp.float32)  35.9 us
    all_to_all x1, waiting for transfers between devices, retreat(): lax.all_to_all(modes_back, 'rows', split_axis=1, concat_axis=2, tiled=True)  32.7 us
    all_to_all x1, waiting for transfers between devices, advance(): lax.all_to_all(back_meridian, 'rows', split_axis=1, concat_axis=2, tiled=...  31.8 us
    unnamed x163, local copies, waits for them, and re-layouts  31.2 us
    all_to_all x1, blocking collectives, retreat(): lax.all_to_all(filter_back, 'cols', split_axis=3, concat_axis=2, tiled=True)  24.9 us
  transfers between devices with their start and end apart: 9, of which 8 were waited for; matrix products, arithmetic and copies ran while one was open for 19% of the time, Pallas kernels for 0%

profile of v1, /device:TPU:0, one launch (start us, length us, event | category | flops | bytes accessed | tf_op | source)
XLA Modules:
  0.0 750.0 jit_solution(1651908399821355314)
XLA Ops:
  26.9 20.0 %all-to-all-done = bf16[2,2,196608]{2,1,0:T(2,128)(2,1)S(1)} async-done(((bf16[2,2,196608]{2,1,0:T(2,128)(2,1)}), bf16[2,2,196608]{2,1,0:T(2,128)(2,1)S(1)}, u32[]{:S(2)}, u32[]{:S(2)}) %all-to-all-start) | async-done | bytes 1572896 | tf_op jit(solution)/shard_map/all_to_all | solution.py:112
  70.5 24.6 %all-to-all-done.1 = bf16[2,8,64,2,384]{4,1,0,3,2:T(8,128)(2,1)S(1)} async-done(((bf16[2,8,64,2,384]{4,1,0,3,2:T(8,128)(2,1)}), bf16[2,8,64,2,384]{4,1,0,3,2:T(8,128)(2,1)S(1)}, u32[]{:S(2)}, u32[]{:S(2)}) %all-to-all-start.1) | async-done | bytes 1572896 | tf_op jit(solution)/shard_map/all_to_all | solution.py:116
  107.4 10.3 %fusion.29 = (bf16[1024,4,192]{0,2,1:T(8,128)(2,1)S(1)}, f32[1024,4,192]{0,2,1:T(8,128)}, f32[4,192,1024]{2,1,0:T(8,128)}) fusion(f32[4,192]{1,0:T(4,128)S(1)} %add.235, bf16[1024,4,192]{2,0,1:T(8,128)(2,1)} %reshape.528, bf16[4,96,96]{1,2,0:T(8,128)(2,1)S(1)} %bitcast.342, bf16[4,96,96]{1,2,0:T(8,128)(2,1)S(1)} %copy-done.30, ...), kind=kOutput, calls=%fused_computation.64 | convolution fusion | flops 355074048 | bytes 9661440 | tf_op jit(solution)/shard_map/nbx,bxy->nby/dot_general | solution.py:131
  132.2 7.0 copy.166
  145.5 9.5 %all-to-all-start.2 = ((bf16[2,128,4,2,384]{4,3,2,0,1:T(2,128)(2,1)}), bf16[2,128,4,2,384]{4,3,2,0,1:T(2,128)(2,1)S(1)}, u32[]{:S(2)}, u32[]{:S(2)}) async-start(bf16[2,128,4,2,384]{4,3,2,0,1:T(2,128)(2,1)} %copy.168), calls=%async_computation.2 | async-start | bytes 3145728 | tf_op jit(solution)/shard_map/all_to_all | solution.py:143
  155.2 31.8 %all-to-all-done.2 = bf16[2,128,4,2,384]{4,3,2,0,1:T(2,128)(2,1)S(1)} async-done(((bf16[2,128,4,2,384]{4,3,2,0,1:T(2,128)(2,1)}), bf16[2,128,4,2,384]{4,3,2,0,1:T(2,128)(2,1)S(1)}, u32[]{:S(2)}, u32[]{:S(2)}) %all-to-all-start.2) | async-done | bytes 1572896 | tf_op jit(solution)/shard_map/all_to_all | solution.py:143
  198.8 20.4 %all-to-all-done.3 = bf16[2,8,128,384]{3,1,0,2:T(8,128)(2,1)S(1)} async-done(((bf16[2,8,128,384]{3,1,0,2:T(8,128)(2,1)}), bf16[2,8,128,384]{3,1,0,2:T(8,128)(2,1)S(1)}, u32[]{:S(2)}, u32[]{:S(2)}) %all-to-all-start.3) | async-done | bytes 1572896 | tf_op jit(solution)/shard_map/all_to_all | solution.py:147
  234.9 35.9 %multiply_convert_fusion = (bf16[1024,3072]{1,0:T(8,128)(2,1)}, f32[1024,3072]{1,0:T(8,128)}, f32[1024,3072]{1,0:T(8,128)}) fusion(f32[3072]{0:T(1024)S(1)} %copy-done.67, bf16[1024,768]{1,0:T(8,128)(2,1)S(1)} %bitcast.334, bf16[768,3072]{1,0:T(8,128)(2,1)S(1)} %bitcast.347), kind=kOutput, calls=%fused_computation.4 | convolution fusion | flops 5039456256 | bytes 37761024 | tf_op jit(solution)/shard_map/dot_general | solution.py:153
  270.9 16.7 %convert_reduce_fusion = (f32[3072]{0:T(1024)S(1)}, bf16[1024,3072]{1,0:T(8,128)(2,1)}) fusion(f32[1024,3072]{1,0:T(8,128)} %get-tuple-element.47, bf16[1024,768]{1,0:T(8,128)(2,1)S(1)} %bitcast.314, bf16[3072,768]{1,0:T(8,128)(2,1)} %param.29, f32[1024,3072]{1,0:T(8,128)} %get-tuple-element.75, f32[3072]{0:T(1024)S(1)} %copy-done.67), kind=kOutput, calls=%fused_computation.2 | convolution fusion | flops 4885312512 | bytes 37773312 | tf_op jit(solution)/shard_map/tc,fc->tf/dot_general | solution.py:211
  287.7 7.6 %fusion.112 = (f32[768]{0:T(1024)S(1)}, f32[1024,768]{1,0:T(8,128)S(1)}) fusion(bf16[1024,3072]{1,0:T(8,128)(2,1)} %get-tuple-element.79, bf16[768,3072]{1,0:T(8,128)(2,1)S(1)} %bitcast.347), kind=kOutput, calls=%fused_computation.224 | convolution fusion | flops 4832623616 | bytes 14158848 | tf_op jit(solution)/shard_map/tf,cf->tc/dot_general | solution.py:220
  318.5 24.9 %all_to_all.126 = bf16[2,2,196608]{2,1,0:T(2,128)(2,1)} all-to-all(bf16[2,2,196608]{2,1,0:T(2,128)(2,1)} %reshape.566), channel_id=1, replica_groups=mesh['rows'=16,'cols'=2] {'cols'}, dimensions={0} | all-to-all | bytes 3145728 | tf_op jit(solution)/shard_map/all_to_all | solution.py:228
  357.1 8.3 %all-to-all-start.5 = ((bf16[2,8,64,2,384]{4,1,0,3,2:T(8,128)(2,1)}), bf16[2,8,64,2,384]{4,1,0,3,2:T(8,128)(2,1)}, u32[]{:S(2)}, u32[]{:S(2)}) async-start(bf16[2,8,64,2,384]{4,1,0,3,2:T(8,128)(2,1)} %copy.175), calls=%async_computation.5 | async-start | bytes 3145728 | tf_op jit(solution)/shard_map/all_to_all | solution.py:232
  365.4 9.5 %convolution_convert_fusion.1 = bf16[768,3072]{1,0:T(8,128)(2,1)} fusion(bf16[1024,768]{1,0:T(8,128)(2,1)} %bitcast.335, bf16[1024,3072]{1,0:T(8,128)(2,1)} %get-tuple-element.79), kind=kOutput, calls=%fused_computation.19 | convolution fusion | flops 4834197504 | bytes 12582912 | tf_op jit(solution)/shard_map/tc,tf->cf/dot_general | solution.py:216
  375.0 9.6 %convolution_convert_fusion = bf16[3072,768]{1,0:T(8,128)(2,1)} fusion(bf16[1024,3072]{1,0:T(8,128)(2,1)} %get-tuple-element.46, bf16[1024,768]{1,0:T(8,128)(2,1)S(1)} %bitcast.315), kind=kOutput, calls=%fused_computation.18 | convolution fusion | flops 4834197504 | bytes 12582912 | tf_op jit(solution)/shard_map/tf,tc->fc/dot_general | solution.py:208
  384.7 14.5 %all-to-all-done.5 = bf16[2,8,64,2,384]{4,1,0,3,2:T(8,128)(2,1)} async-done(((bf16[2,8,64,2,384]{4,1,0,3,2:T(8,128)(2,1)}), bf16[2,8,64,2,384]{4,1,0,3,2:T(8,128)(2,1)}, u32[]{:S(2)}, u32[]{:S(2)}) %all-to-all-start.5) | async-done | bytes 1572896 | tf_op jit(solution)/shard_map/all_to_all | solution.py:232
  402.9 7.0 copy.179
  443.4 7.0 copy.185
  450.4 6.7 fusion.52
  461.9 16.5 %all-to-all-start.6 = ((bf16[2,128,4,2,384]{4,3,2,0,1:T(2,128)(2,1)}), bf16[2,128,4,2,384]{4,3,2,0,1:T(2,128)(2,1)}, u32[]{:S(2)}, u32[]{:S(2)}) async-start(bf16[2,128,4,2,384]{4,3,2,0,1:T(2,128)(2,1)} %copy.187), calls=%async_computation.6 | async-start | bytes 3145728 | tf_op jit(solution)/shard_map/all_to_all | solution.py:260
  484.8 32.7 %all-to-all-done.6 = bf16[2,128,4,2,384]{4,3,2,0,1:T(2,128)(2,1)} async-done(((bf16[2,128,4,2,384]{4,3,2,0,1:T(2,128)(2,1)}), bf16[2,128,4,2,384]{4,3,2,0,1:T(2,128)(2,1)}, u32[]{:S(2)}, u32[]{:S(2)}) %all-to-all-start.6) | async-done | bytes 1572896 | tf_op jit(solution)/shard_map/all_to_all | solution.py:260
  537.7 62.8 %all-reduce.8.cloned.1.call-done = (bf16[768,3072]{1,0:T(8,128)(2,1)}, bf16[3072,768]{1,0:T(8,128)(2,1)}) async-done(((bf16[768,3072]{1,0:T(8,128)(2,1)}, bf16[3072,768]{1,0:T(8,128)(2,1)}), (bf16[768,3072]{1,0:T(8,128)(2,1)}, bf16[3072,768]{1,0:T(8,128)(2,1)})) %all-reduce.8.cloned.1.call-update) | async-done | bytes 9437200 | tf_op jit(solution)/shard_map/psum | solution.py:350
  600.5 7.5 %convert_element_type.229 = f32[768,3072]{1,0:T(8,128)} convert(bf16[768,3072]{1,0:T(8,128)(2,1)} %get-tuple-element.41) | non-fusion elementwise | flops 2359296 | bytes 14155776 | tf_op jit(solution)/shard_map/convert_element_type | solution.py:350
  628.6 40.9 %all-reduce = (f32[6912]{0:T(1024)S(1)}, f32[2,8,96]{2,1,0:T(8,128)}, f32[2,8,96]{2,1,0:T(8,128)}) all-reduce(f32[6912]{0:T(1024)S(1)} %constant_dynamic-update-slice_fusion, f32[2,8,96]{2,1,0:T(8,128)S(1)} %copy_dynamic-update-slice_fusion.1, ...), channel_id=1, replica_groups=mesh['rows'=16,'cols'=2] {'rows','cols'}, use_global_device_ids=true, to_apply=%region_14.15 | all-reduce | flops 9984 | bytes 79872 | tf_op jit(solution)/shard_map/psum | solution.py:352
  675.3 63.5 %all-reduce.6.cloned.1.call-done = (f32[2,8,96,96]{3,2,1,0:T(8,128)}, f32[2,8,96,96]{3,2,1,0:T(8,128)}) async-done(((f32[2,8,96,96]{3,2,1,0:T(8,128)}, f32[2,8,96,96]{3,2,1,0:T(8,128)}), (f32[2,8,96,96]{3,2,1,0:T(8,128)}, f32[2,8,96,96]{3,2,1,0:T(8,128)})) %all-reduce.6.cloned.1.call-update) | async-done | bytes 1179664 | tf_op jit(solution)/shard_map/psum | solution.py:377
  (272 shorter events, 239.4 us)
Async XLA Ops:
  9.0 219.0 %copy-start.22 = (f32[2,8,64]{2,1,0:T(8,128)}, f32[2,8,64]{2,1,0:T(8,128)S(1)}, u32[]{:S(2)}) copy-start(f32[2,8,64]{2,1,0:T(8,128)S(1)} %broadcast_multiply_fusion.1) | copy-start | bytes 12292
  11.5 216.6 %copy-start.40 = (f32[2,8,64]{2,1,0:T(8,128)}, f32[2,8,64]{2,1,0:T(8,128)S(1)}, u32[]{:S(2)}) copy-start(f32[2,8,64]{2,1,0:T(8,128)S(1)} %get-tuple-element.87) | copy-start | bytes 12292
  11.5 216.6 %copy-start.42 = (f32[2,8,64]{2,1,0:T(8,128)}, f32[2,8,64]{2,1,0:T(8,128)S(1)}, u32[]{:S(2)}) copy-start(f32[2,8,64]{2,1,0:T(8,128)S(1)} %get-tuple-element.86) | copy-start | bytes 12292
  22.5 24.4 %all-to-all-start = ((bf16[2,2,196608]{2,1,0:T(2,128)(2,1)}), bf16[2,2,196608]{2,1,0:T(2,128)(2,1)S(1)}, u32[]{:S(2)}, u32[]{:S(2)}) async-start(bf16[2,2,196608]{2,1,0:T(2,128)(2,1)} %reshape.564), calls=%async_computation | async-start | bytes 3145728 | tf_op jit(solution)/shard_map/all_to_all | solution.py:112
  26.9 27.3 %copy-start.32 = (f32[128,1,64]{0,2,1:T(8,128)}, f32[128,1,64]{0,2,1:T(8,128)S(1)}, u32[]{:S(2)}) copy-start(f32[128,1,64]{0,2,1:T(8,128)S(1)} %get-tuple-element.88) | copy-start | bytes 98308
  56.8 38.3 %all-to-all-start.1 = ((bf16[2,8,64,2,384]{4,1,0,3,2:T(8,128)(2,1)}), bf16[2,8,64,2,384]{4,1,0,3,2:T(8,128)(2,1)S(1)}, u32[]{:S(2)}, u32[]{:S(2)}) async-start(bf16[2,8,64,2,384]{4,1,0,3,2:T(8,128)(2,1)} %copy.157), calls=%async_computation.1 | async-start | bytes 3145728 | tf_op jit(solution)/shard_map/all_to_all | solution.py:116
  65.9 41.4 %copy-start.20 = (bf16[1,4,96,96]{2,3,1,0:T(8,128)(2,1)}, bf16[1,4,96,96]{2,3,1,0:T(8,128)(2,1)S(1)}, u32[]{:S(2)}) copy-start(bf16[1,4,96,96]{2,3,1,0:T(8,128)(2,1)S(1)} %copy.231) | copy-start | bytes 221188
  66.8 40.6 %copy-start.61 = (f32[4,192]{1,0:T(4,128)}, f32[4,192]{1,0:T(4,128)S(1)}, u32[]{:S(2)}) copy-start(f32[4,192]{1,0:T(4,128)S(1)} %add.235) | copy-start | bytes 9220
  67.8 49.9 %copy-start.18 = (bf16[1,4,96,96]{2,3,1,0:T(8,128)(2,1)}, bf16[1,4,96,96]{2,3,1,0:T(8,128)(2,1)S(1)}, u32[]{:S(2)}) copy-start(bf16[1,4,96,96]{2,3,1,0:T(8,128)(2,1)S(1)} %copy.228) | copy-start | bytes 221188
  68.6 49.1 %copy-start.54 = (f32[4,192]{1,0:T(4,128)}, f32[4,192]{1,0:T(4,128)S(1)}, u32[]{:S(2)}) copy-start(f32[4,192]{1,0:T(4,128)S(1)} %add.238) | copy-start | bytes 9220
  69.2 70.0 %copy-start.13 = (bf16[128,1,128,2]{2,0,3,1:T(8,128)(2,1)}, bf16[128,1,128,2]{2,0,3,1:T(8,128)(2,1)S(1)}, u32[]{:S(2)}) copy-start(bf16[128,1,128,2]{2,0,3,1:T(8,128)(2,1)S(1)} %get-tuple-element.63) | copy-start | bytes 196612
  69.2 70.0 %copy-start.15 = (bf16[128,1,128,2]{2,0,3,1:T(8,128)(2,1)}, bf16[128,1,128,2]{2,0,3,1:T(8,128)(2,1)S(1)}, u32[]{:S(2)}) copy-start(bf16[128,1,128,2]{2,0,3,1:T(8,128)(2,1)S(1)} %get-tuple-element.64) | copy-start | bytes 196612
  145.5 41.5 %all-to-all-start.2 = ((bf16[2,128,4,2,384]{4,3,2,0,1:T(2,128)(2,1)}), bf16[2,128,4,2,384]{4,3,2,0,1:T(2,128)(2,1)S(1)}, u32[]{:S(2)}, u32[]{:S(2)}) async-start(bf16[2,128,4,2,384]{4,3,2,0,1:T(2,128)(2,1)} %copy.168), calls=%async_computation.2 | async-start | bytes 3145728 | tf_op jit(solution)/shard_map/all_to_all | solution.py:143
  155.2 37.3 %copy-start.36 = (f32[1,64,128]{2,1,0:T(8,128)}, f32[1,64,128]{2,1,0:T(8,128)S(1)}, u32[]{:S(2)}) copy-start(f32[1,64,128]{2,1,0:T(8,128)S(1)} %get-tuple-element.70) | copy-start | bytes 98308
  155.2 37.3 %copy-start.38 = (f32[1,64,128]{2,1,0:T(8,128)}, f32[1,64,128]{2,1,0:T(8,128)S(1)}, u32[]{:S(2)}) copy-start(f32[1,64,128]{2,1,0:T(8,128)S(1)} %get-tuple-element.71) | copy-start | bytes 98308
  195.2 24.1 %all-to-all-start.3 = ((bf16[2,8,128,384]{3,1,0,2:T(8,128)(2,1)}), bf16[2,8,128,384]{3,1,0,2:T(8,128)(2,1)S(1)}, u32[]{:S(2)}, u32[]{:S(2)}) async-start(bf16[2,8,128,384]{3,1,0,2:T(8,128)(2,1)} %copy.171), calls=%async_computation.3 | async-start | bytes 3145728 | tf_op jit(solution)/shard_map/all_to_all | solution.py:147
  232.1 38.7 %copy-start.46 = (f32[2,8,64]{2,1,0:T(8,128)}, f32[2,8,64]{2,1,0:T(8,128)S(1)}, u32[]{:S(2)}) copy-start(f32[2,8,64]{2,1,0:T(8,128)S(1)} %fusion.87) | copy-start | bytes 12292
  232.7 38.2 %copy-start.17 = (bf16[2,8,64,768]{3,2,1,0:T(8,128)(2,1)}, bf16[2,8,64,768]{3,2,1,0:T(8,128)(2,1)S(1)}, u32[]{:S(2)}) copy-start(bf16[2,8,64,768]{3,2,1,0:T(8,128)(2,1)S(1)} %add_convert_fusion.3) | copy-start | bytes 4718596
  234.9 36.0 %copy-start.5 = (bf16[2,8,64,768]{3,2,1,0:T(8,128)(2,1)S(1)}, bf16[2,8,64,768]{3,2,1,0:T(8,128)(2,1)}, u32[]{:S(2)}) copy-start(bf16[2,8,64,768]{3,2,1,0:T(8,128)(2,1)} %param.31) | copy-start | bytes 4718596
  357.1 42.1 %all-to-all-start.5 = ((bf16[2,8,64,2,384]{4,1,0,3,2:T(8,128)(2,1)}), bf16[2,8,64,2,384]{4,1,0,3,2:T(8,128)(2,1)}, u32[]{:S(2)}, u32[]{:S(2)}) async-start(bf16[2,8,64,2,384]{4,1,0,3,2:T(8,128)(2,1)} %copy.175), calls=%async_computation.5 | async-start | bytes 3145728 | tf_op jit(solution)/shard_map/all_to_all | solution.py:232
  365.4 235.1 %all-reduce.8.cloned.1.call-start = ((), (), s32[]{:S(2)}) async-start(), calls=%async_computation.9 | async-start | bytes 18874368 | tf_op jit(solution)/shard_map/psum | solution.py:350
  461.9 55.6 %all-to-all-start.6 = ((bf16[2,128,4,2,384]{4,3,2,0,1:T(2,128)(2,1)}), bf16[2,128,4,2,384]{4,3,2,0,1:T(2,128)(2,1)}, u32[]{:S(2)}, u32[]{:S(2)}) async-start(bf16[2,128,4,2,384]{4,3,2,0,1:T(2,128)(2,1)} %copy.187), calls=%async_computation.6 | async-start | bytes 3145728 | tf_op jit(solution)/shard_map/all_to_all | solution.py:260
  529.7 82.8 %all-to-all-start.7 = ((bf16[2,8,128,384]{3,1,0,2:T(8,128)(2,1)}), bf16[2,8,128,384]{3,1,0,2:T(8,128)(2,1)}, u32[]{:S(2)}, u32[]{:S(2)}) async-start(bf16[2,8,128,384]{3,1,0,2:T(8,128)(2,1)} %copy.190), calls=%async_computation.7 | async-start | bytes 3145728 | tf_op jit(solution)/shard_map/all_to_all | solution.py:264
  534.3 204.5 %all-reduce.6.cloned.1.call-start = ((), (), s32[]{:S(2)}) async-start(), calls=%async_computation.8 | async-start | bytes 3145728 | tf_op jit(solution)/shard_map/psum | solution.py:377
  (59 other events, 332.9 us)
Sparse Core Ops, SparseCore 0:
  384.8 215.6 all-reduce.7
  607.4 131.3 all-reduce.5

commit v2 on v1

--- a/solution.py
+++ b/solution.py
@@ -1,8 +1,13 @@
+import functools
 import math
 
 import jax
 import jax.numpy as jnp
+import ml_dtypes
+import numpy as np
 from jax import lax
+from jax.experimental import pallas as pl
+from jax.experimental.pallas import tpu as pltpu
 from jax.sharding import PartitionSpec as P
 
 shrink_width = 0.01
@@ -285,7 +290,7 @@
     return (gradient_tokens, shared, local_blocks)
 
 
-def shards(
+def shards_general(
     tokens,
     region_sizes,
     region_starts,
@@ -393,6 +398,762 @@
     )
 
 
+MESH = pl.DeviceIdType.MESH
+wide = jnp.float32
+low = jnp.bfloat16
+by_last = (((1,), (1,)), ((), ()))
+vmem = pl.BlockSpec(memory_space=pltpu.VMEM)
+
+
+def dot(a, b):
+    return jnp.dot(a, b, preferred_element_type=wide)
+
+
+def dot_last(a, b):
+    return lax.dot_general(a, b, by_last, preferred_element_type=wide)
+
+
+def task_tables(height, width, rows_here, cols_here):
+    modes = width // 2
+    near = modes // 2
+    column = np.arange(width)
+    frequency = np.arange(modes)
+    angle = (column[:, None] * frequency[None, :] % width).astype(np.float32) * np.float32(
+        2.0 * math.pi / width
+    )
+    scale = np.float32(1.0 / math.sqrt(width))
+    zonal = np.stack([np.cos(angle), -np.sin(angle)], 1) * scale
+    factor = np.where(frequency == 0, 1.0, 2.0).astype(np.float32)
+    inverse = (
+        np.stack([np.cos(angle).T * factor[:, None], -np.sin(angle).T * factor[:, None]], 0) * scale
+    )
+    latitude = np.arange(height)
+    turn = (latitude[:, None] * latitude[None, :] % height).astype(np.float32) * np.float32(
+        2.0 * math.pi / height
+    )
+    cosine = np.cos(turn) / np.float32(math.sqrt(height))
+    sine = np.sin(turn) / np.float32(math.sqrt(height))
+    meridian = np.stack([np.stack([cosine, sine], -1), np.stack([-sine, cosine], -1)], 1)
+    halves = width // cols_here
+    split_f = zonal.reshape(halves, cols_here, 2, 2, near)
+    to_modes = np.zeros((halves, 2, cols_here, 2, 2, 2, near), np.float32)
+    split_g = inverse.reshape(2, 2, near, halves, cols_here)
+    to_columns = np.zeros((2, 2, 2, near, halves, 2, cols_here), np.float32)
+    for i in range(2):
+        to_modes[:, i, :, :, i] = split_f.transpose(0, 1, 3, 2, 4)
+        to_columns[:, i, :, :, :, i] = split_g.transpose(1, 0, 2, 3, 4)
+    side = halves * 2 * cols_here
+    to_modes = to_modes.reshape(side, side)
+    to_columns = to_columns.reshape(side, side)
+    pairs = rows_here // 2
+    senders = height // rows_here
+    order = np.zeros((height // 2, 2), np.int64)
+    for core in range(2):
+        for chip in range(senders // 2):
+            for pair in range(pairs):
+                for i in range(2):
+                    order[(core * (senders // 2) + chip) * pairs + pair, i] = (
+                        (chip * 2 + core) * rows_here + pair * 2 + i
+                    )
+    placed = meridian[:, :, order]
+    ahead = np.zeros((2, 2, 2, height // 2, 2, 2, height), np.float32)
+    for c in range(2):
+        ahead[:, :, c, :, c] = placed.transpose(3, 4, 2, 1, 0)
+    ahead = ahead.reshape(2, 2 * height, 4 * height)
+    behind = ahead.reshape(4 * height, 4 * height).T
+    return tuple(
+        np.asarray(item, ml_dtypes.bfloat16)
+        for item in (to_modes, to_columns, ahead, behind, np.eye(256, dtype=np.float32))
+    )
+
+
+def chip_device(chip, core, cols):
+    return ((chip // cols) * 2 + core, chip % cols)
+
+
+def swap_bits(value, mask, bits):
+    out = 0
+    for k in range(bits):
+        bit = (value // (1 << k)) % 2
+        if (mask >> k) & 1:
+            bit = 1 - bit
+        out = out + bit * (1 << k)
+    return out
+
+
+def greet(chips, cols):
+    row = lax.axis_index("rows")
+    core = row % 2
+    me = (row // 2) * cols + lax.axis_index("cols")
+    barrier = pltpu.get_barrier_semaphore()
+    for step in range(1, chips):
+        other = (me + step) % chips
+        pl.semaphore_signal(
+            barrier, inc=1, device_id=chip_device(other, core, cols), device_id_type=MESH
+        )
+    pl.semaphore_signal(
+        barrier, inc=1, device_id=chip_device(me, 1 - core, cols), device_id_type=MESH
+    )
+    pl.semaphore_wait(barrier, chips)
+    return me, core
+
+
+def send_piece(src, dst, send_sem, recv_sem, target, me, core, cols):
+    @pl.when(target == me)
+    def _():
+        pltpu.make_async_copy(src, dst, recv_sem).start()
+
+    @pl.when(target != me)
+    def _():
+        pltpu.make_async_remote_copy(
+            src_ref=src,
+            dst_ref=dst,
+            send_sem=send_sem,
+            recv_sem=recv_sem,
+            device_id=chip_device(target, core, cols),
+            device_id_type=MESH,
+        ).start()
+
+
+def await_piece(ref, sem):
+    pltpu.make_async_copy(ref, ref, sem).wait()
+
+
+def to_feature_rows(out_ref, region, place, piece, eye):
+    features = piece.shape[1]
+    for low_end in range(0, features, 256):
+        turned = dot_last(eye, piece[:, low_end : low_end + 256])
+        out_ref[region, low_end : low_end + 256, place] = turned.astype(low)
+
+
+def modes_first(block, group, half):
+    columns = []
+    for m in range(group):
+        rows = block[m * half : (m + 1) * half]
+        height = block.shape[1] // 4
+        columns.append(
+            jnp.concatenate(
+                [
+                    rows[:, (c * 2 + p) * height : (c * 2 + p + 1) * height]
+                    for p in range(2)
+                    for c in range(2)
+                ],
+                0,
+            )
+        )
+    return jnp.concatenate(columns, 1)
+
+
+def modes_last(block, group, half):
+    height = block.shape[1] // group
+    rows = []
+    for m in range(group):
+        part = block[:, m * height : (m + 1) * height]
+        rows.append(
+            jnp.concatenate(
+                [
+                    part[(p * 2 + c) * half : (p * 2 + c + 1) * half]
+                    for c in range(2)
+                    for p in range(2)
+                ],
+                1,
+            )
+        )
+    return jnp.concatenate(rows, 0)
+
+
+def filter_pass(sizes, me, core, produce, middle, consume, tables, work, sems):
+    regions, blocks, block_size, chips, cols, tokens = sizes
+    table_in, table_out, ahead, behind = tables
+    sent, got, zonal, zonal_got, tall, flat, turned, back, sibling, leaving, coming = work
+    send_a, recv_a, send_b, recv_b, send_c, recv_c, send_d, recv_d = sems
+    lanes = 128
+    senders = chips // cols
+    pairs = tokens // lanes
+    half = block_size // 2
+    points = senders * pairs
+    group = 4
+    bits = (blocks - 1).bit_length()
+    for region in range(regions):
+        produce(region)
+        for step in range(blocks - 1, -1, -1):
+            target = region * blocks + swap_bits(me % blocks, step, bits)
+            src = sent.at[region, pl.ds(pl.multiple_of(target % blocks * block_size, 32), block_size)]
+            place = region * blocks + step
+            send_piece(src, got.at[me], send_a.at[place], recv_a.at[me], target, me, core, cols)
+
+    def zonal_step(chip, carry):
+        for col in range(cols):
+            await_piece(got.at[chip * cols + col], recv_a.at[chip * cols + col])
+        for pair in range(pairs):
+            x = jnp.concatenate(
+                [got[chip * cols + col, :, pair * lanes : (pair + 1) * lanes] for col in range(cols)], 1
+            )
+            y = dot(x, table_in[...]).astype(low)
+            for part in range(2):
+                zonal[part, chip * pairs + pair] = y[:, part * lanes : (part + 1) * lanes]
+        return carry
+
+    lax.fori_loop(0, senders, zonal_step, 0)
+    swap = pltpu.make_async_remote_copy(
+        src_ref=zonal.at[1 - core],
+        dst_ref=zonal_got,
+        send_sem=send_b,
+        recv_sem=recv_b,
+        device_id=chip_device(me, 1 - core, cols),
+        device_id_type=MESH,
+    )
+    swap.start()
+
+    def widen(source, first):
+        def step(point, carry):
+            row = pl.multiple_of((first + point) * block_size, 32)
+            tall[pl.ds(row, block_size), :] = source(point).astype(wide)
+            return carry
+
+        lax.fori_loop(0, points, step, 0)
+
+    widen(lambda point: zonal[core, point], core * points)
+    swap.wait()
+    widen(lambda point: zonal_got[point], (1 - core) * points)
+    modes = lanes // 4
+
+    def turn_step(c, carry):
+        x = jnp.concatenate(
+            [tall[pl.ds(c + half * side, 2 * points, stride=block_size), :] for side in range(2)], 0
+        )
+        y = jnp.transpose(x)
+        for i in range(4):
+            flat[i, pl.ds(c, modes, stride=half), :] = y[i * modes : (i + 1) * modes]
+        return carry
+
+    lax.fori_loop(0, half, turn_step, 0)
+
+    def mode_step(step, carry):
+        rows = pl.ds(pl.multiple_of(step * group * half, 64), group * half)
+        spectrum = 0.0
+        for i in range(2):
+            x = jnp.concatenate([flat[i * 2, rows, :], flat[i * 2 + 1, rows, :]], 1).astype(low)
+            spectrum = spectrum + dot(x, ahead[i])
+        out = modes_last(middle(step, modes_first(spectrum, group, half)), group, half)
+        high = out.astype(low)
+        rest = (out - high.astype(wide)).astype(low)
+        y = (dot(high, behind[...]) + dot(rest, behind[...])).astype(low).astype(wide)
+        for i in range(4):
+            turned[i, rows, :] = y[:, i * lanes : (i + 1) * lanes]
+        return carry
+
+    lax.fori_loop(0, modes // group, mode_step, 0)
+
+    def return_step(c, carry):
+        x = jnp.concatenate([turned[i, pl.ds(c, modes, stride=half), :] for i in range(4)], 0)
+        y = jnp.transpose(x)
+        for side in range(2):
+            tall[pl.ds(c + half * side, 2 * points, stride=block_size), :] = y[
+                side * 2 * points : (side + 1) * 2 * points
+            ]
+        return carry
+
+    lax.fori_loop(0, half, return_step, 0)
+
+    def narrow(store, first):
+        def step(point, carry):
+            row = pl.multiple_of((first + point) * block_size, 32)
+            store(point, tall[pl.ds(row, block_size), :].astype(low))
+            return carry
+
+        lax.fori_loop(0, points, step, 0)
+
+    def to_sibling(point, value):
+        back[point] = value
+
+    def to_self(point, value):
+        sibling[core, point] = value
+
+    narrow(to_sibling, (1 - core) * points)
+    swap_back = pltpu.make_async_remote_copy(
+        src_ref=back,
+        dst_ref=sibling.at[core],
+        send_sem=send_c,
+        recv_sem=recv_c,
+        device_id=chip_device(me, 1 - core, cols),
+        device_id_type=MESH,
+    )
+    swap_back.start()
+    narrow(to_self, core * points)
+    swap_back.wait_send()
+    await_piece(sibling.at[1 - core], recv_c)
+
+    def column_step(chip, carry):
+        for pair in range(pairs):
+            point = chip * pairs + pair
+            x = jnp.concatenate([sibling[0, point], sibling[1, point]], 1)
+            y = dot(x, table_out[...]).astype(low)
+            for col in range(cols):
+                leaving[chip * cols + col, :, pair * lanes : (pair + 1) * lanes] = y[
+                    :, col * lanes : (col + 1) * lanes
+                ]
+        for col in range(cols):
+            target = chip * cols + col
+            dst = coming.at[
+                me // blocks, pl.ds(pl.multiple_of(me % blocks * block_size, 32), block_size)
+            ]
+            send_piece(
+                leaving.at[target], dst, send_d.at[target], recv_d.at[me], target, me, core, cols
+            )
+        return carry
+
+    lax.fori_loop(0, senders, column_step, 0)
+    for region in range(regions):
+
+        def arrive(block, carry):
+            ref = coming.at[region, pl.ds(pl.multiple_of(block * block_size, 32), block_size)]
+            await_piece(ref, recv_d.at[region * blocks + block])
+            return carry
+
+        lax.fori_loop(0, blocks, arrive, 0)
+        consume(region)
+
+    for place in range(regions * blocks):
+        region, step = place // blocks, place % blocks
+        target = region * blocks + swap_bits(me % blocks, step, bits)
+
+        @pl.when(target != me)
+        def _():
+            await_piece(got.at[0], send_a.at[place])
+
+        @pl.when(place != me)
+        def _():
+            await_piece(leaving.at[0], send_d.at[place])
+
+
+def work_shapes(sizes):
+    regions, blocks, block_size, chips, cols, tokens = sizes
+    lanes = 128
+    features = blocks * block_size
+    points = (chips // cols) * (tokens // lanes)
+    rows = (lanes // 4) * (block_size // 2)
+    return [
+        pltpu.VMEM((regions, features, tokens), low),
+        pltpu.VMEM((chips, block_size, tokens), low),
+        pltpu.VMEM((2, points, block_size, lanes), low),
+        pltpu.VMEM((points, block_size, lanes), low),
+        pltpu.VMEM((2 * points * block_size, lanes), wide),
+        pltpu.VMEM((4, rows, lanes), wide),
+        pltpu.VMEM((4, rows, lanes), wide),
+        pltpu.VMEM((points, block_size, lanes), low),
+        pltpu.VMEM((2, points, block_size, lanes), low),
+        pltpu.VMEM((chips, block_size, tokens), low),
+        pltpu.VMEM((regions, features, tokens), low),
+        pltpu.SemaphoreType.DMA((chips,)),
+        pltpu.SemaphoreType.DMA((chips,)),
+        pltpu.SemaphoreType.DMA,
+        pltpu.SemaphoreType.DMA,
+        pltpu.SemaphoreType.DMA,
+        pltpu.SemaphoreType.DMA,
+        pltpu.SemaphoreType.DMA((chips,)),
+        pltpu.SemaphoreType.DMA((chips,)),
+    ]
+
+
+def normalise(value):
+    centre = jnp.mean(value, -1, keepdims=True)
+    centred = value - centre
+    spread = jnp.mean(centred * centred, -1, keepdims=True)
+    factor = lax.rsqrt(spread + norm_eps)
+    return centred * factor, factor
+
+
+def gelu_parts(value):
+    curve = 0.5 * (1.0 + lax.erf(value * (1.0 / math.sqrt(2.0))))
+    return curve
+
+
+def gelu_slope(value):
+    bell = jnp.exp(-0.5 * value * value) * (1.0 / math.sqrt(2.0 * math.pi))
+    return gelu_parts(value) + value * bell
+
+
+def forward_kernel(sizes, *refs):
+    (
+        tokens_ref,
+        mask_ref,
+        gain_ref,
+        shift_ref,
+        scale_ref,
+        center_ref,
+        kernel_ref,
+        bias_ref,
+        mixer_ref,
+        offset_ref,
+        to_modes,
+        to_columns,
+        ahead,
+        behind,
+        eye,
+        mixed_ref,
+        second_ref,
+        spectrum_ref,
+        first_ref,
+        act_ref,
+        pre_ref,
+    ) = refs[:21]
+    work, sems = refs[21:32], refs[32:]
+    regions, blocks, block_size, chips, cols, tokens = sizes
+    me, core = greet(chips, cols)
+    sent, coming = work[0], work[-1]
+    piece = 128
+
+    def produce(region):
+        def step(part, carry):
+            rows = pl.ds(pl.multiple_of(region * tokens + part * piece, piece), piece)
+            unit, factor = normalise(tokens_ref[rows, :].astype(wide))
+            normed = unit * gain_ref[...] + shift_ref[...]
+            place = pl.ds(pl.multiple_of(part * piece, piece), piece)
+            to_feature_rows(sent, region, place, (mask_ref[rows, :] * normed).astype(low), eye[...])
+            return carry
+
+        lax.fori_loop(0, tokens // piece, step, 0)
+
+    def middle(step, spectrum):
+        spectrum = spectrum.astype(low)
+        spectrum_ref[step] = spectrum
+        first = dot(kernel_ref[...], spectrum) + bias_ref[...]
+        first_ref[step] = first
+        act = (first * gelu_parts(first)).astype(low)
+        act_ref[step] = act
+        second = dot(mixer_ref[...], act) + offset_ref[...]
+        pre_ref[step] = second
+        return second - shrink_width * jnp.tanh(second / shrink_width)
+
+    def consume(region):
+        def step(part, carry):
+            rows = pl.ds(pl.multiple_of(region * tokens + part * 256, 256), 256)
+            place = pl.ds(pl.multiple_of(part * 256, 256), 256)
+            fields = jnp.concatenate(
+                [
+                    dot_last(eye[...], coming[region, first : first + 256, place])
+                    for first in range(0, coming.shape[1], 256)
+                ],
+                1,
+            )
+            residual = tokens_ref[rows, :].astype(wide)
+            unit, factor = normalise(residual)
+            normed = unit * gain_ref[...] + shift_ref[...]
+            mixed = residual + mask_ref[rows, :] * fields + normed
+            mixed_ref[rows, :] = mixed
+            unit, factor = normalise(mixed)
+            second_ref[rows, :] = (unit * scale_ref[...] + center_ref[...]).astype(low)
+            return carry
+
+        lax.fori_loop(0, tokens // 256, step, 0)
+
+    tables = (to_modes, to_columns, ahead, behind)
+    filter_pass(sizes, me, core, produce, middle, consume, tables, work, sems)
+
+
+def backward_kernel(sizes, *refs):
+    (
+        tokens_ref,
+        mixed_back_ref,
+        mask_ref,
+        gain_ref,
+        kernel_ref,
+        mixer_ref,
+        to_modes,
+        to_columns,
+        ahead,
+        behind,
+        eye,
+        spectrum_ref,
+        first_ref,
+        act_ref,
+        pre_ref,
+        slope_ref,
+        gain_slope,
+        shift_slope,
+        kernel_slope,
+        bias_slope,
+        mixer_slope,
+        offset_slope,
+    ) = refs[:22]
+    work, sems = refs[22:33], refs[33:]
+    regions, blocks, block_size, chips, cols, tokens = sizes
+    me, core = greet(chips, cols)
+    sent, coming = work[0], work[-1]
+    piece = 128
+    for ref in (gain_slope, shift_slope, kernel_slope, bias_slope, mixer_slope, offset_slope):
+        ref[...] = jnp.zeros_like(ref)
+
+    def produce(region):
+        def step(part, carry):
+            rows = pl.ds(pl.multiple_of(region * tokens + part * piece, piece), piece)
+            place = pl.ds(pl.multiple_of(part * piece, piece), piece)
+            values = (mask_ref[rows, :] * mixed_back_ref[rows, :]).astype(low)
+            to_feature_rows(sent, region, place, values, eye[...])
+            return carry
+
+        lax.fori_loop(0, tokens // piece, step, 0)
+
+    def middle(step, shrunk_back):
+        level = jnp.tanh(pre_ref[step] / shrink_width)
+        second = shrunk_back * (level * level)
+        offset_slope[...] += jnp.sum(second.astype(low).astype(wide), 1, keepdims=True)
+        second = second.astype(low)
+        mixer_slope[...] += dot_last(act_ref[step], second)
+        first = (dot(mixer_ref[...], second) * gelu_slope(first_ref[step])).astype(low)
+        bias_slope[...] += jnp.sum(first.astype(wide), 1, keepdims=True)
+        kernel_slope[...] += dot_last(spectrum_ref[step], first)
+        return dot(kernel_ref[...], first)
+
+    def consume(region):
+        def step(part, carry):
+            rows = pl.ds(pl.multiple_of(region * tokens + part * 256, 256), 256)
+            place = pl.ds(pl.multiple_of(part * 256, 256), 256)
+            fields = jnp.concatenate(
+                [
+                    dot_last(eye[...], coming[region, first : first + 256, place])
+                    for first in range(0, coming.shape[1], 256)
+                ],
+                1,
+            )
+            unit, factor = normalise(tokens_ref[rows, :].astype(wide))
+            mixed_back = mixed_back_ref[rows, :]
+            normed_back = mixed_back + mask_ref[rows, :] * fields
+            gain_slope[...] += jnp.sum(normed_back * unit, 0, keepdims=True)
+            shift_slope[...] += jnp.sum(normed_back, 0, keepdims=True)
+            pull = normed_back * gain_ref[...]
+            pull = pull - jnp.mean(pull, -1, keepdims=True) - unit * jnp.mean(
+                pull * unit, -1, keepdims=True
+            )
+            slope_ref[rows, :] = mixed_back + factor * pull
+            return carry
+
+        lax.fori_loop(0, tokens // 256, step, 0)
+
+    tables = (to_columns, to_modes, ahead, behind)
+    filter_pass(sizes, me, core, produce, middle, consume, tables, work, sems)
+
+
+def call_filter(body, sizes, outs, cid, operands):
+    shapes = [jax.ShapeDtypeStruct(shape, kind) for shape, kind in outs]
+    return pl.pallas_call(
+        functools.partial(body, sizes),
+        out_shape=shapes,
+        in_specs=[vmem] * len(operands),
+        out_specs=[vmem] * len(shapes),
+        scratch_shapes=work_shapes(sizes),
+        compiler_params=pltpu.CompilerParams(
+            collective_id=cid, has_side_effects=True, vmem_limit_bytes=58 * 1024 * 1024
+        ),
+    )(*operands)
+
+
+def shards(
+    tokens,
+    region_sizes,
+    region_starts,
+    entry_gain,
+    entry_shift,
+    spectral_kernel,
+    spectral_bias,
+    spectral_mixer,
+    spectral_offset,
+    exit_scale,
+    exit_center,
+    dense_expand,
+    dense_lift,
+    dense_project,
+    dense_return,
+    cotangent,
+):
+    regions, rows_here, cols_here, features = tokens.shape
+    row_devices = lax.axis_size("rows")
+    cols = lax.axis_size("cols")
+    blocks, block_size = spectral_kernel.shape[1:3]
+    chips = row_devices // 2 * cols
+    fits = (
+        row_devices % 2 == 0
+        and chips == regions * blocks
+        and cols == 2
+        and cols_here == 64
+        and rows_here == 8
+        and block_size == 96
+        and blocks == 8
+    )
+    if not fits:
+        return shards_general(
+            tokens,
+            region_sizes,
+            region_starts,
+            entry_gain,
+            entry_shift,
+            spectral_kernel,
+            spectral_bias,
+            spectral_mixer,
+            spectral_offset,
+            exit_scale,
+            exit_center,
+            dense_expand,
+            dense_lift,
+            dense_project,
+            dense_return,
+            cotangent,
+        )
+    height = rows_here * row_devices
+    width = cols_here * cols
+    latitude = lax.axis_index("rows") * rows_here + jnp.arange(rows_here, dtype=jnp.int32)
+    longitude = lax.axis_index("cols") * cols_here + jnp.arange(cols_here, dtype=jnp.int32)
+    inside_rows = latitude[None, :, None] < region_sizes[:, 0][:, None, None]
+    offset = (longitude[None, None, :] - region_starts[:, None, None]) % width
+    inside_cols = offset < region_sizes[:, 1][:, None, None]
+    mask = jnp.where(inside_rows & inside_cols, 1.0, 0.0).astype(wide).reshape(-1, 1)
+    patches = rows_here * cols_here
+    count = regions * patches
+    sizes = (regions, blocks, block_size, chips, cols, patches)
+    block = ((lax.axis_index("rows") // 2) * cols + lax.axis_index("cols")) % blocks
+
+    def own(weight):
+        return lax.dynamic_slice_in_dim(weight, block, 1, 1)
+
+    kernel = complex_matrix(own(spectral_kernel))[0]
+    mixer = complex_matrix(own(spectral_mixer))[0]
+    side = 2 * block_size
+    kernel_bias = own(spectral_bias).reshape(side, 1)
+    mixer_bias = own(spectral_offset).reshape(side, 1)
+    to_modes, to_columns, ahead, behind, eye = task_tables(height, width, rows_here, cols_here)
+    flat_tokens = tokens.reshape(count, features)
+    upstream = cotangent.reshape(count, features)
+    group = 4 * 128
+    steps = width // 4 // 4
+    kept_shape = (steps, side, group)
+    mixed, second_norm, spectrum, first_pre, first_act, second_pre = call_filter(
+        forward_kernel,
+        sizes,
+        (
+            ((count, features), wide),
+            ((count, features), low),
+            (kept_shape, low),
+            (kept_shape, wide),
+            (kept_shape, low),
+            (kept_shape, wide),
+        ),
+        1,
+        (
+            flat_tokens,
+            mask,
+            entry_gain[None],
+            entry_shift[None],
+            exit_scale[None],
+            exit_center[None],
+            kernel.T,
+            kernel_bias,
+            mixer.T,
+            mixer_bias,
+            to_modes,
+            to_columns,
+            ahead,
+            behind,
+            eye,
+        ),
+    )
+    hidden_pre = dot(second_norm, dense_expand) + dense_lift
+    hidden = gelu_exact(hidden_pre).astype(low)
+    output = mixed + (dot(hidden, dense_project) + dense_return)
+    project_part = jnp.einsum("tf,tc->fc", hidden, upstream, preferred_element_type=wide)
+    return_part = jnp.sum(upstream.astype(wide), 0)
+    hidden_back = dot_last(upstream, dense_project)
+    pre_back = (hidden_back * gelu_slope(hidden_pre)).astype(low)
+    expand_part = jnp.einsum("tc,tf->cf", second_norm, pre_back, preferred_element_type=wide)
+    lift_part = jnp.sum(pre_back.astype(wide), 0)
+    norm_back = dot_last(pre_back, dense_expand)
+    unit, factor = normalise(mixed)
+    scale_part = jnp.sum(norm_back * unit, 0)
+    center_part = jnp.sum(norm_back, 0)
+    pull = norm_back * exit_scale
+    pull = pull - jnp.mean(pull, -1, keepdims=True) - unit * jnp.mean(pull * unit, -1, keepdims=True)
+    mixed_back = upstream.astype(wide) + factor * pull
+    everywhere = ("rows", "cols")
+    project_sum = lax.psum(project_part.astype(low), everywhere).astype(wide)
+    expand_sum = lax.psum(expand_part.astype(low), everywhere).astype(wide)
+    slopes = call_filter(
+        backward_kernel,
+        sizes,
+        (
+            ((count, features), wide),
+            ((1, features), wide),
+            ((1, features), wide),
+            ((side, side), wide),
+            ((side, 1), wide),
+            ((side, side), wide),
+            ((side, 1), wide),
+        ),
+        2,
+        (
+            flat_tokens,
+            mixed_back,
+            mask,
+            entry_gain[None],
+            kernel,
+            mixer,
+            to_modes.T,
+            to_columns.T,
+            ahead,
+            behind,
+            eye,
+            spectrum,
+            first_pre,
+            first_act,
+            second_pre,
+        ),
+    )
+    token_slope, gain_part, shift_part, kernel_part, bias_part, mixer_part, offset_part = slopes
+
+    def spread(part):
+        total = jnp.zeros(part.shape[:1] + (blocks,) + part.shape[2:], wide)
+        return lax.dynamic_update_slice_in_dim(total, part, block, 1)
+
+    whole = (
+        spread(matrix_gradient(kernel_part[None], block_size)),
+        spread(matrix_gradient(mixer_part[None], block_size)),
+        spread(bias_part.reshape(2, 1, block_size)),
+        spread(offset_part.reshape(2, 1, block_size)),
+    )
+    vectors = (
+        gain_part[0],
+        shift_part[0],
+        scale_part,
+        center_part,
+        lift_part,
+        return_part,
+        whole[2].reshape(-1),
+        whole[3].reshape(-1),
+    )
+    sums = lax.psum(jnp.concatenate(vectors), everywhere)
+    parts = []
+    first = 0
+    for vector in vectors:
+        parts.append(sums[first : first + vector.shape[0]])
+        first += vector.shape[0]
+    kernel_sum, mixer_sum = lax.psum((whole[0], whole[1]), everywhere)
+    return (
+        output.astype(low).reshape(tokens.shape),
+        token_slope.reshape(tokens.shape),
+        parts[0],
+        parts[1],
+        kernel_sum,
+        parts[6].reshape(spectral_bias.shape),
+        mixer_sum,
+        parts[7].reshape(spectral_bias.shape),
+        parts[2],
+        parts[3],
+        expand_sum,
+        parts[4],
+        project_sum,
+        parts[5],
+    )
+
+
 def solution(mesh):
     placed = (
         P(None, "rows", "cols", None),

time: 764 us -> 591 us (0.77); the launches traced: 750 us -> 591 us
  Pallas kernels: 0 us -> 231 us
  local copies, waits for them, and re-layouts: 168 us -> 22.7 us
  waiting for transfers between devices: 270 us -> 159 us
  starting transfers between devices: 53.2 us -> 0.08 us
  matrix products: 129 us -> 80.8 us
  other arithmetic: 48.8 us -> 23.7 us
    pallas_call x0 -> x2, Pallas kernels: none -> 231 us  [call_filter(): pl.pallas_call(functools.partial(body, sizes), out_shape=shapes, in_specs...]
    all_to_all x7 -> x0, waiting for transfers between devices: 144 us -> none  [the longest x1 32.7 us: retreat(): lax.all_to_all(modes_back, 'rows', split_axis=1, concat_axis=2, tiled=True)]
    all_to_all x7 -> x0, starting transfers between devices: 53.1 us -> none  [the longest x1 16.5 us: retreat(): lax.all_to_all(modes_back, 'rows', split_axis=1, concat_axis=2, tiled=True)]
    dot_general x20 -> x6, matrix products: 129 us -> 80.8 us  [the longest x2 44 us: dot(): return jnp.dot(a, b, preferred_element_type=wide)]
    convert_element_type x12 -> x0, local copies, waits for them, and re-layouts: 44.3 us -> none  [the longest x2 10.4 us: retreat(): normed_back = mixed_back + mask * token_back.astype(jnp.float32)]
    reshape x9 -> x8, local copies, waits for them, and re-layouts: 40.6 us -> 3.29 us  [the longest x1 0.82 us: shards(): kernel_bias = own(spectral_bias).reshape(side, 1)]
    psum x2, waiting for transfers between devices: 126 us -> 159 us  [the longest x1 127 us: shards(): kernel_sum, mixer_sum = lax.psum((whole[0], whole[1]), everywhere)]
    unnamed x163 -> x46, local copies, waits for them, and re-layouts: 31.2 us -> 5.92 us
  transfers between devices with their start and end apart: 9 -> 2, of which waited for: 8 -> 2; matrix products, arithmetic and copies ran while one was open for 19% -> 8% of each run, Pallas kernels for 0% -> 21%
where the time goes in v2:
time: 591 us
  Pallas kernels  231 us (39%)
  waiting for transfers between devices  159 us (27%)
  matrix products  80.8 us (14%)
  blocking collectives  59.3 us (10%)
  other arithmetic  23.7 us (4%)
  local copies, waits for them, and re-layouts  22.7 us (4%)
  between operations  14.5 us (2%)
    pallas_call x2, Pallas kernels, call_filter(): pl.pallas_call(functools.partial(body, sizes), out_shape=shapes, in_specs...  231 us
    psum x1, waiting for transfers between devices, shards(): kernel_sum, mixer_sum = lax.psum((whole[0], whole[1]), everywhere)  127 us
    psum x1, blocking collectives, shards(): sums = lax.psum(jnp.concatenate(vectors), everywhere)  59.3 us
    dot_general x2, matrix products, dot(): return jnp.dot(a, b, preferred_element_type=wide)  44 us
    psum x1, waiting for transfers between devices, shards(): expand_sum = lax.psum(expand_part.astype(low), everywhere).astype(wide)  31.5 us
    dot_general x2, matrix products, dot_last(): return lax.dot_general(a, b, by_last, preferred_element_type=wide)  22.7 us
  transfers between devices with their start and end apart: 2, of which 2 were waited for; matrix products, arithmetic and copies ran while one was open for 8% of the time, Pallas kernels for 21%

profile of v2, /device:TPU:0, one launch (start us, length us, event | category | flops | bytes accessed | tf_op | source)
XLA Modules:
  0.0 590.7 jit_solution(13106713360938527261)
XLA Ops:
  9.1 1.3 select_n.52.refs_1_.refs_2_
  10.4 1.3 broadcast_in_dim.39.refs_2_.refs_3_
  11.7 1.3 broadcast_in_dim.40.refs_3_
  12.9 1.3 broadcast_in_dim.41.refs_4_
  14.2 1.3 broadcast_in_dim.42.refs_5_
  22.3 104.8 %shard_map.326 = (f32[1024,768]{1,0:T(8,128)}, bf16[1024,768]{1,0:T(8,128)(2,1)}, bf16[8,192,512]{2,1,0:T(8,128)(2,1)}, f32[8,192,512]{2,1,0:T(8,128)}, bf16[8,1...) custom-call(bf16[1024,768]{1,0:T(8,128)(2,1)} %bitcast.49, f32[1024,1]{1,0:T(8,128)} %select_n.52.refs_1_.refs_2_, ...), custom_call_target="tpu_custom_call" | custom-call | tf_op jit(solution)/shard_map/pallas_call | solution.py:940
  127.2 34.5 %fusion.2 = (bf16[1024,3072]{1,0:T(8,128)(2,1)S(1)}, f32[1024,3072]{1,0:T(8,128)}) fusion(f32[3072]{0:T(1024)} %param.35, bf16[1024,768]{1,0:T(8,128)(2,1)} %get-tuple-element.28, bf16[768,3072]{1,0:T(8,128)(2,1)} %param.34), kind=kOutput, calls=%fused_computation.4 | convolution fusion | flops 5039456256 | bytes 25178112 | tf_op jit(solution)/shard_map/dot_general | solution.py:409
  161.7 13.4 %convert_reduce_fusion = (f32[3072]{0:T(1024)S(1)}, bf16[1024,3072]{1,0:T(8,128)(2,1)S(1)}) fusion(f32[1024,3072]{1,0:T(8,128)} %get-tuple-element.70, f32[3072]{0:T(1024)S(1)} %copy-done.10, bf16[1024,768]{1,0:T(8,128)(2,1)S(1)} %bitcast.51, bf16[3072,768]{1,0:T(8,128)(2,1)S(1)} %bitcast.61), kind=kOutput, calls=%fused_computation.11 | convolution fusion | flops 4872729600 | bytes 25190400 | tf_op jit(solution)/shard_map/dot_general | solution.py:413
  175.1 6.9 %convolution_convert_fusion.1 = bf16[768,3072]{1,0:T(8,128)(2,1)} fusion(bf16[1024,768]{1,0:T(8,128)(2,1)S(1)} %copy-done.9, bf16[1024,3072]{1,0:T(8,128)(2,1)S(1)} %get-tuple-element.73), kind=kOutput, calls=%fused_computation.28 | convolution fusion | flops 4834197504 | bytes 12582912 | tf_op jit(solution)/shard_map/tc,tf->cf/dot_general | solution.py:1067
  182.0 7.2 %convolution_convert_fusion = bf16[3072,768]{1,0:T(8,128)(2,1)} fusion(bf16[1024,3072]{1,0:T(8,128)(2,1)S(1)} %get-tuple-element.69, bf16[1024,768]{1,0:T(8,128)(2,1)S(1)} %bitcast.52), kind=kOutput, calls=%fused_computation.27 | convolution fusion | flops 4834197504 | bytes 12582912 | tf_op jit(solution)/shard_map/tf,tc->fc/dot_general | solution.py:1063
  190.1 9.4 %multiply_reduce_fusion = (f32[768]{0:T(1024)S(1)}, f32[1024]{0:T(1024)S(1)}, f32[1024]{0:T(1024)S(1)}, f32[768]{0:T(1024)S(1)}, f32[1024,768]{1,0:T(8,128)S(1)}) fusion(f32[1024,768]{1,0:T(8,128)S(1)} %copy-done, f32[1024]{0:T(1024)S(1)} %add_rsqrt_fusion, f32[1024]{0:T(1024)S(1)} %broadcast_multiply_fusion.2, f32[768]{0:T(1024)S(1)} %copy-done.6, ...), kind=kOutput, calls=%fused_computation.30 | convolution fusion | flops 4838912000 | bytes 17327104 | tf_op jit(solution)/shard_map/dot_general | solution.py:413
  199.5 2.5 multiply_add_fusion.refs_1_
  201.9 126.2 %shard_map.327 = (f32[1024,768]{1,0:T(8,128)}, f32[1,768]{1,0:T(1,128)}, f32[1,768]{1,0:T(1,128)}, f32[192,192]{1,0:T(8,128)}, f32[192,1]{1,0:T(8,128)}, /*index=5*/f32[192,192]{1,0:T(8,128)}, f32[192,1]{1,0:T(8,128)}) custom-call(bf16[1024,768]{1,0:T(8,128)(2,1)} %bitcast.50, f32[1024,768]{1,0:T(8,128)} %multiply_add_fusion.refs_1_, ...), custom_call_target="tpu_custom_call" | custom-call | tf_op jit(solution)/shard_map/pallas_call | solution.py:940
  328.1 1.1 fusion.19
  333.5 1.7 convert_reduce_fusion.1
  335.3 9.5 %add_convert_fusion = bf16[1024,768]{1,0:T(8,128)(2,1)} fusion(f32[1024,768]{1,0:T(8,128)S(1)} %copy-done, bf16[1024,3072]{1,0:T(8,128)(2,1)} %copy-done.13, bf16[3072,768]{1,0:T(8,128)(2,1)} %param.36, f32[768]{0:T(1024)S(1)} %copy-done.11), kind=kOutput, calls=%fused_computation.34 | convolution fusion | flops 4834197504 | bytes 15731712 | tf_op jit(solution)/shard_map/dot_general | solution.py:409
  345.5 59.3 %psum.35 = f32[9984]{0:T(1024)S(1)} all-reduce(f32[9984]{0:T(1024)S(1)} %constant_dynamic-update-slice_fusion), channel_id=1, replica_groups=mesh['rows'=16,'cols'=2] {'rows','cols'}, use_global_device_ids=true, to_apply=%region_8.9 | all-reduce | flops 9984 | bytes 79872 | tf_op jit(solution)/shard_map/psum | solution.py:1132
  407.4 31.5 %all-reduce.7.cloned.1.call-done = (bf16[768,3072]{1,0:T(8,128)(2,1)}, bf16[3072,768]{1,0:T(8,128)(2,1)}) async-done(((bf16[768,3072]{1,0:T(8,128)(2,1)}, bf16[3072,768]{1,0:T(8,128)(2,1)}), (bf16[768,3072]{1,0:T(8,128)(2,1)}, bf16[3072,768]{1,0:T(8,128)(2,1)})) %all-reduce.7.cloned.1.call-update) | async-done | bytes 9437200 | tf_op jit(solution)/shard_map/psum | solution.py:1078
  438.8 7.5 %convert_element_type.38 = f32[768,3072]{1,0:T(8,128)} convert(bf16[768,3072]{1,0:T(8,128)(2,1)} %get-tuple-element.48) | non-fusion elementwise | flops 2359296 | bytes 14155776 | tf_op jit(solution)/shard_map/convert_element_type | solution.py:1078
  446.4 4.5 convert_element_type.40
  450.8 127.3 %all-reduce.5.cloned.1.call-done = (f32[2,8,96,96]{3,2,1,0:T(8,128)}, f32[2,8,96,96]{3,2,1,0:T(8,128)}) async-done(((f32[2,8,96,96]{3,2,1,0:T(8,128)}, f32[2,8,96,96]{3,2,1,0:T(8,128)}), (f32[2,8,96,96]{3,2,1,0:T(8,128)}, f32[2,8,96,96]{3,2,1,0:T(8,128)})) %all-reduce.5.cloned.1.call-update) | async-done | bytes 1179664 | tf_op jit(solution)/shard_map/psum | solution.py:1138
  578.1 1.7 copy.65
  579.8 2.1 copy.66
  581.8 2.1 copy.67
  (94 shorter events, 17.1 us)
Async XLA Ops:
  7.2 431.7 %all-reduce.7.cloned.1.call-start = ((), (), s32[]{:S(2)}) async-start(), calls=%async_computation.1 | async-start | bytes 18874368 | tf_op jit(solution)/shard_map/psum | solution.py:1078
  20.0 141.6 %slice-start.2 = ((s8[4718592]{0:T(1024)(128)(4,1)}), s8[524288]{0:T(1024)(128)(4,1)S(1)}, s32[]{:S(2)}) async-start(s8[4718592]{0:T(1024)(128)(4,1)} %bitcast.60), calls=%async_computation.4 | async-start | bytes 1048576
  127.2 34.5 %copy-start.1 = (bf16[2,8,64,768]{3,2,1,0:T(8,128)(2,1)S(1)}, bf16[2,8,64,768]{3,2,1,0:T(8,128)(2,1)}, u32[]{:S(2)}) copy-start(bf16[2,8,64,768]{3,2,1,0:T(8,128)(2,1)} %param.38) | copy-start | bytes 4718596
  127.2 34.5 %slice-start.3 = ((s8[4718592]{0:T(1024)(128)(4,1)}), s8[4194304]{0:T(1024)(128)(4,1)S(1)}, s32[]{:S(2)}) async-start(s8[4718592]{0:T(1024)(128)(4,1)} %bitcast.60), calls=%async_computation.5 | async-start | bytes 8388608
  127.2 34.5 %copy-start.10 = (f32[3072]{0:T(1024)S(1)}, f32[3072]{0:T(1024)}, u32[]{:S(2)}) copy-start(f32[3072]{0:T(1024)} %param.35) | copy-start | bytes 36868
  161.7 20.3 %copy-start.13 = (bf16[1024,3072]{1,0:T(8,128)(2,1)}, bf16[1024,3072]{1,0:T(8,128)(2,1)S(1)}, u32[]{:S(2)}) copy-start(bf16[1024,3072]{1,0:T(8,128)(2,1)S(1)} %get-tuple-element.69) | copy-start | bytes 18874372
  161.7 13.4 %copy-start.9 = (bf16[1024,768]{1,0:T(8,128)(2,1)S(1)}, bf16[1024,768]{1,0:T(8,128)(2,1)}, u32[]{:S(2)}) copy-start(bf16[1024,768]{1,0:T(8,128)(2,1)} %get-tuple-element.28) | copy-start | bytes 4718596
  175.1 6.9 %copy-start.12 = (bf16[1024,3072]{1,0:T(8,128)(2,1)}, bf16[1024,3072]{1,0:T(8,128)(2,1)S(1)}, u32[]{:S(2)}) copy-start(bf16[1024,3072]{1,0:T(8,128)(2,1)S(1)} %get-tuple-element.73) | copy-start | bytes 18874372
  182.0 7.3 %copy-start = (f32[1024,768]{1,0:T(8,128)S(1)}, f32[1024,768]{1,0:T(8,128)}, u32[]{:S(2)}) copy-start(f32[1024,768]{1,0:T(8,128)} %get-tuple-element.27) | copy-start | bytes 9437188
  189.2 0.8 copy-start.6
  189.3 388.8 %all-reduce.5.cloned.1.call-start = ((), (), s32[]{:S(2)}) async-start(), calls=%async_computation | async-start | bytes 3145728 | tf_op jit(solution)/shard_map/psum | solution.py:1138
  190.1 9.4 %copy-start.2 = (bf16[2,8,64,768]{3,2,1,0:T(8,128)(2,1)S(1)}, bf16[2,8,64,768]{3,2,1,0:T(8,128)(2,1)}, u32[]{:S(2)}) copy-start(bf16[2,8,64,768]{3,2,1,0:T(8,128)(2,1)} %param.38) | copy-start | bytes 4718596
  201.9 133.3 %copy-start.11 = (f32[768]{0:T(1024)S(1)}, f32[768]{0:T(1024)}, u32[]{:S(2)}) copy-start(f32[768]{0:T(1024)} %param.37) | copy-start | bytes 9220
  335.2 9.5 %copy-start.8 = (f32[1,768]{1,0:T(1,128)S(1)}, f32[1,768]{1,0:T(1,128)}, u32[]{:S(2)}) copy-start(f32[1,768]{1,0:T(1,128)} %get-tuple-element.34) | copy-start | bytes 9220
  335.2 9.5 %copy-start.7 = (f32[1,768]{1,0:T(1,128)S(1)}, f32[1,768]{1,0:T(1,128)}, u32[]{:S(2)}) copy-start(f32[1,768]{1,0:T(1,128)} %get-tuple-element.35) | copy-start | bytes 9220
  335.2 9.6 %copy-start.5 = (f32[192,1]{1,0:T(8,128)S(1)}, f32[192,1]{1,0:T(8,128)}, u32[]{:S(2)}) copy-start(f32[192,1]{1,0:T(8,128)} %get-tuple-element.36) | copy-start | bytes 2308
  335.2 10.0 %copy-start.4 = (f32[192,1]{1,0:T(8,128)S(1)}, f32[192,1]{1,0:T(8,128)}, u32[]{:S(2)}) copy-start(f32[192,1]{1,0:T(8,128)} %get-tuple-element.37) | copy-start | bytes 2308
  438.8 7.5 %slice-start = ((s8[4718592]{0:T(1024)(128)(4,1)}), s8[4194304]{0:T(1024)(128)(4,1)S(1)}, s32[]{:S(2)}) async-start(s8[4718592]{0:T(1024)(128)(4,1)} %bitcast.53), calls=%async_computation.2 | async-start | bytes 8388608
  438.8 7.5 %slice-start.1 = ((s8[4718592]{0:T(1024)(128)(4,1)}), s8[524288]{0:T(1024)(128)(4,1)S(1)}, s32[]{:S(2)}) async-start(s8[4718592]{0:T(1024)(128)(4,1)} %bitcast.53), calls=%async_computation.3 | async-start | bytes 1048576
  438.8 139.3 %copy-start.3 = (f32[1024,768]{1,0:T(8,128)S(1)}, f32[1024,768]{1,0:T(8,128)}, u32[]{:S(2)}) copy-start(f32[1024,768]{1,0:T(8,128)} %get-tuple-element.33) | copy-start | bytes 9437188
Sparse Core Ops, SparseCore 0:
  189.4 249.4 all-reduce.6
  445.8 132.2 all-reduce.4

commit v3 on v2

--- a/solution.py
+++ b/solution.py
@@ -562,10 +562,10 @@
     return jnp.concatenate(rows, 0)
 
 
-def filter_pass(sizes, me, core, produce, middle, consume, tables, work, sems):
+def filter_pass(sizes, me, core, produce, middle, consume, tables, work, sems, tick):
     regions, blocks, block_size, chips, cols, tokens = sizes
     table_in, table_out, ahead, behind = tables
-    sent, got, zonal, zonal_got, tall, flat, turned, back, sibling, leaving, coming = work
+    sent, got, zonal, zonal_got, tall, flat, back, sibling, leaving, coming = work
     send_a, recv_a, send_b, recv_b, send_c, recv_c, send_d, recv_d = sems
     lanes = 128
     senders = chips // cols
@@ -581,6 +581,7 @@
             src = sent.at[region, pl.ds(pl.multiple_of(target % blocks * block_size, 32), block_size)]
             place = region * blocks + step
             send_piece(src, got.at[me], send_a.at[place], recv_a.at[me], target, me, core, cols)
+    tick("sent")
 
     def zonal_step(chip, carry):
         for col in range(cols):
@@ -604,6 +605,7 @@
         device_id_type=MESH,
     )
     swap.start()
+    tick("zonal")
 
     def widen(source, first):
         def step(point, carry):
@@ -628,6 +630,7 @@
         return carry
 
     lax.fori_loop(0, half, turn_step, 0)
+    tick("turned")
 
     def mode_step(step, carry):
         rows = pl.ds(pl.multiple_of(step * group * half, 64), group * half)
@@ -640,13 +643,16 @@
         rest = (out - high.astype(wide)).astype(low)
         y = (dot(high, behind[...]) + dot(rest, behind[...])).astype(low).astype(wide)
         for i in range(4):
-            turned[i, rows, :] = y[:, i * lanes : (i + 1) * lanes]
+            flat[i, rows, :] = y[:, i * lanes : (i + 1) * lanes]
         return carry
 
-    lax.fori_loop(0, modes // group, mode_step, 0)
+    lax.fori_loop(0, modes // group // 2, mode_step, 0)
+    tick("halfway")
+    lax.fori_loop(modes // group // 2, modes // group, mode_step, 0)
+    tick("modes")
 
     def return_step(c, carry):
-        x = jnp.concatenate([turned[i, pl.ds(c, modes, stride=half), :] for i in range(4)], 0)
+        x = jnp.concatenate([flat[i, pl.ds(c, modes, stride=half), :] for i in range(4)], 0)
         y = jnp.transpose(x)
         for side in range(2):
             tall[pl.ds(c + half * side, 2 * points, stride=block_size), :] = y[
@@ -680,6 +686,7 @@
         device_id_type=MESH,
     )
     swap_back.start()
+    tick("back")
     narrow(to_self, core * points)
     swap_back.wait_send()
     await_piece(sibling.at[1 - core], recv_c)
@@ -704,6 +711,7 @@
         return carry
 
     lax.fori_loop(0, senders, column_step, 0)
+    tick("columns")
     for region in range(regions):
 
         def arrive(block, carry):
@@ -713,6 +721,7 @@
 
         lax.fori_loop(0, blocks, arrive, 0)
         consume(region)
+        tick("region")
 
     for place in range(regions * blocks):
         region, step = place // blocks, place % blocks
@@ -739,7 +748,6 @@
         pltpu.VMEM((2, points, block_size, lanes), low),
         pltpu.VMEM((points, block_size, lanes), low),
         pltpu.VMEM((2 * points * block_size, lanes), wide),
-        pltpu.VMEM((4, rows, lanes), wide),
         pltpu.VMEM((4, rows, lanes), wide),
         pltpu.VMEM((points, block_size, lanes), low),
         pltpu.VMEM((2, points, block_size, lanes), low),
@@ -798,7 +806,7 @@
         act_ref,
         pre_ref,
     ) = refs[:21]
-    work, sems = refs[21:32], refs[32:]
+    work, sems = refs[21:31], refs[31:]
     regions, blocks, block_size, chips, cols, tokens = sizes
     me, core = greet(chips, cols)
     sent, coming = work[0], work[-1]
@@ -849,7 +857,141 @@
         lax.fori_loop(0, tokens // 256, step, 0)
 
     tables = (to_modes, to_columns, ahead, behind)
-    filter_pass(sizes, me, core, produce, middle, consume, tables, work, sems)
+    filter_pass(
+        sizes, me, core, produce, middle, consume, tables, work, sems, lambda place: None
+    )
+
+
+def place_of(row, col):
+    return {"core": row % 2, "x": (row // 2) % 2, "z": row // 4, "y": col}
+
+
+def device_at(spot):
+    return (spot["z"] * 4 + spot["x"] * 2 + spot["core"], spot["y"])
+
+
+def across(spot, axis, step=1):
+    size = 4 if axis == "z" else 2
+    return device_at({**spot, axis: (spot[axis] + step) % size})
+
+
+def remote(src, dst, send_sem, recv_sem, device):
+    return pltpu.make_async_remote_copy(
+        src_ref=src,
+        dst_ref=dst,
+        send_sem=send_sem,
+        recv_sem=recv_sem,
+        device_id=device,
+        device_id_type=MESH,
+    )
+
+
+def add_rows(out_ref, out_row, terms, rows):
+    step = 48
+
+    def add(part, carry):
+        total = 0.0
+        for ref, row in terms:
+            here = pl.ds(pl.multiple_of(row + part * step, 16), step)
+            total = total + ref[here, :].astype(wide)
+        there = pl.ds(pl.multiple_of(out_row + part * step, 16), step)
+        out_ref[there, :] = total.astype(low)
+        return carry
+
+    lax.fori_loop(0, rows // step, add, 0)
+
+
+def tile_sum(spot, order, own, total, halves, quarters, pieces, sends, recvs):
+    first, second = order
+    side = own.shape[0]
+    half, quarter, piece = side // 2, side // 4, side // 16
+    a, b, z = spot[first], spot[second], spot["z"]
+
+    def part(ref, row, rows):
+        return ref.at[pl.ds(pl.multiple_of(row, 16), rows)]
+
+    mine_a = a * half
+    mine_b = mine_a + b * quarter
+    mine_z = mine_b + z * piece
+    out = part(total, mine_z, piece)
+    hop_a = remote(
+        part(own, (1 - a) * half, half), halves, sends.at[0], recvs.at[0], across(spot, first)
+    )
+    hop_b = remote(
+        part(halves, (1 - b) * quarter, quarter),
+        quarters,
+        sends.at[1],
+        recvs.at[1],
+        across(spot, second),
+    )
+    hops_z = [
+        remote(
+            part(quarters, (z + step) % 4 * piece, piece),
+            pieces.at[step - 1],
+            sends.at[1 + step],
+            recvs.at[1 + step],
+            across(spot, "z", step),
+        )
+        for step in (2, 1, 3)
+    ]
+    back_z = [
+        remote(out, out, sends.at[4 + step], recvs.at[4 + step], across(spot, "z", step))
+        for step in (2, 1, 3)
+    ]
+    quarter_ref = part(total, mine_b, quarter)
+    half_ref = part(total, mine_a, half)
+    back_b = remote(quarter_ref, quarter_ref, sends.at[8], recvs.at[8], across(spot, second))
+    back_a = remote(half_ref, half_ref, sends.at[9], recvs.at[9], across(spot, first))
+    back_core = remote(total, total, sends.at[10], recvs.at[10], across(spot, "core"))
+
+    def start_a():
+        hop_a.start()
+
+    def start_b():
+        hop_a.wait()
+        add_rows(halves, 0, ((halves, 0), (own, mine_a)), half)
+        hop_b.start()
+
+    def start_z():
+        hop_b.wait()
+        add_rows(quarters, 0, ((quarters, 0), (halves, b * quarter)), quarter)
+        for hop in hops_z:
+            hop.start()
+
+    def start_back_z():
+        for hop in hops_z:
+            hop.wait()
+        terms = ((quarters, z * piece), (pieces.at[0], 0), (pieces.at[1], 0), (pieces.at[2], 0))
+        add_rows(total, mine_z, terms, piece)
+        for hop in back_z:
+            hop.start()
+
+    def start_back_b():
+        for hop in back_z:
+            hop.wait()
+        back_b.start()
+
+    def start_back_a():
+        back_b.wait()
+        back_a.start()
+
+    def start_back_core():
+        back_a.wait()
+        back_core.start()
+
+    def finish():
+        back_core.wait()
+
+    return (
+        start_a,
+        start_b,
+        start_z,
+        start_back_z,
+        start_back_b,
+        start_back_a,
+        start_back_core,
+        finish,
+    )
 
 
 def backward_kernel(sizes, *refs):
@@ -866,24 +1008,86 @@
         behind,
         eye,
         spectrum_ref,
-        first_ref,
+        first_hbm,
         act_ref,
-        pre_ref,
+        pre_hbm,
+        project_ref,
+        expand_ref,
+        vectors_ref,
         slope_ref,
-        gain_slope,
-        shift_slope,
+        project_total,
+        expand_total,
+        gathered,
+        vector_sum,
+    ) = refs[:23]
+    work, sems = refs[23:33], refs[33:41]
+    (
         kernel_slope,
         bias_slope,
         mixer_slope,
         offset_slope,
-    ) = refs[:22]
-    work, sems = refs[22:33], refs[33:]
+        first_slots,
+        pre_slots,
+        slot_sems,
+        halves,
+        quarters,
+        pieces,
+        tile_sends,
+        tile_recvs,
+        slab,
+        slab_sibling,
+        slab_region,
+        slab_sends,
+        slab_recvs,
+        vector_sent,
+        vector_got,
+        vector_sends,
+        vector_recvs,
+    ) = refs[41:]
     regions, blocks, block_size, chips, cols, tokens = sizes
+    steps = spectrum_ref.shape[0]
+
+    def fetch(step, slot):
+        return [
+            pltpu.make_async_copy(hbm.at[step], slots.at[slot], slot_sems.at[k, slot])
+            for k, (hbm, slots) in enumerate(((first_hbm, first_slots), (pre_hbm, pre_slots)))
+        ]
+
+    for copy in fetch(0, 0):
+        copy.start()
     me, core = greet(chips, cols)
+    spot = place_of(lax.axis_index("rows"), lax.axis_index("cols"))
+    block = me % blocks
     sent, coming = work[0], work[-1]
     piece = 128
-    for ref in (gain_slope, shift_slope, kernel_slope, bias_slope, mixer_slope, offset_slope):
+    vector_sum[...] = vectors_ref[...]
+    for ref in (kernel_slope, bias_slope, mixer_slope, offset_slope):
         ref[...] = jnp.zeros_like(ref)
+    tiles = []
+    for j in range(2):
+        width = project_ref.shape[1]
+        first = pl.multiple_of((core * 2 + j) * width, width)
+        places = (project_total.at[pl.ds(first, width)], expand_total.at[:, pl.ds(first, width)])
+        for k, own in enumerate((project_ref, expand_ref)):
+            s = j * 2 + k
+            order = ("x", "y") if j == 0 else ("y", "x")
+            tiles.append(
+                tile_sum(
+                    spot,
+                    order,
+                    own.at[j],
+                    places[k],
+                    halves.at[s],
+                    quarters.at[s],
+                    pieces.at[s],
+                    tile_sends.at[s],
+                    tile_recvs.at[s],
+                )
+            )
+
+    def run_tiles(phase, which=(0, 1, 2, 3)):
+        for s in which:
+            tiles[s][phase]()
 
     def produce(region):
         def step(part, carry):
@@ -896,12 +1100,20 @@
         lax.fori_loop(0, tokens // piece, step, 0)
 
     def middle(step, shrunk_back):
-        level = jnp.tanh(pre_ref[step] / shrink_width)
-        second = shrunk_back * (level * level)
-        offset_slope[...] += jnp.sum(second.astype(low).astype(wide), 1, keepdims=True)
-        second = second.astype(low)
+        slot = step % 2
+        for copy in fetch(step, slot):
+            copy.wait()
+
+        @pl.when(step + 1 < steps)
+        def _():
+            for copy in fetch(step + 1, 1 - slot):
+                copy.start()
+
+        level = jnp.tanh(pre_slots[slot] / shrink_width)
+        second = (shrunk_back * (level * level)).astype(low)
+        offset_slope[...] += jnp.sum(second.astype(wide), 1, keepdims=True)
         mixer_slope[...] += dot_last(act_ref[step], second)
-        first = (dot(mixer_ref[...], second) * gelu_slope(first_ref[step])).astype(low)
+        first = (dot(mixer_ref[...], second) * gelu_slope(first_slots[slot])).astype(low)
         bias_slope[...] += jnp.sum(first.astype(wide), 1, keepdims=True)
         kernel_slope[...] += dot_last(spectrum_ref[step], first)
         return dot(kernel_ref[...], first)
@@ -920,8 +1132,8 @@
             unit, factor = normalise(tokens_ref[rows, :].astype(wide))
             mixed_back = mixed_back_ref[rows, :]
             normed_back = mixed_back + mask_ref[rows, :] * fields
-            gain_slope[...] += jnp.sum(normed_back * unit, 0, keepdims=True)
-            shift_slope[...] += jnp.sum(normed_back, 0, keepdims=True)
+            vector_sum[0:1, :] += jnp.sum(normed_back * unit, 0, keepdims=True)
+            vector_sum[1:2, :] += jnp.sum(normed_back, 0, keepdims=True)
             pull = normed_back * gain_ref[...]
             pull = pull - jnp.mean(pull, -1, keepdims=True) - unit * jnp.mean(
                 pull * unit, -1, keepdims=True
@@ -931,22 +1143,331 @@
 
         lax.fori_loop(0, tokens // 256, step, 0)
 
+    side = 2 * block_size
+    slab_core = remote(
+        slab, slab_sibling, slab_sends.at[0], slab_recvs.at[0], across(spot, "core")
+    )
+    my_rows = pl.ds(pl.multiple_of(core * side, 32), side)
+    slab_far = remote(
+        slab_sibling.at[my_rows],
+        slab_region,
+        slab_sends.at[1],
+        slab_recvs.at[1],
+        chip_device((me + blocks) % chips, core, cols),
+    )
+
+    def slab_peer(step):
+        other = me // blocks * blocks + (block + step) % blocks
+        ref = gathered.at[block, my_rows]
+        return remote(
+            ref, ref, slab_sends.at[1 + step], slab_recvs.at[1 + step], chip_device(other, core, cols)
+        )
+
+    slab_last = remote(
+        gathered.at[:, my_rows],
+        gathered.at[:, my_rows],
+        slab_sends.at[1 + blocks],
+        slab_recvs.at[1 + blocks],
+        across(spot, "core"),
+    )
+
+    def slab_start():
+        for k, (weight, bias) in enumerate(
+            ((kernel_slope, bias_slope), (mixer_slope, offset_slope))
+        ):
+            whole = weight[...]
+            upper, lower = whole[:block_size], whole[block_size:]
+            first = k * side
+            slab[first : first + block_size, :block_size] = (
+                upper[:, :block_size] + lower[:, block_size:]
+            )
+            slab[first + block_size : first + side, :block_size] = (
+                upper[:, block_size:] - lower[:, :block_size]
+            )
+            slab[first : first + side, block_size:] = jnp.broadcast_to(
+                bias[...], (side, slab.shape[1] - block_size)
+            )
+        slab_core.start()
+
+    def slab_regions():
+        slab_core.wait()
+        slab_sibling[...] = slab_sibling[...] + slab[...]
+        slab_far.start()
+
+    def slab_blocks():
+        slab_far.wait()
+        gathered[block, my_rows] = slab_region[...] + slab_sibling[my_rows, :]
+        for step in range(1, blocks):
+            slab_peer(step).start()
+
+    def slab_cores():
+        for step in range(1, blocks):
+            slab_peer(step).wait()
+        slab_last.start()
+
+    regions_seen = []
+
+    def tick(place):
+        if place == "sent":
+            run_tiles(0)
+        if place == "zonal":
+            run_tiles(1)
+        if place == "turned":
+            run_tiles(2)
+        if place == "modes":
+            run_tiles(3)
+            slab_start()
+        if place == "back":
+            slab_regions()
+        if place == "columns":
+            run_tiles(4)
+            slab_blocks()
+        if place == "region":
+            regions_seen.append(place)
+            if len(regions_seen) == 1:
+                run_tiles(5)
+                slab_cores()
+
     tables = (to_columns, to_modes, ahead, behind)
-    filter_pass(sizes, me, core, produce, middle, consume, tables, work, sems)
-
-
-def call_filter(body, sizes, outs, cid, operands):
+    filter_pass(sizes, me, core, produce, middle, consume, tables, work, sems, tick)
+    hops = [
+        remote(
+            vector_sent.at[k],
+            vector_got.at[k],
+            vector_sends.at[k],
+            vector_recvs.at[k],
+            device,
+        )
+        for k, device in enumerate(
+            (
+                across(spot, "core"),
+                across(spot, "x"),
+                across(spot, "y"),
+                device_at({**spot, "z": spot["z"] // 2 * 2 + 1 - spot["z"] % 2}),
+                across(spot, "z", 2),
+            )
+        )
+    ]
+    for k, hop in enumerate(hops):
+        vector_sent[k] = vector_sum[...]
+        hop.start()
+        if k == 0:
+            run_tiles(6)
+            slab_last.wait()
+        hop.wait()
+        vector_sum[...] = vector_sum[...] + vector_got[k]
+    run_tiles(7)
+
+
+def call_filter(body, sizes, outs, cid, operands, spaces=(), scratch=()):
     shapes = [jax.ShapeDtypeStruct(shape, kind) for shape, kind in outs]
+    anywhere = pl.BlockSpec(memory_space=pl.ANY)
     return pl.pallas_call(
         functools.partial(body, sizes),
         out_shape=shapes,
-        in_specs=[vmem] * len(operands),
+        in_specs=[anywhere if place in spaces else vmem for place in range(len(operands))],
         out_specs=[vmem] * len(shapes),
-        scratch_shapes=work_shapes(sizes),
+        scratch_shapes=[*work_shapes(sizes), *scratch],
+        compiler_params=pltpu.CompilerParams(
+            collective_id=cid, has_side_effects=True, vmem_limit_bytes=60 * 1024 * 1024
+        ),
+    )(*operands)
+
+
+def backward_scratch(sizes, features, steps):
+    regions, blocks, block_size, chips, cols, tokens = sizes
+    side = 2 * block_size
+    dma = pltpu.SemaphoreType.DMA
+    return (
+        pltpu.VMEM((side, side), wide),
+        pltpu.VMEM((side, 1), wide),
+        pltpu.VMEM((side, side), wide),
+        pltpu.VMEM((side, 1), wide),
+        pltpu.VMEM((2, side, 512), wide),
+        pltpu.VMEM((2, side, 512), wide),
+        dma((2, 2)),
+        pltpu.VMEM((4, features // 2, features), low),
+        pltpu.VMEM((4, features // 4, features), low),
+        pltpu.VMEM((4, 3, features // 16, features), low),
+        dma((4, 11)),
+        dma((4, 11)),
+        pltpu.VMEM((2 * side, 128), wide),
+        pltpu.VMEM((2 * side, 128), wide),
+        pltpu.VMEM((side, 128), wide),
+        dma((2 + blocks,)),
+        dma((2 + blocks,)),
+        pltpu.VMEM((5, 16, features), wide),
+        pltpu.VMEM((5, 16, features), wide),
+        dma((5,)),
+        dma((5,)),
+    )
+
+
+by_first = (((0,), (0,)), ((), ()))
+
+
+def dot_first(a, b):
+    return lax.dot_general(a, b, by_first, preferred_element_type=wide)
+
+
+def dense_kernel(sizes, *refs):
+    tile, half_tiles, cols = sizes
+    (
+        second_ref,
+        mixed_ref,
+        up_ref,
+        scale_ref,
+        expand_ref,
+        lift_ref,
+        project_ref,
+        return_ref,
+        out_ref,
+        mixed_back_ref,
+        project_half,
+        expand_half,
+        vectors,
+        out_sum,
+        back_sum,
+        hidden_tile,
+        back_tile,
+        project_sent,
+        expand_sent,
+        project_got,
+        expand_got,
+        sent_sem,
+        got_sem,
+    ) = refs
+    row = lax.axis_index("rows")
+    core = row % 2
+    sibling = (row - core + 1 - core, lax.axis_index("cols"))
+    barrier = pltpu.get_barrier_semaphore()
+    pl.semaphore_signal(barrier, inc=1, device_id=sibling, device_id_type=MESH)
+    count = second_ref.shape[0]
+    piece = 512
+
+    def tile_step(place):
+        here = pl.ds(pl.multiple_of(place * tile, tile), tile)
+
+        def piece_step(part, carry):
+            rows = pl.ds(pl.multiple_of(part * piece, piece), piece)
+            pre = dot(second_ref[rows, :], expand_ref[:, here]) + lift_ref[:, here]
+            back = dot_last(up_ref[rows, :], project_ref[here, :])
+            curve = gelu_parts(pre)
+            bell = jnp.exp(-0.5 * pre * pre) * (1.0 / math.sqrt(2.0 * math.pi))
+            hidden = (pre * curve).astype(low)
+            hidden_tile[rows, :] = hidden
+            pre_back = (back * (curve + pre * bell)).astype(low)
+            back_tile[rows, :] = pre_back
+            out_sum[rows, :] += dot(hidden, project_ref[here, :])
+            back_sum[rows, :] += dot_last(pre_back, expand_ref[:, here])
+            return carry + jnp.sum(pre_back.astype(wide), 0, keepdims=True)
+
+        lift = lax.fori_loop(0, count // piece, piece_step, jnp.zeros((1, tile), wide))
+        vectors[pl.ds(5 + place, 1), :] = lift
+        return (
+            dot_first(hidden_tile[...], up_ref[...]),
+            dot_first(second_ref[...], back_tile[...]),
+        )
+
+    def start_step(part, carry):
+        rows = pl.ds(pl.multiple_of(part * piece, piece), piece)
+        out_sum[rows, :] = mixed_ref[rows, :] + return_ref[...]
+        back_sum[rows, :] = jnp.zeros((piece, back_sum.shape[1]), wide)
+        return carry + jnp.sum(up_ref[rows, :].astype(wide), 0, keepdims=True)
+
+    vectors[...] = jnp.zeros_like(vectors)
+    vectors[4:5, :] = lax.fori_loop(0, count // piece, start_step, jnp.zeros((1, tile), wide))
+    pl.semaphore_wait(barrier, 1)
+
+    def copies(place):
+        return [
+            pltpu.make_async_remote_copy(
+                src_ref=src.at[place],
+                dst_ref=dst.at[place],
+                send_sem=sent_sem.at[k, place],
+                recv_sem=got_sem.at[k, place],
+                device_id=sibling,
+                device_id_type=MESH,
+            )
+            for k, (src, dst) in enumerate(
+                ((project_sent, project_got), (expand_sent, expand_got))
+            )
+        ]
+
+    def away_step(place, carry):
+        project, expand = tile_step((1 - core) * half_tiles + place)
+        project_sent[place] = project.astype(low)
+        expand_sent[place] = expand.astype(low)
+        for copy in copies(place):
+            copy.start()
+        return carry
+
+    lax.fori_loop(0, half_tiles, away_step, 0)
+
+    def home_step(place, carry):
+        project, expand = tile_step(core * half_tiles + place)
+        for copy in copies(place):
+            copy.wait()
+        project_half[place] = (project + project_got[place].astype(wide)).astype(low)
+        expand_half[place] = (expand + expand_got[place].astype(wide)).astype(low)
+        return carry
+
+    lax.fori_loop(0, half_tiles, home_step, 0)
+
+    def end_step(part, carry):
+        rows = pl.ds(pl.multiple_of(part * piece, piece), piece)
+        out_ref[rows, :] = out_sum[rows, :].astype(low)
+        unit, factor = normalise(mixed_ref[rows, :])
+        norm_back = back_sum[rows, :]
+        vectors[2:3, :] += jnp.sum(norm_back * unit, 0, keepdims=True)
+        vectors[3:4, :] += jnp.sum(norm_back, 0, keepdims=True)
+        pull = norm_back * scale_ref[...]
+        pull = pull - jnp.mean(pull, -1, keepdims=True) - unit * jnp.mean(
+            pull * unit, -1, keepdims=True
+        )
+        mixed_back_ref[rows, :] = up_ref[rows, :].astype(wide) + factor * pull
+        return carry
+
+    lax.fori_loop(0, count // piece, end_step, 0)
+
+
+def call_dense(second_norm, mixed, upstream, exit_scale, expand, lift, project, returned, tile, cid):
+    count, features = second_norm.shape
+    hidden = expand.shape[1]
+    half_tiles = hidden // tile // 2
+    tall = (half_tiles, tile, features)
+    broad = (half_tiles, features, tile)
+    outs = (
+        ((count, features), low),
+        ((count, features), wide),
+        (tall, low),
+        (broad, low),
+        ((16, features), wide),
+    )
+    shapes = [jax.ShapeDtypeStruct(shape, kind) for shape, kind in outs]
+    work = 6 * count * features * hidden * 2
+    return pl.pallas_call(
+        functools.partial(dense_kernel, (tile, half_tiles, 0)),
+        out_shape=shapes,
+        in_specs=[vmem] * 8,
+        out_specs=[vmem] * len(shapes),
+        scratch_shapes=[
+            pltpu.VMEM((count, features), wide),
+            pltpu.VMEM((count, features), wide),
+            pltpu.VMEM((count, tile), low),
+            pltpu.VMEM((count, tile), low),
+            pltpu.VMEM(tall, low),
+            pltpu.VMEM(broad, low),
+            pltpu.VMEM(tall, low),
+            pltpu.VMEM(broad, low),
+            pltpu.SemaphoreType.DMA((2, half_tiles)),
+            pltpu.SemaphoreType.DMA((2, half_tiles)),
+        ],
         compiler_params=pltpu.CompilerParams(
             collective_id=cid, has_side_effects=True, vmem_limit_bytes=58 * 1024 * 1024
         ),
-    )(*operands)
+        cost_estimate=pl.CostEstimate(flops=work, bytes_accessed=40000000, transcendentals=0),
+    )(second_norm, mixed, upstream, exit_scale, expand, lift, project, returned)
 
 
 def shards(
@@ -980,6 +1501,8 @@
         and rows_here == 8
         and block_size == 96
         and blocks == 8
+        and regions == 2
+        and dense_expand.shape == (features, 4 * features)
     )
     if not fits:
         return shards_general(
@@ -1057,36 +1580,27 @@
             eye,
         ),
     )
-    hidden_pre = dot(second_norm, dense_expand) + dense_lift
-    hidden = gelu_exact(hidden_pre).astype(low)
-    output = mixed + (dot(hidden, dense_project) + dense_return)
-    project_part = jnp.einsum("tf,tc->fc", hidden, upstream, preferred_element_type=wide)
-    return_part = jnp.sum(upstream.astype(wide), 0)
-    hidden_back = dot_last(upstream, dense_project)
-    pre_back = (hidden_back * gelu_slope(hidden_pre)).astype(low)
-    expand_part = jnp.einsum("tc,tf->cf", second_norm, pre_back, preferred_element_type=wide)
-    lift_part = jnp.sum(pre_back.astype(wide), 0)
-    norm_back = dot_last(pre_back, dense_expand)
-    unit, factor = normalise(mixed)
-    scale_part = jnp.sum(norm_back * unit, 0)
-    center_part = jnp.sum(norm_back, 0)
-    pull = norm_back * exit_scale
-    pull = pull - jnp.mean(pull, -1, keepdims=True) - unit * jnp.mean(pull * unit, -1, keepdims=True)
-    mixed_back = upstream.astype(wide) + factor * pull
-    everywhere = ("rows", "cols")
-    project_sum = lax.psum(project_part.astype(low), everywhere).astype(wide)
-    expand_sum = lax.psum(expand_part.astype(low), everywhere).astype(wide)
-    slopes = call_filter(
+    output, mixed_back, project_half, expand_half, vectors = call_dense(
+        second_norm,
+        mixed,
+        upstream,
+        exit_scale[None],
+        dense_expand,
+        dense_lift[None],
+        dense_project,
+        dense_return[None],
+        features,
+        3,
+    )
+    slope, project_sum, expand_sum, gathered, sums = call_filter(
         backward_kernel,
         sizes,
         (
             ((count, features), wide),
-            ((1, features), wide),
-            ((1, features), wide),
-            ((side, side), wide),
-            ((side, 1), wide),
-            ((side, side), wide),
-            ((side, 1), wide),
+            (dense_project.shape, low),
+            (dense_expand.shape, low),
+            ((blocks, 2 * side, 128), wide),
+            ((16, features), wide),
         ),
         2,
         (
@@ -1105,52 +1619,31 @@
             first_pre,
             first_act,
             second_pre,
+            project_half,
+            expand_half,
+            vectors,
         ),
-    )
-    token_slope, gain_part, shift_part, kernel_part, bias_part, mixer_part, offset_part = slopes
-
-    def spread(part):
-        total = jnp.zeros(part.shape[:1] + (blocks,) + part.shape[2:], wide)
-        return lax.dynamic_update_slice_in_dim(total, part, block, 1)
-
-    whole = (
-        spread(matrix_gradient(kernel_part[None], block_size)),
-        spread(matrix_gradient(mixer_part[None], block_size)),
-        spread(bias_part.reshape(2, 1, block_size)),
-        spread(offset_part.reshape(2, 1, block_size)),
-    )
-    vectors = (
-        gain_part[0],
-        shift_part[0],
-        scale_part,
-        center_part,
-        lift_part,
-        return_part,
-        whole[2].reshape(-1),
-        whole[3].reshape(-1),
-    )
-    sums = lax.psum(jnp.concatenate(vectors), everywhere)
-    parts = []
-    first = 0
-    for vector in vectors:
-        parts.append(sums[first : first + vector.shape[0]])
-        first += vector.shape[0]
-    kernel_sum, mixer_sum = lax.psum((whole[0], whole[1]), everywhere)
+        (12, 14),
+        backward_scratch(sizes, features, steps),
+    )
+    weights = gathered[:, :, :block_size].reshape(blocks, 2, 2, block_size, block_size)
+    weights = weights.transpose(1, 2, 0, 3, 4)
+    biases = gathered[:, :, block_size].reshape(blocks, 2, 2, block_size).transpose(1, 2, 0, 3)
     return (
-        output.astype(low).reshape(tokens.shape),
-        token_slope.reshape(tokens.shape),
-        parts[0],
-        parts[1],
-        kernel_sum,
-        parts[6].reshape(spectral_bias.shape),
-        mixer_sum,
-        parts[7].reshape(spectral_bias.shape),
-        parts[2],
-        parts[3],
-        expand_sum,
-        parts[4],
-        project_sum,
-        parts[5],
+        output.reshape(tokens.shape),
+        slope.reshape(tokens.shape),
+        sums[0],
+        sums[1],
+        weights[0],
+        biases[0],
+        weights[1],
+        biases[1],
+        sums[2],
+        sums[3],
+        expand_sum.astype(wide),
+        sums[5:9].reshape(-1),
+        project_sum.astype(wide),
+        sums[4],
     )
 
 

time: 591 us -> 400 us (0.68)
  waiting for transfers between devices: 159 us -> 0 us
  Pallas kernels: 231 us -> 359 us
  matrix products: 80.8 us -> 0 us
  blocking collectives: 59.3 us -> 0 us
  between operations: 14.5 us -> 0.79 us
  other arithmetic: 23.7 us -> 12.7 us
    psum x2 -> x0, waiting for transfers between devices: 159 us -> none  [the longest x1 127 us: shards(): kernel_sum, mixer_sum = lax.psum((whole[0], whole[1]), everywhere)]
    pallas_call x2, Pallas kernels: 231 us -> 314 us  [call_filter(): pl.pallas_call(functools.partial(body, sizes), out_shape=shapes, in_specs...]
    dot_general x6 -> x0, matrix products: 80.8 us -> none  [the longest x2 44 us: dot(): return jnp.dot(a, b, preferred_element_type=wide)]
    psum x1 -> x0, blocking collectives: 59.3 us -> none  [shards(): sums = lax.psum(jnp.concatenate(vectors), everywhere)]
    pallas_call x0 -> x1, Pallas kernels: none -> 45.2 us  [call_dense(): pl.pallas_call(functools.partial(dense_kernel, (tile, half_tiles, 0)), ou...]
  transfers between devices with their start and end apart: 2 -> 0, of which waited for: 2 -> 0; matrix products, arithmetic and copies ran while one was open for 8% -> 0% of each run, Pallas kernels for 21% -> 0%
where the time goes in v3:
time: 400 us
  Pallas kernels  359 us (90%)
  local copies, waits for them, and re-layouts  27 us (7%)
  other arithmetic  12.7 us (3%)
    pallas_call x2, Pallas kernels, call_filter(): pl.pallas_call(functools.partial(body, sizes), out_shape=shapes, in_specs...  314 us
    pallas_call x1, Pallas kernels, call_dense(): pl.pallas_call(functools.partial(dense_kernel, (tile, half_tiles, 0)), ou...  45.2 us

profile of v3, /device:TPU:0, one launch (start us, length us, event | category | flops | bytes accessed | tf_op | source)
XLA Modules:
  0.0 399.7 jit_solution(5600455057542267423)
XLA Ops:
  0.7 1.0 slice_reduce_fusion.7
  3.2 1.3 broadcast_in_dim.33.refs_2_.refs_3_
  4.5 1.3 broadcast_in_dim.35.refs_4_.refs_3_
  5.8 1.3 broadcast_in_dim.34.refs_3_
  7.0 1.3 broadcast_in_dim.36.refs_5_
  8.3 1.3 broadcast_in_dim.38.refs_7_
  9.6 0.8 dynamic-slice_bitcast_fusion.1
  10.4 0.8 reshape.219.refs_7_
  11.2 0.8 fusion.8
  12.0 0.8 reshape.220.refs_9_
  15.8 1.3 select_n.48.refs_1_.refs_2_
  17.0 105.2 %shard_map.326 = (f32[1024,768]{1,0:T(8,128)}, bf16[1024,768]{1,0:T(8,128)(2,1)}, bf16[8,192,512]{2,1,0:T(8,128)(2,1)}, f32[8,192,512]{2,1,0:T(8,128)}, bf16[8,1...) custom-call(bf16[1024,768]{1,0:T(8,128)(2,1)} %bitcast.39, f32[1024,1]{1,0:T(8,128)} %select_n.48.refs_1_.refs_2_, ...), custom_call_target="tpu_custom_call" | custom-call | tf_op jit(solution)/shard_map/pallas_call | solution.py:1265
  122.3 45.2 %shard_map.327 = (bf16[1024,768]{1,0:T(8,128)(2,1)}, f32[1024,768]{1,0:T(8,128)}, bf16[2,768,768]{2,1,0:T(8,128)(2,1)}, bf16[2,768,768]{2,1,0:T(8,128)(2,1)}, f32[16,768]{1,0:T(8,128)}) custom-call(bf16[1024,768]{1,0:T(8,128)(2,1)} %get-tuple-element.30.refs_0_, f32[1024,768]{1,0:T(8,128)} %get-tuple-element.31.refs_1_, bf16[1024,768]{1,0:T(8,128)(2,1)} %bitcast.48, ...), custom_call_target="tpu_custom_call" | custom-call | flops 28991029248 | bytes 40000000 | tf_op jit(solution)/shard_map/pallas_call | solution.py:1449
  167.5 208.8 %shard_map.328 = (f32[1024,768]{1,0:T(8,128)}, bf16[3072,768]{1,0:T(8,128)(2,1)}, bf16[768,3072]{1,0:T(8,128)(2,1)}, f32[8,384,128]{2,1,0:T(8,128)}, f32[16,768]{1,0:T(8,128)}) custom-call(bf16[1024,768]{1,0:T(8,128)(2,1)} %bitcast.40, f32[1024,768]{1,0:T(8,128)} %get-tuple-element.33.refs_1_, f32[1024,1]{1,0:T(8,128)} %select_n.48.refs_1_.refs_2_, ...), custom_call_target="tpu_custom_call" | custom-call | tf_op jit(solution)/shard_map/pallas_call | solution.py:1265
  376.3 0.9 slice.73
  377.2 1.6 slice_reduce_fusion.1
  379.5 2.3 slice_reduce_fusion
  383.2 1.3 slice_bitcast_fusion
  384.5 1.5 copy-done.1
  386.0 5.0 %convert_element_type.6 = f32[768,3072]{1,0:T(8,128)} convert(bf16[768,3072]{1,0:T(8,128)(2,1)S(1)} %copy-done.1) | non-fusion elementwise | flops 2359296 | bytes 14155776 | tf_op jit(solution)/shard_map/convert_element_type | solution.py:1643
  391.1 4.5 %convert_element_type.7 = f32[3072,768]{1,0:T(8,128)} convert(bf16[3072,768]{1,0:T(8,128)(2,1)S(1)} %bitcast.44) | non-fusion elementwise | flops 2359296 | bytes 14155776 | tf_op jit(solution)/shard_map/convert_element_type | solution.py:1645
  395.6 1.1 copy.54
  396.7 1.3 copy-done.2
  398.0 1.7 copy.55
  (27 shorter events, 6.6 us)
Async XLA Ops:
  376.3 6.8 %copy-start = (f32[8,384,128]{2,1,0:T(8,128)S(1)}, f32[8,384,128]{2,1,0:T(8,128)}, u32[]{:S(2)}) copy-start(f32[8,384,128]{2,1,0:T(8,128)} %get-tuple-element.43) | copy-start | bytes 4718596
  383.1 2.9 copy-start.1
  383.2 7.8 %slice-start = ((s8[4718592]{0:T(1024)(128)(4,1)}), s8[4194304]{0:T(1024)(128)(4,1)S(1)}, s32[]{:S(2)}) async-start(s8[4718592]{0:T(1024)(128)(4,1)} %bitcast.43), calls=%async_computation | async-start | bytes 8388608
  386.0 5.1 %slice-start.1 = ((s8[4718592]{0:T(1024)(128)(4,1)}), s8[524288]{0:T(1024)(128)(4,1)S(1)}, s32[]{:S(2)}) async-start(s8[4718592]{0:T(1024)(128)(4,1)} %bitcast.43), calls=%async_computation.1 | async-start | bytes 1048576
  391.1 4.5 %copy-start.3 = (bf16[1024,768]{1,0:T(8,128)(2,1)S(1)}, bf16[1024,768]{1,0:T(8,128)(2,1)}, u32[]{:S(2)}) copy-start(bf16[1024,768]{1,0:T(8,128)(2,1)} %get-tuple-element.32) | copy-start | bytes 4718596
  395.5 2.5 copy-start.2

commit v4 on v3

--- a/solution.py
+++ b/solution.py
@@ -402,6 +402,7 @@
 wide = jnp.float32
 low = jnp.bfloat16
 by_last = (((1,), (1,)), ((), ()))
+by_first = (((0,), (0,)), ((), ()))
 vmem = pl.BlockSpec(memory_space=pltpu.VMEM)
 
 
@@ -411,6 +412,10 @@
 
 def dot_last(a, b):
     return lax.dot_general(a, b, by_last, preferred_element_type=wide)
+
+
+def dot_first(a, b):
+    return lax.dot_general(a, b, by_first, preferred_element_type=wide)
 
 
 def task_tables(height, width, rows_here, cols_here):
@@ -574,16 +579,19 @@
     points = senders * pairs
     group = 4
     bits = (blocks - 1).bit_length()
-    for region in range(regions):
+    home = me // blocks
+    for turn in range(regions):
+        region = (home + 1 + turn) % regions
         produce(region)
         for step in range(blocks - 1, -1, -1):
             target = region * blocks + swap_bits(me % blocks, step, bits)
             src = sent.at[region, pl.ds(pl.multiple_of(target % blocks * block_size, 32), block_size)]
-            place = region * blocks + step
+            place = turn * blocks + step
             send_piece(src, got.at[me], send_a.at[place], recv_a.at[me], target, me, core, cols)
     tick("sent")
 
-    def zonal_step(chip, carry):
+    def zonal_step(index, carry):
+        chip = (index + home * senders // regions) % senders
         for col in range(cols):
             await_piece(got.at[chip * cols + col], recv_a.at[chip * cols + col])
         for pair in range(pairs):
@@ -629,7 +637,7 @@
             flat[i, pl.ds(c, modes, stride=half), :] = y[i * modes : (i + 1) * modes]
         return carry
 
-    lax.fori_loop(0, half, turn_step, 0)
+    lax.fori_loop(0, half, turn_step, 0, unroll=4)
     tick("turned")
 
     def mode_step(step, carry):
@@ -660,7 +668,8 @@
             ]
         return carry
 
-    lax.fori_loop(0, half, return_step, 0)
+    lax.fori_loop(0, half, return_step, 0, unroll=4)
+    tick("returned")
 
     def narrow(store, first):
         def step(point, carry):
@@ -691,7 +700,8 @@
     swap_back.wait_send()
     await_piece(sibling.at[1 - core], recv_c)
 
-    def column_step(chip, carry):
+    def column_step(index, carry):
+        chip = (index + (home + 1) * senders // regions) % senders
         for pair in range(pairs):
             point = chip * pairs + pair
             x = jnp.concatenate([sibling[0, point], sibling[1, point]], 1)
@@ -712,9 +722,10 @@
 
     lax.fori_loop(0, senders, column_step, 0)
     tick("columns")
-    for region in range(regions):
-
-        def arrive(block, carry):
+    for turn in range(regions):
+        region = (home + turn) % regions
+
+        def arrive(block, carry, region=region):
             ref = coming.at[region, pl.ds(pl.multiple_of(block * block_size, 32), block_size)]
             await_piece(ref, recv_d.at[region * blocks + block])
             return carry
@@ -724,8 +735,8 @@
         tick("region")
 
     for place in range(regions * blocks):
-        region, step = place // blocks, place % blocks
-        target = region * blocks + swap_bits(me % blocks, step, bits)
+        turn, step = place // blocks, place % blocks
+        target = (home + 1 + turn) % regions * blocks + swap_bits(me % blocks, step, bits)
 
         @pl.when(target != me)
         def _():
@@ -782,84 +793,141 @@
     return gelu_parts(value) + value * bell
 
 
+def inside_region(sizes_ref, starts_ref, region, first, shape, width):
+    rows, rows_here, cols_here = shape
+    index = first + lax.broadcasted_iota(jnp.int32, (rows, 1), 0)
+    bits = cols_here.bit_length() - 1
+    latitude = lax.axis_index("rows") * rows_here + lax.shift_right_logical(index, bits)
+    longitude = lax.axis_index("cols") * cols_here + (index & (cols_here - 1))
+    offset = longitude - starts_ref[region]
+    offset = jnp.where(offset < 0, offset + width, offset)
+    near = jnp.where(latitude < sizes_ref[region, 0], 1.0, 0.0)
+    return jnp.where(offset < sizes_ref[region, 1], near, 0.0)
+
+
+def as_row(ref):
+    return ref[...].reshape(1, ref.shape[0])
+
+
+def field_rows(coming, region, place, eye):
+    return jnp.concatenate(
+        [
+            dot_last(eye, coming[region, first : first + 256, place])
+            for first in range(0, coming.shape[1], 256)
+        ],
+        1,
+    )
+
+
 def forward_kernel(sizes, *refs):
     (
+        region_sizes,
+        region_starts,
         tokens_ref,
-        mask_ref,
         gain_ref,
         shift_ref,
         scale_ref,
         center_ref,
-        kernel_ref,
-        bias_ref,
-        mixer_ref,
-        offset_ref,
+        weights_ref,
+        biases_ref,
         to_modes,
         to_columns,
         ahead,
         behind,
         eye,
-        mixed_ref,
-        second_ref,
-        spectrum_ref,
-        first_ref,
-        act_ref,
-        pre_ref,
-    ) = refs[:21]
-    work, sems = refs[21:31], refs[31:]
+        mixed_hbm,
+        second_hbm,
+        *kept_hbm,
+    ) = refs[:20]
+    work, sems = refs[20:30], refs[30:38]
+    mixed, second, mixed_sems, second_sems, kept_sems, *kept = refs[38:]
     regions, blocks, block_size, chips, cols, tokens = sizes
     me, core = greet(chips, cols)
     sent, coming = work[0], work[-1]
     piece = 128
+    steps = kept_hbm[0].shape[0]
+    cols_here = 128 // cols
+    gain, shift, scale, center = (
+        as_row(ref) for ref in (gain_ref, shift_ref, scale_ref, center_ref)
+    )
+
+    def inside(region, first, rows):
+        shape = (rows, tokens // cols_here, cols_here)
+        return inside_region(region_sizes, region_starts, region, first, shape, 128)
 
     def produce(region):
         def step(part, carry):
             rows = pl.ds(pl.multiple_of(region * tokens + part * piece, piece), piece)
             unit, factor = normalise(tokens_ref[rows, :].astype(wide))
-            normed = unit * gain_ref[...] + shift_ref[...]
+            values = (inside(region, part * piece, piece) * (unit * gain + shift)).astype(low)
             place = pl.ds(pl.multiple_of(part * piece, piece), piece)
-            to_feature_rows(sent, region, place, (mask_ref[rows, :] * normed).astype(low), eye[...])
+            to_feature_rows(sent, region, place, values, eye[...])
             return carry
 
         lax.fori_loop(0, tokens // piece, step, 0)
 
+    def keep(step):
+        slot = step % 2
+        return [
+            pltpu.make_async_copy(ref.at[slot], hbm.at[step], kept_sems.at[k, slot])
+            for k, (ref, hbm) in enumerate(zip(kept, kept_hbm))
+        ]
+
     def middle(step, spectrum):
+        slot = step % 2
+
+        @pl.when(step >= 2)
+        def _():
+            for copy in keep(step - 2):
+                copy.wait()
+
+        spectrum_kept, first_kept, act_kept, second_kept = kept
         spectrum = spectrum.astype(low)
-        spectrum_ref[step] = spectrum
-        first = dot(kernel_ref[...], spectrum) + bias_ref[...]
-        first_ref[step] = first
+        spectrum_kept[slot] = spectrum
+        first = dot_first(weights_ref[0], spectrum) + biases_ref[:, 0:1]
+        first_kept[slot] = first
         act = (first * gelu_parts(first)).astype(low)
-        act_ref[step] = act
-        second = dot(mixer_ref[...], act) + offset_ref[...]
-        pre_ref[step] = second
-        return second - shrink_width * jnp.tanh(second / shrink_width)
+        act_kept[slot] = act
+        second_pre = dot_first(weights_ref[1], act) + biases_ref[:, 1:2]
+        second_kept[slot] = second_pre
+        for copy in keep(step):
+            copy.start()
+        return second_pre - shrink_width * jnp.tanh(second_pre / shrink_width)
+
+    def leave(region):
+        rows = pl.ds(pl.multiple_of(region * tokens, tokens), tokens)
+        return [
+            pltpu.make_async_copy(mixed.at[rows], mixed_hbm.at[rows], mixed_sems.at[region]),
+            pltpu.make_async_copy(second.at[rows], second_hbm.at[rows], second_sems.at[region]),
+        ]
 
     def consume(region):
         def step(part, carry):
             rows = pl.ds(pl.multiple_of(region * tokens + part * 256, 256), 256)
             place = pl.ds(pl.multiple_of(part * 256, 256), 256)
-            fields = jnp.concatenate(
-                [
-                    dot_last(eye[...], coming[region, first : first + 256, place])
-                    for first in range(0, coming.shape[1], 256)
-                ],
-                1,
-            )
+            fields = field_rows(coming, region, place, eye[...])
             residual = tokens_ref[rows, :].astype(wide)
             unit, factor = normalise(residual)
-            normed = unit * gain_ref[...] + shift_ref[...]
-            mixed = residual + mask_ref[rows, :] * fields + normed
-            mixed_ref[rows, :] = mixed
-            unit, factor = normalise(mixed)
-            second_ref[rows, :] = (unit * scale_ref[...] + center_ref[...]).astype(low)
+            value = residual + inside(region, part * 256, 256) * fields + (unit * gain + shift)
+            mixed[rows, :] = value
+            unit, factor = normalise(value)
+            second[rows, :] = (unit * scale + center).astype(low)
             return carry
 
         lax.fori_loop(0, tokens // 256, step, 0)
+        for copy in leave(region):
+            copy.start()
 
     tables = (to_modes, to_columns, ahead, behind)
     filter_pass(
         sizes, me, core, produce, middle, consume, tables, work, sems, lambda place: None
     )
+    for step in (steps - 2, steps - 1):
+        for copy in keep(step):
+            copy.wait()
+    for region in range(regions):
+        for copy in leave(region):
+            copy.wait()
 
 
 def place_of(row, col):
@@ -901,120 +969,115 @@
     lax.fori_loop(0, rows // step, add, 0)
 
 
-def tile_sum(spot, order, own, total, halves, quarters, pieces, sends, recvs):
-    first, second = order
-    side = own.shape[0]
-    half, quarter, piece = side // 2, side // 4, side // 16
-    a, b, z = spot[first], spot[second], spot["z"]
-
-    def part(ref, row, rows):
-        return ref.at[pl.ds(pl.multiple_of(row, 16), rows)]
-
-    mine_a = a * half
-    mine_b = mine_a + b * quarter
-    mine_z = mine_b + z * piece
-    out = part(total, mine_z, piece)
-    hop_a = remote(
-        part(own, (1 - a) * half, half), halves, sends.at[0], recvs.at[0], across(spot, first)
-    )
-    hop_b = remote(
-        part(halves, (1 - b) * quarter, quarter),
-        quarters,
-        sends.at[1],
-        recvs.at[1],
-        across(spot, second),
-    )
-    hops_z = [
-        remote(
-            part(quarters, (z + step) % 4 * piece, piece),
-            pieces.at[step - 1],
-            sends.at[1 + step],
-            recvs.at[1 + step],
-            across(spot, "z", step),
+def row_part(ref, row, rows):
+    return ref.at[pl.ds(pl.multiple_of(row, 16), rows)]
+
+
+def facing(spot, axis):
+    if axis == "near":
+        z = spot["z"] // 2 * 2 + 1 - spot["z"] % 2
+        return spot["z"] % 2, device_at({**spot, "z": z})
+    if axis == "far":
+        return spot["z"] // 2, across(spot, "z", 2)
+    return spot[axis], across(spot, axis)
+
+
+def reduce_steps(spot, axes, buffers, sends, recvs):
+    steps = []
+    for k, axis in enumerate(axes):
+        bit, device = facing(spot, axis)
+        source, target = buffers[k], buffers[k + 1]
+        rows = target.shape[0]
+        hop = remote(
+            row_part(source, (1 - bit) * rows, rows), target, sends.at[k], recvs.at[k], device
         )
-        for step in (2, 1, 3)
-    ]
-    back_z = [
-        remote(out, out, sends.at[4 + step], recvs.at[4 + step], across(spot, "z", step))
-        for step in (2, 1, 3)
-    ]
-    quarter_ref = part(total, mine_b, quarter)
-    half_ref = part(total, mine_a, half)
-    back_b = remote(quarter_ref, quarter_ref, sends.at[8], recvs.at[8], across(spot, second))
-    back_a = remote(half_ref, half_ref, sends.at[9], recvs.at[9], across(spot, first))
-    back_core = remote(total, total, sends.at[10], recvs.at[10], across(spot, "core"))
-
-    def start_a():
-        hop_a.start()
-
-    def start_b():
-        hop_a.wait()
-        add_rows(halves, 0, ((halves, 0), (own, mine_a)), half)
-        hop_b.start()
-
-    def start_z():
-        hop_b.wait()
-        add_rows(quarters, 0, ((quarters, 0), (halves, b * quarter)), quarter)
-        for hop in hops_z:
-            hop.start()
-
-    def start_back_z():
-        for hop in hops_z:
+
+        def finish(hop=hop, source=source, target=target, rows=rows, bit=bit):
             hop.wait()
-        terms = ((quarters, z * piece), (pieces.at[0], 0), (pieces.at[1], 0), (pieces.at[2], 0))
-        add_rows(total, mine_z, terms, piece)
-        for hop in back_z:
-            hop.start()
-
-    def start_back_b():
-        for hop in back_z:
-            hop.wait()
-        back_b.start()
-
-    def start_back_a():
-        back_b.wait()
-        back_a.start()
-
-    def start_back_core():
-        back_a.wait()
-        back_core.start()
+            add_rows(target, 0, ((target, 0), (source, bit * rows)), rows)
+
+        steps.append((hop.start, finish))
+    return steps
+
+
+def share_steps(spot, axes, piece, total, sends, recvs, own_sem):
+    offsets, rows, bits, devices = [0], [total.shape[0]], [], []
+    for axis in axes:
+        bit, device = facing(spot, axis)
+        bits.append(bit)
+        devices.append(device)
+        rows.append(rows[-1] // 2)
+        offsets.append(offsets[-1] + bit * rows[-1])
+    last = len(axes) - 1
+    hops = []
+    for k in range(last, -1, -1):
+        place = row_part(total, offsets[k + 1], rows[k + 1])
+        source = piece if k == last else place
+        hops.append(remote(source, place, sends.at[k], recvs.at[k], devices[k]))
+    keep = pltpu.make_async_copy(piece, row_part(total, offsets[-1], rows[-1]), own_sem)
+    ready = (
+        (offsets[2], rows[2]),
+        (offsets[1] + (1 - bits[1]) * rows[2], rows[2]),
+        ((1 - bits[0]) * rows[1], rows[1]),
+    )
+    cores = []
+    for k, (offset, size) in enumerate(ready):
+        place = row_part(total, offset, size)
+        cores.append(
+            remote(place, place, sends.at[4 + k], recvs.at[4 + k], across(spot, "core"))
+        )
+
+    def begin():
+        keep.start()
+        hops[0].start()
+
+    def second():
+        keep.wait()
+        hops[0].wait()
+        hops[1].start()
+
+    def third():
+        hops[1].wait()
+        hops[2].start()
+        cores[0].start()
+
+    def fourth():
+        hops[2].wait()
+        hops[3].start()
+        cores[1].start()
+
+    def fifth():
+        hops[3].wait()
+        cores[2].start()
 
     def finish():
-        back_core.wait()
-
-    return (
-        start_a,
-        start_b,
-        start_z,
-        start_back_z,
-        start_back_b,
-        start_back_a,
-        start_back_core,
-        finish,
-    )
+        for core in cores:
+            core.wait()
+
+    return begin, second, third, fourth, fifth, finish
 
 
 def backward_kernel(sizes, *refs):
     (
-        tokens_ref,
+        region_sizes,
+        region_starts,
+        tokens_hbm,
         mixed_back_ref,
-        mask_ref,
         gain_ref,
-        kernel_ref,
-        mixer_ref,
+        weights_ref,
         to_modes,
         to_columns,
         ahead,
         behind,
         eye,
-        spectrum_ref,
+        spectrum_hbm,
         first_hbm,
-        act_ref,
+        act_hbm,
         pre_hbm,
-        project_ref,
-        expand_ref,
-        vectors_ref,
-        slope_ref,
+        own_hbm,
+        ready_ref,
+        sums_ref,
+        slope_hbm,
         project_total,
         expand_total,
         gathered,
@@ -1022,18 +1085,29 @@
     ) = refs[:23]
     work, sems = refs[23:33], refs[33:41]
     (
+        tokens_ref,
+        slope,
+        slope_sems,
+        own,
+        load_sems,
         kernel_slope,
         bias_slope,
         mixer_slope,
         offset_slope,
+        spectrum_slots,
         first_slots,
+        act_slots,
         pre_slots,
         slot_sems,
         halves,
         quarters,
+        eighths,
         pieces,
-        tile_sends,
-        tile_recvs,
+        reduce_sends,
+        reduce_recvs,
+        share_sends,
+        share_recvs,
+        own_sems,
         slab,
         slab_sibling,
         slab_region,
@@ -1043,57 +1117,84 @@
         vector_got,
         vector_sends,
         vector_recvs,
+        late,
+        late_got,
+        late_all,
+        late_sends,
+        late_recvs,
     ) = refs[41:]
     regions, blocks, block_size, chips, cols, tokens = sizes
-    steps = spectrum_ref.shape[0]
+    steps = spectrum_hbm.shape[0]
+    slots = (spectrum_slots, first_slots, act_slots, pre_slots)
+    streams = (spectrum_hbm, first_hbm, act_hbm, pre_hbm)
 
     def fetch(step, slot):
         return [
-            pltpu.make_async_copy(hbm.at[step], slots.at[slot], slot_sems.at[k, slot])
-            for k, (hbm, slots) in enumerate(((first_hbm, first_slots), (pre_hbm, pre_slots)))
+            pltpu.make_async_copy(hbm.at[step], ref.at[slot], slot_sems.at[k, slot])
+            for k, (hbm, ref) in enumerate(zip(streams, slots))
         ]
 
+    load_own = pltpu.make_async_copy(own_hbm.at[1], own, load_sems.at[0])
+    load_tokens = pltpu.make_async_copy(tokens_hbm, tokens_ref, load_sems.at[1])
+    load_own.start()
     for copy in fetch(0, 0):
         copy.start()
+    load_tokens.start()
     me, core = greet(chips, cols)
     spot = place_of(lax.axis_index("rows"), lax.axis_index("cols"))
     block = me % blocks
     sent, coming = work[0], work[-1]
     piece = 128
-    vector_sum[...] = vectors_ref[...]
+    cols_here = 128 // cols
+    width = own.shape[1]
+    late[...] = jnp.zeros_like(late)
+    vector_sum[...] = sums_ref[...]
     for ref in (kernel_slope, bias_slope, mixer_slope, offset_slope):
         ref[...] = jnp.zeros_like(ref)
-    tiles = []
+    reducing, sharing = [], []
     for j in range(2):
-        width = project_ref.shape[1]
-        first = pl.multiple_of((core * 2 + j) * width, width)
-        places = (project_total.at[pl.ds(first, width)], expand_total.at[:, pl.ds(first, width)])
-        for k, own in enumerate((project_ref, expand_ref)):
+        place = pl.multiple_of((core * 2 + j) * width, width)
+        totals = (project_total.at[pl.ds(place, width)], expand_total.at[:, pl.ds(place, width)])
+        for k in range(2):
             s = j * 2 + k
-            order = ("x", "y") if j == 0 else ("y", "x")
-            tiles.append(
-                tile_sum(
-                    spot,
-                    order,
-                    own.at[j],
-                    places[k],
-                    halves.at[s],
-                    quarters.at[s],
-                    pieces.at[s],
-                    tile_sends.at[s],
-                    tile_recvs.at[s],
+            axes = (("x", "y"), ("y", "x"))[k] + ("near", "far")
+            buffers = (own.at[k], halves.at[k], quarters.at[k], eighths.at[s], pieces.at[s])
+            if j == 0:
+                buffers = (ready_ref.at[k],) + buffers[3:]
+            reducing.append(
+                reduce_steps(
+                    spot, axes[5 - len(buffers) :], buffers, reduce_sends.at[s], reduce_recvs.at[s]
                 )
             )
-
-    def run_tiles(phase, which=(0, 1, 2, 3)):
-        for s in which:
-            tiles[s][phase]()
+            sharing.append(
+                share_steps(
+                    spot,
+                    axes,
+                    pieces.at[s],
+                    totals[k],
+                    share_sends.at[s],
+                    share_recvs.at[s],
+                    own_sems.at[s],
+                )
+            )
+
+    def reduce(j, step, finish):
+        for steps_of in reducing[j * 2 : j * 2 + 2]:
+            steps_of[step][finish]()
+
+    def share(j, step):
+        for steps_of in sharing[j * 2 : j * 2 + 2]:
+            steps_of[step]()
+
+    def inside(region, first, rows):
+        shape = (rows, tokens // cols_here, cols_here)
+        return inside_region(region_sizes, region_starts, region, first, shape, 128)
 
     def produce(region):
         def step(part, carry):
             rows = pl.ds(pl.multiple_of(region * tokens + part * piece, piece), piece)
             place = pl.ds(pl.multiple_of(part * piece, piece), piece)
-            values = (mask_ref[rows, :] * mixed_back_ref[rows, :]).astype(low)
+            values = (inside(region, part * piece, piece) * mixed_back_ref[rows, :]).astype(low)
             to_feature_rows(sent, region, place, values, eye[...])
             return carry
 
@@ -1112,36 +1213,38 @@
         level = jnp.tanh(pre_slots[slot] / shrink_width)
         second = (shrunk_back * (level * level)).astype(low)
         offset_slope[...] += jnp.sum(second.astype(wide), 1, keepdims=True)
-        mixer_slope[...] += dot_last(act_ref[step], second)
-        first = (dot(mixer_ref[...], second) * gelu_slope(first_slots[slot])).astype(low)
+        mixer_slope[...] += dot_last(act_slots[slot], second)
+        first = (dot(weights_ref[1], second) * gelu_slope(first_slots[slot])).astype(low)
         bias_slope[...] += jnp.sum(first.astype(wide), 1, keepdims=True)
-        kernel_slope[...] += dot_last(spectrum_ref[step], first)
-        return dot(kernel_ref[...], first)
+        kernel_slope[...] += dot_last(spectrum_slots[slot], first)
+        return dot(weights_ref[0], first)
+
+    def leave(region):
+        rows = pl.ds(pl.multiple_of(region * tokens, tokens), tokens)
+        return pltpu.make_async_copy(slope.at[rows], slope_hbm.at[rows], slope_sems.at[region])
 
     def consume(region):
         def step(part, carry):
             rows = pl.ds(pl.multiple_of(region * tokens + part * 256, 256), 256)
             place = pl.ds(pl.multiple_of(part * 256, 256), 256)
-            fields = jnp.concatenate(
-                [
-                    dot_last(eye[...], coming[region, first : first + 256, place])
-                    for first in range(0, coming.shape[1], 256)
-                ],
-                1,
-            )
+            fields = field_rows(coming, region, place, eye[...])
             unit, factor = normalise(tokens_ref[rows, :].astype(wide))
             mixed_back = mixed_back_ref[rows, :]
-            normed_back = mixed_back + mask_ref[rows, :] * fields
-            vector_sum[0:1, :] += jnp.sum(normed_back * unit, 0, keepdims=True)
-            vector_sum[1:2, :] += jnp.sum(normed_back, 0, keepdims=True)
-            pull = normed_back * gain_ref[...]
+            normed_back = mixed_back + inside(region, part * 256, 256) * fields
+            gains = jnp.sum(normed_back * unit, 0, keepdims=True)
+            shifts = jnp.sum(normed_back, 0, keepdims=True)
+            for k in range(3):
+                late[k : k + 1, :] += gains[:, k * 256 : (k + 1) * 256]
+                late[3 + k : 4 + k, :] += shifts[:, k * 256 : (k + 1) * 256]
+            pull = normed_back * as_row(gain_ref)
             pull = pull - jnp.mean(pull, -1, keepdims=True) - unit * jnp.mean(
                 pull * unit, -1, keepdims=True
             )
-            slope_ref[rows, :] = mixed_back + factor * pull
+            slope[rows, :] = mixed_back + factor * pull
             return carry
 
         lax.fori_loop(0, tokens // 256, step, 0)
+        leave(region).start()
 
     side = 2 * block_size
     slab_core = remote(
@@ -1205,92 +1308,163 @@
             slab_peer(step).wait()
         slab_last.start()
 
+    partners = (
+        across(spot, "core"),
+        across(spot, "x"),
+        across(spot, "y"),
+        device_at({**spot, "z": spot["z"] // 2 * 2 + 1 - spot["z"] % 2}),
+        across(spot, "z", 2),
+    )
+    hops = [
+        remote(
+            vector_sent.at[k], vector_got.at[k], vector_sends.at[k], vector_recvs.at[k], device
+        )
+        for k, device in enumerate(partners)
+    ]
+
+    def vector_step(k):
+        if k > 0:
+            hops[k - 1].wait()
+            vector_sum[...] = vector_sum[...] + vector_got[k - 1]
+        if k < len(hops):
+            vector_sent[k] = vector_sum[...]
+            hops[k].start()
+
     regions_seen = []
 
     def tick(place):
         if place == "sent":
-            run_tiles(0)
+            load_own.wait()
+            reduce(1, 0, 0)
+            vector_step(0)
         if place == "zonal":
-            run_tiles(1)
+            reduce(1, 0, 1)
+            reduce(1, 1, 0)
+            reduce(0, 0, 0)
+            vector_step(1)
         if place == "turned":
-            run_tiles(2)
+            reduce(0, 0, 1)
+            reduce(0, 1, 0)
+            reduce(1, 1, 1)
+            reduce(1, 2, 0)
+            vector_step(2)
+        if place == "halfway":
+            reduce(0, 1, 1)
+            share(0, 0)
+            reduce(1, 2, 1)
+            reduce(1, 3, 0)
+            vector_step(3)
         if place == "modes":
-            run_tiles(3)
             slab_start()
+            share(0, 1)
+            reduce(1, 3, 1)
+            share(1, 0)
+            vector_step(4)
+        if place == "returned":
+            share(0, 2)
+            share(1, 1)
+            vector_step(5)
         if place == "back":
             slab_regions()
         if place == "columns":
-            run_tiles(4)
+            load_tokens.wait()
             slab_blocks()
+            share(0, 3)
+            share(1, 2)
+            share(1, 3)
+            slab_cores()
         if place == "region":
             regions_seen.append(place)
             if len(regions_seen) == 1:
-                run_tiles(5)
-                slab_cores()
+                share(0, 4)
 
     tables = (to_columns, to_modes, ahead, behind)
     filter_pass(sizes, me, core, produce, middle, consume, tables, work, sems, tick)
-    hops = [
-        remote(
-            vector_sent.at[k],
-            vector_got.at[k],
-            vector_sends.at[k],
-            vector_recvs.at[k],
-            device,
-        )
-        for k, device in enumerate(
-            (
-                across(spot, "core"),
-                across(spot, "x"),
-                across(spot, "y"),
-                device_at({**spot, "z": spot["z"] // 2 * 2 + 1 - spot["z"] % 2}),
-                across(spot, "z", 2),
-            )
-        )
-    ]
-    for k, hop in enumerate(hops):
-        vector_sent[k] = vector_sum[...]
-        hop.start()
-        if k == 0:
-            run_tiles(6)
-            slab_last.wait()
-        hop.wait()
-        vector_sum[...] = vector_sum[...] + vector_got[k]
-    run_tiles(7)
-
-
-def call_filter(body, sizes, outs, cid, operands, spaces=(), scratch=()):
+    late_core = remote(late, late_got, late_sends.at[0], late_recvs.at[0], across(spot, "core"))
+    late_core.start()
+    late_core.wait()
+    late[...] = late[...] + late_got[...]
+    late_all[me] = late[...]
+
+    def late_hop(step):
+        other = chip_device((me + step) % chips, core, cols)
+        return remote(late, late_all.at[me], late_sends.at[step], late_recvs.at[step], other)
+
+    for step in range(1, chips):
+        late_hop(step).start()
+    slab_last.wait()
+    share(1, 4)
+    share(0, 5)
+    share(1, 5)
+    for step in range(1, chips):
+        late_hop(step).wait()
+    total = late_all[0]
+    for chip in range(1, chips):
+        total = total + late_all[chip]
+    for k in range(3):
+        vector_sum[0:1, k * 256 : (k + 1) * 256] = total[k : k + 1, :]
+        vector_sum[1:2, k * 256 : (k + 1) * 256] = total[3 + k : 4 + k, :]
+    for region in range(regions):
+        leave(region).wait()
+
+
+def call_filter(body, sizes, outs, cid, operands, scalars, spaces, out_spaces, scratch):
     shapes = [jax.ShapeDtypeStruct(shape, kind) for shape, kind in outs]
     anywhere = pl.BlockSpec(memory_space=pl.ANY)
+    scalar = pl.BlockSpec(memory_space=pltpu.SMEM)
     return pl.pallas_call(
         functools.partial(body, sizes),
         out_shape=shapes,
-        in_specs=[anywhere if place in spaces else vmem for place in range(len(operands))],
-        out_specs=[vmem] * len(shapes),
+        in_specs=[scalar] * len(scalars)
+        + [anywhere if place in spaces else vmem for place in range(len(operands))],
+        out_specs=[anywhere if place in out_spaces else vmem for place in range(len(outs))],
         scratch_shapes=[*work_shapes(sizes), *scratch],
         compiler_params=pltpu.CompilerParams(
             collective_id=cid, has_side_effects=True, vmem_limit_bytes=60 * 1024 * 1024
         ),
-    )(*operands)
-
-
-def backward_scratch(sizes, features, steps):
+    )(*scalars, *operands)
+
+
+def forward_scratch(sizes, kept):
     regions, blocks, block_size, chips, cols, tokens = sizes
+    dma = pltpu.SemaphoreType.DMA
+    features = blocks * block_size
+    return (
+        pltpu.VMEM((regions * tokens, features), wide),
+        pltpu.VMEM((regions * tokens, features), low),
+        dma((regions,)),
+        dma((regions,)),
+        dma((len(kept), 2)),
+        *(pltpu.VMEM((2, *shape[1:]), kind) for shape, kind in kept),
+    )
+
+
+def backward_scratch(sizes, kept):
+    regions, blocks, block_size, chips, cols, tokens = sizes
+    features = blocks * block_size
     side = 2 * block_size
     dma = pltpu.SemaphoreType.DMA
     return (
+        pltpu.VMEM((regions * tokens, features), low),
+        pltpu.VMEM((regions * tokens, features), wide),
+        dma((regions,)),
+        pltpu.VMEM((2, features, features), low),
+        dma((2,)),
         pltpu.VMEM((side, side), wide),
         pltpu.VMEM((side, 1), wide),
         pltpu.VMEM((side, side), wide),
         pltpu.VMEM((side, 1), wide),
-        pltpu.VMEM((2, side, 512), wide),
-        pltpu.VMEM((2, side, 512), wide),
-        dma((2, 2)),
-        pltpu.VMEM((4, features // 2, features), low),
-        pltpu.VMEM((4, features // 4, features), low),
-        pltpu.VMEM((4, 3, features // 16, features), low),
-        dma((4, 11)),
-        dma((4, 11)),
+        *(pltpu.VMEM((2, *shape[1:]), kind) for shape, kind in kept),
+        dma((len(kept), 2)),
+        pltpu.VMEM((2, features // 2, features), low),
+        pltpu.VMEM((2, features // 4, features), low),
+        pltpu.VMEM((4, features // 8, features), low),
+        pltpu.VMEM((4, features // 16, features), low),
+        dma((4, 4)),
+        dma((4, 4)),
+        dma((4, 7)),
+        dma((4, 7)),
+        dma((4,)),
         pltpu.VMEM((2 * side, 128), wide),
         pltpu.VMEM((2 * side, 128), wide),
         pltpu.VMEM((side, 128), wide),
@@ -1300,174 +1474,251 @@
         pltpu.VMEM((5, 16, features), wide),
         dma((5,)),
         dma((5,)),
-    )
-
-
-by_first = (((0,), (0,)), ((), ()))
-
-
-def dot_first(a, b):
-    return lax.dot_general(a, b, by_first, preferred_element_type=wide)
-
-
-def dense_kernel(sizes, *refs):
-    tile, half_tiles, cols = sizes
+        pltpu.VMEM((8, 256), wide),
+        pltpu.VMEM((8, 256), wide),
+        pltpu.VMEM((chips, 8, 256), wide),
+        dma((chips,)),
+        dma((chips,)),
+    )
+
+
+def dense_kernel(*refs):
     (
         second_ref,
-        mixed_ref,
         up_ref,
         scale_ref,
+        returned_ref,
+        lift_ref,
+        mixed_hbm,
+        expand_hbm,
+        project_hbm,
+        out_hbm,
+        mixed_back_hbm,
+        own_hbm,
+        ready_ref,
+        vectors,
+        mixed_ref,
         expand_ref,
-        lift_ref,
         project_ref,
-        return_ref,
         out_ref,
-        mixed_back_ref,
-        project_half,
-        expand_half,
-        vectors,
         out_sum,
         back_sum,
         hidden_tile,
         back_tile,
-        project_sent,
-        expand_sent,
-        project_got,
-        expand_got,
+        sent,
+        got,
+        own,
+        halves,
+        load_sems,
+        weight_sems,
+        leave_sems,
+        own_sems,
         sent_sem,
         got_sem,
+        first_sends,
+        first_recvs,
     ) = refs
-    row = lax.axis_index("rows")
-    core = row % 2
-    sibling = (row - core + 1 - core, lax.axis_index("cols"))
+    tile = expand_ref.shape[2]
+    spot = place_of(lax.axis_index("rows"), lax.axis_index("cols"))
+    core = spot["core"]
+    orders = (("x", "y"), ("y", "x"))
+    places = [
+        (1 - core) * 2,
+        core * 2,
+        (1 - core) * 2 + 1,
+        core * 2 + 1,
+    ]
+
+    def weights(k):
+        here = pl.ds(pl.multiple_of(places[k] * tile, tile), tile)
+        return [
+            pltpu.make_async_copy(project_hbm.at[here], project_ref.at[k], weight_sems.at[0, k]),
+            pltpu.make_async_copy(expand_hbm.at[:, here], expand_ref.at[k], weight_sems.at[1, k]),
+        ]
+
+    for k in range(4):
+        for copy in weights(k):
+            copy.start()
+    load_mixed = pltpu.make_async_copy(mixed_hbm, mixed_ref, load_sems.at[0])
+    load_mixed.start()
     barrier = pltpu.get_barrier_semaphore()
-    pl.semaphore_signal(barrier, inc=1, device_id=sibling, device_id_type=MESH)
+    for axis in ("core", "x", "y"):
+        pl.semaphore_signal(barrier, inc=1, device_id=across(spot, axis), device_id_type=MESH)
     count = second_ref.shape[0]
     piece = 512
-
-    def tile_step(place):
-        here = pl.ds(pl.multiple_of(place * tile, tile), tile)
+    vectors[...] = jnp.zeros_like(vectors)
+
+    def start_step(part, carry):
+        rows = pl.ds(pl.multiple_of(part * piece, piece), piece)
+        out_sum[rows, :] = jnp.broadcast_to(as_row(returned_ref), (piece, out_sum.shape[1]))
+        back_sum[rows, :] = jnp.zeros((piece, back_sum.shape[1]), wide)
+        return carry + jnp.sum(up_ref[rows, :].astype(wide), 0, keepdims=True)
+
+    vectors[4:5, :] = lax.fori_loop(0, count // piece, start_step, jnp.zeros((1, tile), wide))
+    pl.semaphore_wait(barrier, 3)
+
+    def tile_step(k, place, between):
+        lift_row = lift_ref[pl.ds(place, 1), :]
 
         def piece_step(part, carry):
             rows = pl.ds(pl.multiple_of(part * piece, piece), piece)
-            pre = dot(second_ref[rows, :], expand_ref[:, here]) + lift_ref[:, here]
-            back = dot_last(up_ref[rows, :], project_ref[here, :])
+            pre = dot(second_ref[rows, :], expand_ref[k]) + lift_row
+            back = dot_last(up_ref[rows, :], project_ref[k])
             curve = gelu_parts(pre)
             bell = jnp.exp(-0.5 * pre * pre) * (1.0 / math.sqrt(2.0 * math.pi))
             hidden = (pre * curve).astype(low)
             hidden_tile[rows, :] = hidden
             pre_back = (back * (curve + pre * bell)).astype(low)
             back_tile[rows, :] = pre_back
-            out_sum[rows, :] += dot(hidden, project_ref[here, :])
-            back_sum[rows, :] += dot_last(pre_back, expand_ref[:, here])
+            out_sum[rows, :] += dot(hidden, project_ref[k])
+            back_sum[rows, :] += dot_last(pre_back, expand_ref[k])
             return carry + jnp.sum(pre_back.astype(wide), 0, keepdims=True)
 
         lift = lax.fori_loop(0, count // piece, piece_step, jnp.zeros((1, tile), wide))
         vectors[pl.ds(5 + place, 1), :] = lift
+        between()
         return (
             dot_first(hidden_tile[...], up_ref[...]),
             dot_first(second_ref[...], back_tile[...]),
         )
 
-    def start_step(part, carry):
+    def swap(j, k):
+        return remote(
+            sent.at[j, k], got.at[j, k], sent_sem.at[j, k], got_sem.at[j, k], across(spot, "core")
+        )
+
+    hops = [
+        reduce_steps(
+            spot,
+            orders[k],
+            (own.at[0, k], halves.at[k], ready_ref.at[k]),
+            first_sends.at[k],
+            first_recvs.at[k],
+        )
+        for k in range(2)
+    ]
+
+    def pair_step(j, carry):
+        for copy in weights_at(2 * j):
+            copy.wait()
+        away = tile_step(2 * j, (1 - core) * 2 + j, lambda: None)
+        for k in range(2):
+            sent[j, k] = away[k].astype(low)
+            swap(j, k).start()
+
+        def forward():
+            @pl.when(j == 1)
+            def _():
+                for hop in hops:
+                    hop[0][1]()
+                    hop[1][0]()
+
+        for copy in weights_at(2 * j + 1):
+            copy.wait()
+        home = tile_step(2 * j + 1, core * 2 + j, forward)
+        for k in range(2):
+            swap(j, k).wait()
+            own[j, k] = (home[k] + got[j, k].astype(wide)).astype(low)
+
+        @pl.when(j == 0)
+        def _():
+            for hop in hops:
+                hop[0][0]()
+
+        return carry
+
+    def weights_at(k):
+        return [
+            pltpu.make_async_copy(project_ref.at[k], project_ref.at[k], weight_sems.at[0, k]),
+            pltpu.make_async_copy(expand_ref.at[k], expand_ref.at[k], weight_sems.at[1, k]),
+        ]
+
+    lax.fori_loop(0, 2, pair_step, 0)
+    keep = pltpu.make_async_copy(own.at[1], own_hbm.at[1], own_sems.at[0])
+    keep.start()
+    load_mixed.wait()
+
+    def leave(part):
         rows = pl.ds(pl.multiple_of(part * piece, piece), piece)
-        out_sum[rows, :] = mixed_ref[rows, :] + return_ref[...]
-        back_sum[rows, :] = jnp.zeros((piece, back_sum.shape[1]), wide)
-        return carry + jnp.sum(up_ref[rows, :].astype(wide), 0, keepdims=True)
-
-    vectors[...] = jnp.zeros_like(vectors)
-    vectors[4:5, :] = lax.fori_loop(0, count // piece, start_step, jnp.zeros((1, tile), wide))
-    pl.semaphore_wait(barrier, 1)
-
-    def copies(place):
         return [
-            pltpu.make_async_remote_copy(
-                src_ref=src.at[place],
-                dst_ref=dst.at[place],
-                send_sem=sent_sem.at[k, place],
-                recv_sem=got_sem.at[k, place],
-                device_id=sibling,
-                device_id_type=MESH,
+            pltpu.make_async_copy(out_ref.at[rows], out_hbm.at[rows], leave_sems.at[0, part]),
+            pltpu.make_async_copy(
+                back_sum.at[rows], mixed_back_hbm.at[rows], leave_sems.at[1, part]
+            ),
+        ]
+
+    def end_step(part, carry):
+        for quarter in range(4):
+            size = piece // 4
+            rows = pl.ds(pl.multiple_of(part * piece + quarter * size, size), size)
+            mixed = mixed_ref[rows, :]
+            out_ref[rows, :] = (out_sum[rows, :] + mixed).astype(low)
+            unit, factor = normalise(mixed)
+            norm_back = back_sum[rows, :]
+            vectors[2:3, :] += jnp.sum(norm_back * unit, 0, keepdims=True)
+            vectors[3:4, :] += jnp.sum(norm_back, 0, keepdims=True)
+            pull = norm_back * as_row(scale_ref)
+            pull = pull - jnp.mean(pull, -1, keepdims=True) - unit * jnp.mean(
+                pull * unit, -1, keepdims=True
             )
-            for k, (src, dst) in enumerate(
-                ((project_sent, project_got), (expand_sent, expand_got))
-            )
-        ]
-
-    def away_step(place, carry):
-        project, expand = tile_step((1 - core) * half_tiles + place)
-        project_sent[place] = project.astype(low)
-        expand_sent[place] = expand.astype(low)
-        for copy in copies(place):
+            back_sum[rows, :] = up_ref[rows, :].astype(wide) + factor * pull
+        for copy in leave(part):
             copy.start()
         return carry
 
-    lax.fori_loop(0, half_tiles, away_step, 0)
-
-    def home_step(place, carry):
-        project, expand = tile_step(core * half_tiles + place)
-        for copy in copies(place):
+    lax.fori_loop(0, count // piece, end_step, 0)
+    for hop in hops:
+        hop[1][1]()
+    keep.wait()
+    for part in range(count // piece):
+        for copy in leave(part):
             copy.wait()
-        project_half[place] = (project + project_got[place].astype(wide)).astype(low)
-        expand_half[place] = (expand + expand_got[place].astype(wide)).astype(low)
-        return carry
-
-    lax.fori_loop(0, half_tiles, home_step, 0)
-
-    def end_step(part, carry):
-        rows = pl.ds(pl.multiple_of(part * piece, piece), piece)
-        out_ref[rows, :] = out_sum[rows, :].astype(low)
-        unit, factor = normalise(mixed_ref[rows, :])
-        norm_back = back_sum[rows, :]
-        vectors[2:3, :] += jnp.sum(norm_back * unit, 0, keepdims=True)
-        vectors[3:4, :] += jnp.sum(norm_back, 0, keepdims=True)
-        pull = norm_back * scale_ref[...]
-        pull = pull - jnp.mean(pull, -1, keepdims=True) - unit * jnp.mean(
-            pull * unit, -1, keepdims=True
-        )
-        mixed_back_ref[rows, :] = up_ref[rows, :].astype(wide) + factor * pull
-        return carry
-
-    lax.fori_loop(0, count // piece, end_step, 0)
-
-
-def call_dense(second_norm, mixed, upstream, exit_scale, expand, lift, project, returned, tile, cid):
+
+
+def call_dense(second_norm, upstream, scale, returned, lift, mixed, expand, project, cid):
     count, features = second_norm.shape
-    hidden = expand.shape[1]
-    half_tiles = hidden // tile // 2
-    tall = (half_tiles, tile, features)
-    broad = (half_tiles, features, tile)
+    square = (features, features)
     outs = (
         ((count, features), low),
         ((count, features), wide),
-        (tall, low),
-        (broad, low),
+        ((2, 2, *square), low),
+        ((2, features // 4, features), low),
         ((16, features), wide),
     )
     shapes = [jax.ShapeDtypeStruct(shape, kind) for shape, kind in outs]
-    work = 6 * count * features * hidden * 2
+    anywhere = pl.BlockSpec(memory_space=pl.ANY)
+    dma = pltpu.SemaphoreType.DMA
     return pl.pallas_call(
-        functools.partial(dense_kernel, (tile, half_tiles, 0)),
+        dense_kernel,
         out_shape=shapes,
-        in_specs=[vmem] * 8,
-        out_specs=[vmem] * len(shapes),
+        in_specs=[vmem] * 5 + [anywhere] * 3,
+        out_specs=[anywhere] * 3 + [vmem] * 2,
         scratch_shapes=[
             pltpu.VMEM((count, features), wide),
+            pltpu.VMEM((4, *square), low),
+            pltpu.VMEM((4, *square), low),
+            pltpu.VMEM((count, features), low),
             pltpu.VMEM((count, features), wide),
-            pltpu.VMEM((count, tile), low),
-            pltpu.VMEM((count, tile), low),
-            pltpu.VMEM(tall, low),
-            pltpu.VMEM(broad, low),
-            pltpu.VMEM(tall, low),
-            pltpu.VMEM(broad, low),
-            pltpu.SemaphoreType.DMA((2, half_tiles)),
-            pltpu.SemaphoreType.DMA((2, half_tiles)),
+            pltpu.VMEM((count, features), wide),
+            pltpu.VMEM((count, features), low),
+            pltpu.VMEM((count, features), low),
+            pltpu.VMEM((2, 2, *square), low),
+            pltpu.VMEM((2, 2, *square), low),
+            pltpu.VMEM((2, 2, *square), low),
+            pltpu.VMEM((2, features // 2, features), low),
+            dma((1,)),
+            dma((2, 4)),
+            dma((2, count // 512)),
+            dma((1,)),
+            dma((2, 2)),
+            dma((2, 2)),
+            dma((2, 2)),
+            dma((2, 2)),
         ],
         compiler_params=pltpu.CompilerParams(
-            collective_id=cid, has_side_effects=True, vmem_limit_bytes=58 * 1024 * 1024
+            collective_id=cid, has_side_effects=True, vmem_limit_bytes=60 * 1024 * 1024
         ),
-        cost_estimate=pl.CostEstimate(flops=work, bytes_accessed=40000000, transcendentals=0),
-    )(second_norm, mixed, upstream, exit_scale, expand, lift, project, returned)
+    )(second_norm, upstream, scale, returned, lift, mixed, expand, project)
 
 
 def shards(
@@ -1525,71 +1776,69 @@
         )
     height = rows_here * row_devices
     width = cols_here * cols
-    latitude = lax.axis_index("rows") * rows_here + jnp.arange(rows_here, dtype=jnp.int32)
-    longitude = lax.axis_index("cols") * cols_here + jnp.arange(cols_here, dtype=jnp.int32)
-    inside_rows = latitude[None, :, None] < region_sizes[:, 0][:, None, None]
-    offset = (longitude[None, None, :] - region_starts[:, None, None]) % width
-    inside_cols = offset < region_sizes[:, 1][:, None, None]
-    mask = jnp.where(inside_rows & inside_cols, 1.0, 0.0).astype(wide).reshape(-1, 1)
     patches = rows_here * cols_here
     count = regions * patches
     sizes = (regions, blocks, block_size, chips, cols, patches)
     block = ((lax.axis_index("rows") // 2) * cols + lax.axis_index("cols")) % blocks
 
     def own(weight):
-        return lax.dynamic_slice_in_dim(weight, block, 1, 1)
-
-    kernel = complex_matrix(own(spectral_kernel))[0]
-    mixer = complex_matrix(own(spectral_mixer))[0]
+        return lax.dynamic_index_in_dim(weight, block, 1, False)
+
+    def square(weight):
+        real, imaginary = weight[0], weight[1]
+        return jnp.concatenate(
+            [
+                jnp.concatenate([real, imaginary], 1),
+                jnp.concatenate([-imaginary, real], 1),
+            ],
+            0,
+        )
+
     side = 2 * block_size
-    kernel_bias = own(spectral_bias).reshape(side, 1)
-    mixer_bias = own(spectral_offset).reshape(side, 1)
+    weights = jnp.stack([square(own(spectral_kernel)), square(own(spectral_mixer))])
+    biases = jnp.stack(
+        [own(spectral_bias).reshape(side), own(spectral_offset).reshape(side)], 1
+    )
     to_modes, to_columns, ahead, behind, eye = task_tables(height, width, rows_here, cols_here)
     flat_tokens = tokens.reshape(count, features)
     upstream = cotangent.reshape(count, features)
-    group = 4 * 128
     steps = width // 4 // 4
-    kept_shape = (steps, side, group)
-    mixed, second_norm, spectrum, first_pre, first_act, second_pre = call_filter(
+    shape = (steps, side, 4 * 128)
+    kept = ((shape, low), (shape, wide), (shape, low), (shape, wide))
+    scalars = (region_sizes, region_starts)
+    mixed, second_norm, *stream = call_filter(
         forward_kernel,
         sizes,
-        (
-            ((count, features), wide),
-            ((count, features), low),
-            (kept_shape, low),
-            (kept_shape, wide),
-            (kept_shape, low),
-            (kept_shape, wide),
-        ),
+        (((count, features), wide), ((count, features), low), *kept),
         1,
         (
             flat_tokens,
-            mask,
-            entry_gain[None],
-            entry_shift[None],
-            exit_scale[None],
-            exit_center[None],
-            kernel.T,
-            kernel_bias,
-            mixer.T,
-            mixer_bias,
+            entry_gain,
+            entry_shift,
+            exit_scale,
+            exit_center,
+            weights,
+            biases,
             to_modes,
             to_columns,
             ahead,
             behind,
             eye,
         ),
-    )
-    output, mixed_back, project_half, expand_half, vectors = call_dense(
+        scalars,
+        (),
+        range(6),
+        forward_scratch(sizes, kept),
+    )
+    output, mixed_back, own_tiles, ready, part_sums = call_dense(
         second_norm,
+        upstream,
+        exit_scale,
+        dense_return,
+        dense_lift.reshape(-1, features),
         mixed,
-        upstream,
-        exit_scale[None],
         dense_expand,
-        dense_lift[None],
         dense_project,
-        dense_return[None],
-        features,
         3,
     )
     slope, project_sum, expand_sum, gathered, sums = call_filter(
@@ -1606,25 +1855,22 @@
         (
             flat_tokens,
             mixed_back,
-            mask,
-            entry_gain[None],
-            kernel,
-            mixer,
+            entry_gain,
+            weights,
             to_modes.T,
             to_columns.T,
             ahead,
             behind,
             eye,
-            spectrum,
-            first_pre,
-            first_act,
-            second_pre,
-            project_half,
-            expand_half,
-            vectors,
+            *stream,
+            own_tiles,
+            ready,
+            part_sums,
         ),
-        (12, 14),
-        backward_scratch(sizes, features, steps),
+        scalars,
+        (0, 9, 10, 11, 12, 13),
+        range(3),
+        backward_scratch(sizes, kept),
     )
     weights = gathered[:, :, :block_size].reshape(blocks, 2, 2, block_size, block_size)
     weights = weights.transpose(1, 2, 0, 3, 4)

time: 400 us -> 333 us (0.83)
  Pallas kernels: 359 us -> 303 us
  local copies, waits for them, and re-layouts: 27 us -> 17.5 us
    pallas_call x2, Pallas kernels: 314 us -> 258 us  [call_filter(): pl.pallas_call(functools.partial(body, sizes), out_shape=shapes, in_specs...]
    broadcast_in_dim x5 -> x0, local copies, waits for them, and re-layouts: 6.33 us -> none  [the longest x1 1.27 us: shards(): entry_gain[None]]
where the time goes in v4:
time: 333 us
  Pallas kernels  303 us (91%)
  local copies, waits for them, and re-layouts  17.5 us (5%)
  other arithmetic  11.2 us (3%)
    pallas_call x2, Pallas kernels, call_filter(): pl.pallas_call(functools.partial(body, sizes), out_shape=shapes, in_specs...  258 us
    pallas_call x1, Pallas kernels, call_dense(): pl.pallas_call(dense_kernel, out_shape=shapes, in_specs=[vmem] * 5 + [any...  45.1 us

profile of v4, /device:TPU:0, one launch (start us, length us, event | category | flops | bytes accessed | tf_op | source)
XLA Modules:
  0.0 332.6 jit_solution(4301742284351939724)
XLA Ops:
  0.7 0.7 fusion
  1.6 1.3 reshape.61.refs_4_
  2.9 0.8 dynamic-slice_bitcast_fusion.1
  3.7 0.8 copy.44.refs_8_
  4.4 0.8 fusion.2
  5.2 0.1 maximum_bitcast_fusion
  5.3 0.1 maximum_bitcast_fusion.1
  5.4 0.7 pad_maximum_fusion.refs_7_.refs_5_
  6.1 99.2 %shard_map.326 = (f32[1024,768]{1,0:T(8,128)}, bf16[1024,768]{1,0:T(8,128)(2,1)}, bf16[8,192,512]{2,1,0:T(8,128)(2,1)}, f32[8,192,512]{2,1,0:T(8,128)}, bf16[8,1...) custom-call(s32[2,2]{1,0:T(2,128)} %refs_0_.3, s32[2]{0:T(128)} %refs_1_.3, bf16[1024,768]{1,0:T(8,128)(2,1)} %bitcast.32, ...), custom_call_target="tpu_custom_call" | custom-call | tf_op jit(solution)/shard_map/pallas_call | solution.py:1415
  105.3 45.1 %shard_map.327 = (bf16[1024,768]{1,0:T(8,128)(2,1)}, f32[1024,768]{1,0:T(8,128)}, bf16[2,2,768,768]{3,2,1,0:T(8,128)(2,1)}, bf16[2,192,768]{2,1,0:T(8,128)(2,1)}, f32[16,768]{1,0:T(8,128)}) custom-call(bf16[1024,768]{1,0:T(8,128)(2,1)} %get-tuple-element.30.refs_0_, bf16[1024,768]{1,0:T(8,128)(2,1)} %bitcast.39, f32[768]{0:T(1024)} %refs_2_.1, f32[768]{0:T(1024)} %refs_3_.3, ...), custom_call_target="tpu_custom_call" | custom-call | tf_op jit(solution)/shard_map/pallas_call | solution.py:1691
  150.5 158.8 %shard_map.328 = (f32[1024,768]{1,0:T(8,128)}, bf16[3072,768]{1,0:T(8,128)(2,1)}, bf16[768,3072]{1,0:T(8,128)(2,1)}, f32[8,384,128]{2,1,0:T(8,128)}, f32[16,768]{1,0:T(8,128)}) custom-call(s32[2,2]{1,0:T(2,128)} %refs_0_.3, s32[2]{0:T(128)} %refs_1_.3, bf16[1024,768]{1,0:T(8,128)(2,1)} %bitcast.33, f32[1024,768]{1,0:T(8,128)} %get-tuple-element.33.refs_3_, ...), custom_call_target="tpu_custom_call" | custom-call | tf_op jit(solution)/shard_map/pallas_call | solution.py:1415
  309.2 0.8 slice.66
  310.0 1.6 slice_reduce_fusion.1
  311.7 0.6 reshape.65
  312.3 2.3 slice_reduce_fusion
  314.7 0.6 copy.47
  315.3 0.6 copy.46
  315.9 1.7 copy.49
  317.6 1.3 slice_bitcast_fusion
  318.9 5.0 %convert_element_type.6 = f32[768,3072]{1,0:T(8,128)} convert(bf16[768,3072]{1,0:T(8,128)(2,1)S(1)} %copy-done) | non-fusion elementwise | flops 2359296 | bytes 14155776 | tf_op jit(solution)/shard_map/convert_element_type | solution.py:1889
  324.0 4.5 %convert_element_type.7 = f32[3072,768]{1,0:T(8,128)} convert(bf16[3072,768]{1,0:T(8,128)(2,1)S(1)} %bitcast.37) | non-fusion elementwise | flops 2359296 | bytes 14155776 | tf_op jit(solution)/shard_map/convert_element_type | solution.py:1891
  328.4 1.1 copy.52
  329.6 1.3 copy-done.1
  330.9 1.7 copy.53
  (15 shorter events, 0.3 us)
Async XLA Ops:
  315.9 3.0 copy-start
  317.6 6.3 %slice-start = ((s8[4718592]{0:T(1024)(128)(4,1)}), s8[4194304]{0:T(1024)(128)(4,1)S(1)}, s32[]{:S(2)}) async-start(s8[4718592]{0:T(1024)(128)(4,1)} %bitcast.36), calls=%async_computation | async-start | bytes 8388608
  318.9 5.1 %slice-start.1 = ((s8[4718592]{0:T(1024)(128)(4,1)}), s8[524288]{0:T(1024)(128)(4,1)S(1)}, s32[]{:S(2)}) async-start(s8[4718592]{0:T(1024)(128)(4,1)} %bitcast.36), calls=%async_computation.1 | async-start | bytes 1048576
  324.0 4.5 %copy-start.2 = (bf16[1024,768]{1,0:T(8,128)(2,1)S(1)}, bf16[1024,768]{1,0:T(8,128)(2,1)}, u32[]{:S(2)}) copy-start(bf16[1024,768]{1,0:T(8,128)(2,1)} %get-tuple-element.32) | copy-start | bytes 4718596
  328.4 2.5 copy-start.1

commit v5 on v4

--- a/solution.py
+++ b/solution.py
@@ -580,6 +580,7 @@
     group = 4
     bits = (blocks - 1).bit_length()
     home = me // blocks
+    tick("start")
     for turn in range(regions):
         region = (home + 1 + turn) % regions
         produce(region)
@@ -591,6 +592,7 @@
     tick("sent")
 
     def zonal_step(index, carry):
+        tick("arrival", index)
         chip = (index + home * senders // regions) % senders
         for col in range(cols):
             await_piece(got.at[chip * cols + col], recv_a.at[chip * cols + col])
@@ -652,11 +654,10 @@
         y = (dot(high, behind[...]) + dot(rest, behind[...])).astype(low).astype(wide)
         for i in range(4):
             flat[i, rows, :] = y[:, i * lanes : (i + 1) * lanes]
+        tick("mode", step)
         return carry
 
-    lax.fori_loop(0, modes // group // 2, mode_step, 0)
-    tick("halfway")
-    lax.fori_loop(modes // group // 2, modes // group, mode_step, 0)
+    lax.fori_loop(0, modes // group, mode_step, 0)
     tick("modes")
 
     def return_step(c, carry):
@@ -920,7 +921,7 @@
 
     tables = (to_modes, to_columns, ahead, behind)
     filter_pass(
-        sizes, me, core, produce, middle, consume, tables, work, sems, lambda place: None
+        sizes, me, core, produce, middle, consume, tables, work, sems, lambda place, step=0: None
     )
     for step in (steps - 2, steps - 1):
         for copy in keep(step):
@@ -955,7 +956,7 @@
 
 
 def add_rows(out_ref, out_row, terms, rows):
-    step = 48
+    step = [size for size in (96, 64, 48, 32) if rows % size == 0][0]
 
     def add(part, carry):
         total = 0.0
@@ -1074,21 +1075,27 @@
         first_hbm,
         act_hbm,
         pre_hbm,
-        own_hbm,
-        ready_ref,
+        project_hbm,
+        expand_hbm,
+        project_piece,
+        expand_piece,
+        project_ready,
+        expand_ready,
         sums_ref,
         slope_hbm,
         project_total,
         expand_total,
         gathered,
+        gathered_bias,
         vector_sum,
-    ) = refs[:23]
-    work, sems = refs[23:33], refs[33:41]
+    ) = refs[:28]
+    work, sems = refs[28:38], refs[38:46]
     (
         tokens_ref,
         slope,
         slope_sems,
-        own,
+        project_own,
+        expand_own,
         load_sems,
         kernel_slope,
         bias_slope,
@@ -1099,18 +1106,25 @@
         act_slots,
         pre_slots,
         slot_sems,
-        halves,
-        quarters,
-        eighths,
-        pieces,
+        project_halves,
+        expand_halves,
+        project_quarters,
+        expand_quarters,
+        project_eighths,
+        expand_eighths,
+        project_pieces,
+        expand_pieces,
         reduce_sends,
         reduce_recvs,
         share_sends,
         share_recvs,
         own_sems,
         slab,
-        slab_sibling,
+        slab_bias,
+        slab_got,
+        slab_bias_got,
         slab_region,
+        slab_bias_region,
         slab_sends,
         slab_recvs,
         vector_sent,
@@ -1122,7 +1136,7 @@
         late_all,
         late_sends,
         late_recvs,
-    ) = refs[41:]
+    ) = refs[46:]
     regions, blocks, block_size, chips, cols, tokens = sizes
     steps = spectrum_hbm.shape[0]
     slots = (spectrum_slots, first_slots, act_slots, pre_slots)
@@ -1134,9 +1148,14 @@
             for k, (hbm, ref) in enumerate(zip(streams, slots))
         ]
 
-    load_own = pltpu.make_async_copy(own_hbm.at[1], own, load_sems.at[0])
-    load_tokens = pltpu.make_async_copy(tokens_hbm, tokens_ref, load_sems.at[1])
-    load_own.start()
+    own = (project_own, expand_own)
+    load_own = [
+        pltpu.make_async_copy(hbm, own[k], load_sems.at[1 + k])
+        for k, hbm in enumerate((project_hbm, expand_hbm))
+    ]
+    load_tokens = pltpu.make_async_copy(tokens_hbm, tokens_ref, load_sems.at[0])
+    for copy in load_own:
+        copy.start()
     for copy in fetch(0, 0):
         copy.start()
     load_tokens.start()
@@ -1146,44 +1165,68 @@
     sent, coming = work[0], work[-1]
     piece = 128
     cols_here = 128 // cols
-    width = own.shape[1]
     late[...] = jnp.zeros_like(late)
     vector_sum[...] = sums_ref[...]
     for ref in (kernel_slope, bias_slope, mixer_slope, offset_slope):
         ref[...] = jnp.zeros_like(ref)
     reducing, sharing = [], []
-    for j in range(2):
-        place = pl.multiple_of((core * 2 + j) * width, width)
-        totals = (project_total.at[pl.ds(place, width)], expand_total.at[:, pl.ds(place, width)])
+    pairs = 3
+    tile = project_own.shape[0]
+    own_pieces = (
+        (project_piece, expand_piece),
+        (project_pieces.at[0], expand_pieces.at[0]),
+        (project_pieces.at[1], expand_pieces.at[1]),
+    )
+    chains = (
+        ((project_piece,), (expand_piece,)),
+        (
+            (project_ready, project_eighths.at[0], own_pieces[1][0]),
+            (expand_ready, expand_eighths.at[0], own_pieces[1][1]),
+        ),
+        (
+            (
+                project_own,
+                project_halves,
+                project_quarters,
+                project_eighths.at[1],
+                own_pieces[2][0],
+            ),
+            (expand_own, expand_halves, expand_quarters, expand_eighths.at[1], own_pieces[2][1]),
+        ),
+    )
+    for j in range(pairs):
+        place = pl.multiple_of((core * pairs + j) * tile, tile)
+        totals = (project_total.at[pl.ds(place, tile)], expand_total.at[:, pl.ds(place, tile)])
         for k in range(2):
-            s = j * 2 + k
             axes = (("x", "y"), ("y", "x"))[k] + ("near", "far")
-            buffers = (own.at[k], halves.at[k], quarters.at[k], eighths.at[s], pieces.at[s])
-            if j == 0:
-                buffers = (ready_ref.at[k],) + buffers[3:]
+            buffers = chains[j][k]
             reducing.append(
                 reduce_steps(
-                    spot, axes[5 - len(buffers) :], buffers, reduce_sends.at[s], reduce_recvs.at[s]
+                    spot,
+                    axes[5 - len(buffers) :],
+                    buffers,
+                    reduce_sends.at[j, k],
+                    reduce_recvs.at[j, k],
                 )
             )
             sharing.append(
                 share_steps(
                     spot,
                     axes,
-                    pieces.at[s],
+                    own_pieces[j][k],
                     totals[k],
-                    share_sends.at[s],
-                    share_recvs.at[s],
-                    own_sems.at[s],
+                    share_sends.at[j, k],
+                    share_recvs.at[j, k],
+                    own_sems.at[j, k],
                 )
             )
 
     def reduce(j, step, finish):
-        for steps_of in reducing[j * 2 : j * 2 + 2]:
+        for steps_of in reducing[2 * j : 2 * j + 2]:
             steps_of[step][finish]()
 
     def share(j, step):
-        for steps_of in sharing[j * 2 : j * 2 + 2]:
+        for steps_of in sharing[2 * j : 2 * j + 2]:
             steps_of[step]()
 
     def inside(region, first, rows):
@@ -1212,10 +1255,11 @@
 
         level = jnp.tanh(pre_slots[slot] / shrink_width)
         second = (shrunk_back * (level * level)).astype(low)
-        offset_slope[...] += jnp.sum(second.astype(wide), 1, keepdims=True)
+        ones = jnp.ones((8, second.shape[1]), low)
+        offset_slope[...] += dot_last(ones, second)
         mixer_slope[...] += dot_last(act_slots[slot], second)
         first = (dot(weights_ref[1], second) * gelu_slope(first_slots[slot])).astype(low)
-        bias_slope[...] += jnp.sum(first.astype(wide), 1, keepdims=True)
+        bias_slope[...] += dot_last(ones, first)
         kernel_slope[...] += dot_last(spectrum_slots[slot], first)
         return dot(weights_ref[0], first)
 
@@ -1246,33 +1290,29 @@
         lax.fori_loop(0, tokens // 256, step, 0)
         leave(region).start()
 
-    side = 2 * block_size
-    slab_core = remote(
-        slab, slab_sibling, slab_sends.at[0], slab_recvs.at[0], across(spot, "core")
-    )
-    my_rows = pl.ds(pl.multiple_of(core * side, 32), side)
-    slab_far = remote(
-        slab_sibling.at[my_rows],
-        slab_region,
-        slab_sends.at[1],
-        slab_recvs.at[1],
+    def slab_hops(place, mine, theirs, device):
+        return [
+            remote(src, dst, slab_sends.at[k, place], slab_recvs.at[k, place], device)
+            for k, (src, dst) in enumerate(zip(mine, theirs))
+        ]
+
+    slab_core = slab_hops(
+        0, (slab, slab_bias), (slab_got, slab_bias_got), across(spot, "core")
+    )
+    slab_far = slab_hops(
+        1,
+        (slab_got.at[core], slab_bias_got.at[core]),
+        (slab_region, slab_bias_region),
         chip_device((me + blocks) % chips, core, cols),
     )
+    here = (gathered.at[core, :, block], gathered_bias.at[core, block])
 
     def slab_peer(step):
         other = me // blocks * blocks + (block + step) % blocks
-        ref = gathered.at[block, my_rows]
-        return remote(
-            ref, ref, slab_sends.at[1 + step], slab_recvs.at[1 + step], chip_device(other, core, cols)
-        )
-
-    slab_last = remote(
-        gathered.at[:, my_rows],
-        gathered.at[:, my_rows],
-        slab_sends.at[1 + blocks],
-        slab_recvs.at[1 + blocks],
-        across(spot, "core"),
-    )
+        return slab_hops(1 + step, here, here, chip_device(other, core, cols))
+
+    everything = (gathered.at[core], gathered_bias.at[core])
+    slab_last = slab_hops(1 + blocks, everything, everything, across(spot, "core"))
 
     def slab_start():
         for k, (weight, bias) in enumerate(
@@ -1280,33 +1320,35 @@
         ):
             whole = weight[...]
             upper, lower = whole[:block_size], whole[block_size:]
-            first = k * side
-            slab[first : first + block_size, :block_size] = (
-                upper[:, :block_size] + lower[:, block_size:]
-            )
-            slab[first + block_size : first + side, :block_size] = (
-                upper[:, block_size:] - lower[:, :block_size]
-            )
-            slab[first : first + side, block_size:] = jnp.broadcast_to(
-                bias[...], (side, slab.shape[1] - block_size)
-            )
-        slab_core.start()
+            slab[k, 0] = upper[:, :block_size] + lower[:, block_size:]
+            slab[k, 1] = upper[:, block_size:] - lower[:, :block_size]
+            slab_bias[k] = bias[...]
+        for hop in slab_core:
+            hop.start()
 
     def slab_regions():
-        slab_core.wait()
-        slab_sibling[...] = slab_sibling[...] + slab[...]
-        slab_far.start()
+        for hop in slab_core:
+            hop.wait()
+        slab_got[...] = slab_got[...] + slab[...]
+        slab_bias_got[...] = slab_bias_got[...] + slab_bias[...]
+        for hop in slab_far:
+            hop.start()
 
     def slab_blocks():
-        slab_far.wait()
-        gathered[block, my_rows] = slab_region[...] + slab_sibling[my_rows, :]
+        for hop in slab_far:
+            hop.wait()
+        gathered[core, :, block] = slab_region[...] + slab_got[core]
+        gathered_bias[core, block] = slab_bias_region[...] + slab_bias_got[core]
         for step in range(1, blocks):
-            slab_peer(step).start()
+            for hop in slab_peer(step):
+                hop.start()
 
     def slab_cores():
         for step in range(1, blocks):
-            slab_peer(step).wait()
-        slab_last.start()
+            for hop in slab_peer(step):
+                hop.wait()
+        for hop in slab_last:
+            hop.start()
 
     partners = (
         across(spot, "core"),
@@ -1332,51 +1374,71 @@
 
     regions_seen = []
 
-    def tick(place):
-        if place == "sent":
-            load_own.wait()
+    def tick(place, step=0):
+        if place == "arrival":
+
+            @pl.when(step == 4)
+            def _():
+                reduce(2, 0, 1)
+                reduce(2, 1, 0)
+
+        if place == "mode":
+
+            @pl.when(step == 3)
+            def _():
+                share(0, 3)
+                reduce(2, 2, 1)
+                reduce(2, 3, 0)
+                share(1, 1)
+
+            @pl.when(step == 5)
+            def _():
+                reduce(2, 3, 1)
+
+        if place == "start":
+            for copy in load_own:
+                copy.wait()
+            reduce(2, 0, 0)
             reduce(1, 0, 0)
             vector_step(0)
+        if place == "sent":
+            reduce(1, 0, 1)
+            share(0, 0)
+            vector_step(1)
         if place == "zonal":
-            reduce(1, 0, 1)
+            share(0, 1)
             reduce(1, 1, 0)
-            reduce(0, 0, 0)
-            vector_step(1)
+            reduce(2, 1, 1)
+            reduce(2, 2, 0)
+            vector_step(2)
         if place == "turned":
-            reduce(0, 0, 1)
-            reduce(0, 1, 0)
+            share(0, 2)
             reduce(1, 1, 1)
-            reduce(1, 2, 0)
-            vector_step(2)
-        if place == "halfway":
-            reduce(0, 1, 1)
-            share(0, 0)
-            reduce(1, 2, 1)
-            reduce(1, 3, 0)
+            share(1, 0)
             vector_step(3)
         if place == "modes":
             slab_start()
-            share(0, 1)
-            reduce(1, 3, 1)
-            share(1, 0)
+            share(1, 2)
+            share(2, 0)
             vector_step(4)
         if place == "returned":
-            share(0, 2)
-            share(1, 1)
+            share(0, 4)
+            share(1, 3)
+            share(2, 1)
             vector_step(5)
         if place == "back":
             slab_regions()
         if place == "columns":
             load_tokens.wait()
             slab_blocks()
-            share(0, 3)
-            share(1, 2)
-            share(1, 3)
+            share(2, 2)
+            share(1, 4)
+            share(2, 3)
             slab_cores()
         if place == "region":
             regions_seen.append(place)
             if len(regions_seen) == 1:
-                share(0, 4)
+                share(2, 4)
 
     tables = (to_columns, to_modes, ahead, behind)
     filter_pass(sizes, me, core, produce, middle, consume, tables, work, sems, tick)
@@ -1392,10 +1454,11 @@
 
     for step in range(1, chips):
         late_hop(step).start()
-    slab_last.wait()
-    share(1, 4)
+    for hop in slab_last:
+        hop.wait()
     share(0, 5)
     share(1, 5)
+    share(2, 5)
     for step in range(1, chips):
         late_hop(step).wait()
     total = late_all[0]
@@ -1439,7 +1502,7 @@
     )
 
 
-def backward_scratch(sizes, kept):
+def backward_scratch(sizes, kept, tile, pairs):
     regions, blocks, block_size, chips, cols, tokens = sizes
     features = blocks * block_size
     side = 2 * block_size
@@ -1448,28 +1511,36 @@
         pltpu.VMEM((regions * tokens, features), low),
         pltpu.VMEM((regions * tokens, features), wide),
         dma((regions,)),
-        pltpu.VMEM((2, features, features), low),
-        dma((2,)),
+        pltpu.VMEM((tile, features), low),
+        pltpu.VMEM((features, tile), low),
+        dma((3,)),
         pltpu.VMEM((side, side), wide),
-        pltpu.VMEM((side, 1), wide),
+        pltpu.VMEM((8, side), wide),
         pltpu.VMEM((side, side), wide),
-        pltpu.VMEM((side, 1), wide),
+        pltpu.VMEM((8, side), wide),
         *(pltpu.VMEM((2, *shape[1:]), kind) for shape, kind in kept),
         dma((len(kept), 2)),
-        pltpu.VMEM((2, features // 2, features), low),
-        pltpu.VMEM((2, features // 4, features), low),
-        pltpu.VMEM((4, features // 8, features), low),
-        pltpu.VMEM((4, features // 16, features), low),
-        dma((4, 4)),
-        dma((4, 4)),
-        dma((4, 7)),
-        dma((4, 7)),
-        dma((4,)),
-        pltpu.VMEM((2 * side, 128), wide),
-        pltpu.VMEM((2 * side, 128), wide),
-        pltpu.VMEM((side, 128), wide),
-        dma((2 + blocks,)),
-        dma((2 + blocks,)),
+        pltpu.VMEM((tile // 2, features), low),
+        pltpu.VMEM((features // 2, tile), low),
+        pltpu.VMEM((tile // 4, features), low),
+        pltpu.VMEM((features // 4, tile), low),
+        pltpu.VMEM((2, tile // 8, features), low),
+        pltpu.VMEM((2, features // 8, tile), low),
+        pltpu.VMEM((2, tile // 16, features), low),
+        pltpu.VMEM((2, features // 16, tile), low),
+        dma((pairs, 2, 4)),
+        dma((pairs, 2, 4)),
+        dma((pairs, 2, 7)),
+        dma((pairs, 2, 7)),
+        dma((pairs, 2)),
+        pltpu.VMEM((2, 2, block_size, block_size), wide),
+        pltpu.VMEM((2, 8, side), wide),
+        pltpu.VMEM((2, 2, block_size, block_size), wide),
+        pltpu.VMEM((2, 8, side), wide),
+        pltpu.VMEM((2, block_size, block_size), wide),
+        pltpu.VMEM((8, side), wide),
+        dma((2, 2 + blocks)),
+        dma((2, 2 + blocks)),
         pltpu.VMEM((5, 16, features), wide),
         pltpu.VMEM((5, 16, features), wide),
         dma((5,)),
@@ -1494,8 +1565,12 @@
         project_hbm,
         out_hbm,
         mixed_back_hbm,
-        own_hbm,
-        ready_ref,
+        project_hbm_own,
+        expand_hbm_own,
+        project_piece,
+        expand_piece,
+        project_ready,
+        expand_ready,
         vectors,
         mixed_ref,
         expand_ref,
@@ -1505,10 +1580,18 @@
         back_sum,
         hidden_tile,
         back_tile,
-        sent,
-        got,
-        own,
-        halves,
+        project_sent,
+        expand_sent,
+        project_got,
+        expand_got,
+        project_own,
+        expand_own,
+        project_halves,
+        expand_halves,
+        project_quarters,
+        expand_quarters,
+        project_eighths,
+        expand_eighths,
         load_sems,
         weight_sems,
         leave_sems,
@@ -1519,15 +1602,21 @@
         first_recvs,
     ) = refs
     tile = expand_ref.shape[2]
+    pairs = project_own.shape[0]
     spot = place_of(lax.axis_index("rows"), lax.axis_index("cols"))
     core = spot["core"]
     orders = (("x", "y"), ("y", "x"))
-    places = [
-        (1 - core) * 2,
-        core * 2,
-        (1 - core) * 2 + 1,
-        core * 2 + 1,
-    ]
+    sent = (project_sent, expand_sent)
+    got = (project_got, expand_got)
+    own = (project_own, expand_own)
+    halves = (project_halves, expand_halves)
+    quarters = (project_quarters, expand_quarters)
+    eighths = (project_eighths, expand_eighths)
+    piece0 = (project_piece, expand_piece)
+    ready = (project_ready, expand_ready)
+    places = []
+    for j in range(pairs):
+        places += [(1 - core) * pairs + j, core * pairs + j]
 
     def weights(k):
         here = pl.ds(pl.multiple_of(places[k] * tile, tile), tile)
@@ -1536,14 +1625,15 @@
             pltpu.make_async_copy(expand_hbm.at[:, here], expand_ref.at[k], weight_sems.at[1, k]),
         ]
 
-    for k in range(4):
+    for k in range(2 * pairs):
         for copy in weights(k):
             copy.start()
     load_mixed = pltpu.make_async_copy(mixed_hbm, mixed_ref, load_sems.at[0])
     load_mixed.start()
     barrier = pltpu.get_barrier_semaphore()
-    for axis in ("core", "x", "y"):
-        pl.semaphore_signal(barrier, inc=1, device_id=across(spot, axis), device_id_type=MESH)
+    for axis in ("core", "x", "y", "near", "far"):
+        device = facing(spot, axis)[1]
+        pl.semaphore_signal(barrier, inc=1, device_id=device, device_id_type=MESH)
     count = second_ref.shape[0]
     piece = 512
     vectors[...] = jnp.zeros_like(vectors)
@@ -1554,11 +1644,13 @@
         back_sum[rows, :] = jnp.zeros((piece, back_sum.shape[1]), wide)
         return carry + jnp.sum(up_ref[rows, :].astype(wide), 0, keepdims=True)
 
-    vectors[4:5, :] = lax.fori_loop(0, count // piece, start_step, jnp.zeros((1, tile), wide))
-    pl.semaphore_wait(barrier, 3)
+    vectors[4:5, :] = lax.fori_loop(
+        0, count // piece, start_step, jnp.zeros((1, up_ref.shape[1]), wide)
+    )
+    pl.semaphore_wait(barrier, 5)
 
     def tile_step(k, place, between):
-        lift_row = lift_ref[pl.ds(place, 1), :]
+        lift_row = lift_ref[pl.ds(pl.multiple_of(place * tile, tile), tile)].reshape(1, tile)
 
         def piece_step(part, carry):
             rows = pl.ds(pl.multiple_of(part * piece, piece), piece)
@@ -1575,7 +1667,7 @@
             return carry + jnp.sum(pre_back.astype(wide), 0, keepdims=True)
 
         lift = lax.fori_loop(0, count // piece, piece_step, jnp.zeros((1, tile), wide))
-        vectors[pl.ds(5 + place, 1), :] = lift
+        vectors[pl.ds(5 + place, 1), 0:tile] = lift
         between()
         return (
             dot_first(hidden_tile[...], up_ref[...]),
@@ -1584,46 +1676,77 @@
 
     def swap(j, k):
         return remote(
-            sent.at[j, k], got.at[j, k], sent_sem.at[j, k], got_sem.at[j, k], across(spot, "core")
+            sent[k].at[j], got[k].at[j], sent_sem.at[j, k], got_sem.at[j, k], across(spot, "core")
         )
 
-    hops = [
-        reduce_steps(
-            spot,
-            orders[k],
-            (own.at[0, k], halves.at[k], ready_ref.at[k]),
-            first_sends.at[k],
-            first_recvs.at[k],
-        )
-        for k in range(2)
-    ]
+    chains = []
+    for pair in range(2):
+        for k in range(2):
+            buffers = (own[k].at[pair], halves[k].at[pair])
+            if pair == 0:
+                buffers += (quarters[k], eighths[k], piece0[k])
+            else:
+                buffers += (ready[k],)
+            chains.append(
+                reduce_steps(
+                    spot,
+                    (orders[k] + ("near", "far"))[: len(buffers) - 1],
+                    buffers,
+                    first_sends.at[pair, k],
+                    first_recvs.at[pair, k],
+                )
+            )
+
+    def begin(pair, step):
+        for chain in chains[pair * 2 : pair * 2 + 2]:
+            chain[step][0]()
+
+    def finish(pair, step):
+        for chain in chains[pair * 2 : pair * 2 + 2]:
+            chain[step][1]()
 
     def pair_step(j, carry):
         for copy in weights_at(2 * j):
             copy.wait()
-        away = tile_step(2 * j, (1 - core) * 2 + j, lambda: None)
+
+        def away_between():
+            @pl.when(j == 2)
+            def _():
+                finish(0, 1)
+                begin(0, 2)
+
+        away = tile_step(2 * j, (1 - core) * pairs + j, away_between)
         for k in range(2):
-            sent[j, k] = away[k].astype(low)
+            sent[k][j] = away[k].astype(low)
             swap(j, k).start()
-
-        def forward():
+        for copy in weights_at(2 * j + 1):
+            copy.wait()
+
+        def home_between():
             @pl.when(j == 1)
             def _():
-                for hop in hops:
-                    hop[0][1]()
-                    hop[1][0]()
-
-        for copy in weights_at(2 * j + 1):
-            copy.wait()
-        home = tile_step(2 * j + 1, core * 2 + j, forward)
+                finish(0, 0)
+                begin(0, 1)
+
+            @pl.when(j == 2)
+            def _():
+                finish(0, 2)
+                begin(0, 3)
+                finish(1, 0)
+                begin(1, 1)
+
+        home = tile_step(2 * j + 1, core * pairs + j, home_between)
         for k in range(2):
             swap(j, k).wait()
-            own[j, k] = (home[k] + got[j, k].astype(wide)).astype(low)
+            own[k][j] = (home[k] + got[k][j].astype(wide)).astype(low)
 
         @pl.when(j == 0)
         def _():
-            for hop in hops:
-                hop[0][0]()
+            begin(0, 0)
+
+        @pl.when(j == 1)
+        def _():
+            begin(1, 0)
 
         return carry
 
@@ -1633,9 +1756,13 @@
             pltpu.make_async_copy(expand_ref.at[k], expand_ref.at[k], weight_sems.at[1, k]),
         ]
 
-    lax.fori_loop(0, 2, pair_step, 0)
-    keep = pltpu.make_async_copy(own.at[1], own_hbm.at[1], own_sems.at[0])
-    keep.start()
+    lax.fori_loop(0, pairs, pair_step, 0)
+    keeps = [
+        pltpu.make_async_copy(own[k].at[pairs - 1], hbm, own_sems.at[k])
+        for k, hbm in enumerate((project_hbm_own, expand_hbm_own))
+    ]
+    for keep in keeps:
+        keep.start()
     load_mixed.wait()
 
     def leave(part):
@@ -1667,9 +1794,10 @@
         return carry
 
     lax.fori_loop(0, count // piece, end_step, 0)
-    for hop in hops:
-        hop[1][1]()
-    keep.wait()
+    finish(0, 3)
+    finish(1, 1)
+    for keep in keeps:
+        keep.wait()
     for part in range(count // piece):
         for copy in leave(part):
             copy.wait()
@@ -1677,12 +1805,18 @@
 
 def call_dense(second_norm, upstream, scale, returned, lift, mixed, expand, project, cid):
     count, features = second_norm.shape
-    square = (features, features)
+    tile = 512
+    pairs = expand.shape[1] // tile // 2
+    tall, broad = (tile, features), (features, tile)
     outs = (
         ((count, features), low),
         ((count, features), wide),
-        ((2, 2, *square), low),
-        ((2, features // 4, features), low),
+        (tall, low),
+        (broad, low),
+        ((tile // 16, features), low),
+        ((features // 16, tile), low),
+        ((tile // 4, features), low),
+        ((features // 4, tile), low),
         ((16, features), wide),
     )
     shapes = [jax.ShapeDtypeStruct(shape, kind) for shape, kind in outs]
@@ -1692,28 +1826,31 @@
         dense_kernel,
         out_shape=shapes,
         in_specs=[vmem] * 5 + [anywhere] * 3,
-        out_specs=[anywhere] * 3 + [vmem] * 2,
+        out_specs=[anywhere] * 4 + [vmem] * 5,
         scratch_shapes=[
             pltpu.VMEM((count, features), wide),
-            pltpu.VMEM((4, *square), low),
-            pltpu.VMEM((4, *square), low),
+            pltpu.VMEM((2 * pairs, *broad), low),
+            pltpu.VMEM((2 * pairs, *tall), low),
             pltpu.VMEM((count, features), low),
             pltpu.VMEM((count, features), wide),
             pltpu.VMEM((count, features), wide),
-            pltpu.VMEM((count, features), low),
-            pltpu.VMEM((count, features), low),
-            pltpu.VMEM((2, 2, *square), low),
-            pltpu.VMEM((2, 2, *square), low),
-            pltpu.VMEM((2, 2, *square), low),
-            pltpu.VMEM((2, features // 2, features), low),
+            pltpu.VMEM((count, tile), low),
+            pltpu.VMEM((count, tile), low),
+            *(pltpu.VMEM((pairs, *shape), low) for shape in (tall, broad) * 3),
+            pltpu.VMEM((pairs - 1, tile // 2, features), low),
+            pltpu.VMEM((pairs - 1, features // 2, tile), low),
+            pltpu.VMEM((tile // 4, features), low),
+            pltpu.VMEM((features // 4, tile), low),
+            pltpu.VMEM((tile // 8, features), low),
+            pltpu.VMEM((features // 8, tile), low),
             dma((1,)),
-            dma((2, 4)),
+            dma((2, 2 * pairs)),
             dma((2, count // 512)),
-            dma((1,)),
-            dma((2, 2)),
-            dma((2, 2)),
-            dma((2, 2)),
-            dma((2, 2)),
+            dma((2,)),
+            dma((pairs, 2)),
+            dma((pairs, 2)),
+            dma((pairs - 1, 2, 4)),
+            dma((pairs - 1, 2, 4)),
         ],
         compiler_params=pltpu.CompilerParams(
             collective_id=cid, has_side_effects=True, vmem_limit_bytes=60 * 1024 * 1024
@@ -1830,25 +1967,26 @@
         range(6),
         forward_scratch(sizes, kept),
     )
-    output, mixed_back, own_tiles, ready, part_sums = call_dense(
+    output, mixed_back, *tiles, part_sums = call_dense(
         second_norm,
         upstream,
         exit_scale,
         dense_return,
-        dense_lift.reshape(-1, features),
+        dense_lift,
         mixed,
         dense_expand,
         dense_project,
         3,
     )
-    slope, project_sum, expand_sum, gathered, sums = call_filter(
+    slope, project_sum, expand_sum, gathered, gathered_bias, sums = call_filter(
         backward_kernel,
         sizes,
         (
             ((count, features), wide),
             (dense_project.shape, low),
             (dense_expand.shape, low),
-            ((blocks, 2 * side, 128), wide),
+            ((2, 2, blocks, block_size, block_size), wide),
+            ((2, blocks, 8, side), wide),
             ((16, features), wide),
         ),
         2,
@@ -1863,31 +2001,28 @@
             behind,
             eye,
             *stream,
-            own_tiles,
-            ready,
+            *tiles,
             part_sums,
         ),
         scalars,
-        (0, 9, 10, 11, 12, 13),
+        (0, 9, 10, 11, 12, 13, 14),
         range(3),
-        backward_scratch(sizes, kept),
-    )
-    weights = gathered[:, :, :block_size].reshape(blocks, 2, 2, block_size, block_size)
-    weights = weights.transpose(1, 2, 0, 3, 4)
-    biases = gathered[:, :, block_size].reshape(blocks, 2, 2, block_size).transpose(1, 2, 0, 3)
+        backward_scratch(sizes, kept, tiles[0].shape[0], 3),
+    )
+    biases = gathered_bias[:, :, 0].reshape(2, blocks, 2, block_size).swapaxes(1, 2)
     return (
         output.reshape(tokens.shape),
         slope.reshape(tokens.shape),
         sums[0],
         sums[1],
-        weights[0],
+        gathered[0],
         biases[0],
-        weights[1],
+        gathered[1],
         biases[1],
         sums[2],
         sums[3],
         expand_sum.astype(wide),
-        sums[5:9].reshape(-1),
+        sums[5 : 5 + dense_lift.shape[0] // tiles[0].shape[0], : tiles[0].shape[0]].reshape(-1),
         project_sum.astype(wide),
         sums[4],
     )

time: 333 us -> 317 us (0.952)
  Pallas kernels: 303 us -> 288 us
  local copies, waits for them, and re-layouts: 17.5 us -> 14 us
    pallas_call x2, Pallas kernels: 258 us -> 235 us  [call_filter(): pl.pallas_call(functools.partial(body, sizes), out_shape=shapes, in_specs...]
    pallas_call x1, Pallas kernels: 45.1 us -> 53.6 us  [call_dense(): pl.pallas_call(dense_kernel, out_shape=shapes, in_specs=[vmem] * 5 + [any...]
where the time goes in v5:
time: 317 us
  Pallas kernels  288 us (91%)
  local copies, waits for them, and re-layouts  14 us (4%)
  other arithmetic  13.6 us (4%)
    pallas_call x2, Pallas kernels, call_filter(): pl.pallas_call(functools.partial(body, sizes), out_shape=shapes, in_specs...  235 us
    pallas_call x1, Pallas kernels, call_dense(): pl.pallas_call(dense_kernel, out_shape=shapes, in_specs=[vmem] * 5 + [any...  53.6 us
    convert_element_type x1, other arithmetic, shards(): expand_sum.astype(wide)  7.43 us

profile of v5, /device:TPU:0, one launch (start us, length us, event | category | flops | bytes accessed | tf_op | source)
XLA Modules:
  0.0 316.6 jit_solution(10893747845723887540)
XLA Ops:
  0.7 0.7 fusion
  1.4 0.1 stack_reshape.6
  1.5 0.1 stack_reshape.7
  1.6 0.8 dynamic-slice_bitcast_fusion.1
  2.4 0.8 copy.41.refs_8_
  3.1 0.8 fusion.2
  3.9 0.1 maximum_bitcast_fusion
  4.0 0.1 maximum_bitcast_fusion.1
  4.1 0.7 pad_maximum_fusion.refs_7_.refs_5_
  4.8 99.0 %shard_map.326 = (f32[1024,768]{1,0:T(8,128)}, bf16[1024,768]{1,0:T(8,128)(2,1)}, bf16[8,192,512]{2,1,0:T(8,128)(2,1)}, f32[8,192,512]{2,1,0:T(8,128)}, bf16[8,1...) custom-call(s32[2,2]{1,0:T(2,128)} %refs_0_.3, s32[2]{0:T(128)} %refs_1_.3, bf16[1024,768]{1,0:T(8,128)(2,1)} %bitcast.29, ...), custom_call_target="tpu_custom_call" | custom-call | tf_op jit(solution)/shard_map/pallas_call | solution.py:1478
  103.9 53.6 %shard_map.327 = (bf16[1024,768]{1,0:T(8,128)(2,1)}, f32[1024,768]{1,0:T(8,128)}, bf16[512,768]{1,0:T(8,128)(2,1)}, bf16[768,512]{1,0:T(8,128)(2,1)}, bf16[32,76...) custom-call(bf16[1024,768]{1,0:T(8,128)(2,1)} %get-tuple-element.35., ...), custom_call_target="tpu_custom_call" | custom-call | tf_op jit(solution)/shard_map/pallas_call | solution.py:1825
  157.5 135.7 %shard_map.328 = (f32[1024,768]{1,0:T(8,128)}, bf16[3072,768]{1,0:T(8,128)(2,1)}, bf16[768,3072]{1,0:T(8,128)(2,1)}, f32[2,2,8,96,96]{4,3,2,1,0:T(8,128)}, f32[2,8,8,192]{3,2,1,0:T(8,128)}, /*index=5*/f32[16,768]{1,0:T(8,128)}) custom-call(s32[2,2]{1,0:T(2,128)} %refs_0_.3, s32[2]{0:T(128)} %refs_1_.3, bf16[1024,768]{1,0:T(8,128)(2,1)} %bitcast.30, ...), custom_call_target="tpu_custom_call" | custom-call | tf_op jit(solution)/shard_map/pallas_call | solution.py:1478
  293.2 0.9 slice_reduce_fusion
  294.1 0.1 reshape_squeeze.3
  294.2 0.6 slice_bitcast_fusion.2
  294.8 0.8 slice.62
  295.6 1.6 slice_reduce_fusion.1
  297.2 0.6 reshape.57
  297.8 2.8 slice_bitcast_fusion
  300.6 7.4 %convert_element_type.6 = f32[768,3072]{1,0:T(8,128)} convert(bf16[768,3072]{1,0:T(8,128)(2,1)} %get-tuple-element.54) | non-fusion elementwise | flops 2359296 | bytes 14155776 | tf_op jit(solution)/shard_map/convert_element_type | solution.py:2024
  308.0 4.5 %convert_element_type.7 = f32[3072,768]{1,0:T(8,128)} convert(bf16[3072,768]{1,0:T(8,128)(2,1)S(1)} %bitcast.32) | non-fusion elementwise | flops 2359296 | bytes 14155776 | tf_op jit(solution)/shard_map/convert_element_type | solution.py:2026
  312.5 1.1 copy.47
  313.7 1.3 copy-done
  315.0 1.7 copy.48
  (10 shorter events, 0.0 us)
Async XLA Ops:
  297.8 10.2 %slice-start = ((s8[4718592]{0:T(1024)(128)(4,1)}), s8[4194304]{0:T(1024)(128)(4,1)S(1)}, s32[]{:S(2)}) async-start(s8[4718592]{0:T(1024)(128)(4,1)} %bitcast.31), calls=%async_computation | async-start | bytes 8388608
  300.6 7.4 %slice-start.1 = ((s8[4718592]{0:T(1024)(128)(4,1)}), s8[524288]{0:T(1024)(128)(4,1)S(1)}, s32[]{:S(2)}) async-start(s8[4718592]{0:T(1024)(128)(4,1)} %bitcast.31), calls=%async_computation.1 | async-start | bytes 1048576
  308.0 4.5 %copy-start.1 = (bf16[1024,768]{1,0:T(8,128)(2,1)S(1)}, bf16[1024,768]{1,0:T(8,128)(2,1)}, u32[]{:S(2)}) copy-start(bf16[1024,768]{1,0:T(8,128)(2,1)} %get-tuple-element.37) | copy-start | bytes 4718596
  312.5 2.5 copy-start

commit v6 on v5

--- a/solution.py
+++ b/solution.py
@@ -789,9 +789,8 @@
     return curve
 
 
-def gelu_slope(value):
-    bell = jnp.exp(-0.5 * value * value) * (1.0 / math.sqrt(2.0 * math.pi))
-    return gelu_parts(value) + value * bell
+def gelu_bell(value):
+    return jnp.exp(-0.5 * value * value) * (1.0 / math.sqrt(2.0 * math.pi))
 
 
 def inside_region(sizes_ref, starts_ref, region, first, shape, width):
@@ -836,12 +835,33 @@
         ahead,
         behind,
         eye,
+        up_hbm,
+        project_hbm,
         mixed_hbm,
         second_hbm,
         *kept_hbm,
-    ) = refs[:20]
-    work, sems = refs[20:30], refs[30:38]
-    mixed, second, mixed_sems, second_sems, kept_sems, *kept = refs[38:]
+        hidden_back_hbm,
+    ) = refs[:23]
+    work, sems = refs[23:33], refs[33:41]
+    (
+        mixed,
+        second,
+        mixed_sems,
+        second_sems,
+        kept_sems,
+        up_ref,
+        project_ref,
+        hidden_back,
+        load_sems,
+        back_sems,
+        *kept,
+    ) = refs[41:]
+    loads = [
+        pltpu.make_async_copy(up_hbm, up_ref, load_sems.at[0]),
+        pltpu.make_async_copy(project_hbm, project_ref, load_sems.at[1]),
+    ]
+    for copy in loads:
+        copy.start()
     regions, blocks, block_size, chips, cols, tokens = sizes
     me, core = greet(chips, cols)
     sent, coming = work[0], work[-1]
@@ -886,14 +906,16 @@
         spectrum = spectrum.astype(low)
         spectrum_kept[slot] = spectrum
         first = dot_first(weights_ref[0], spectrum) + biases_ref[:, 0:1]
-        first_kept[slot] = first
-        act = (first * gelu_parts(first)).astype(low)
+        curve = gelu_parts(first)
+        first_kept[slot] = curve + first * gelu_bell(first)
+        act = (first * curve).astype(low)
         act_kept[slot] = act
         second_pre = dot_first(weights_ref[1], act) + biases_ref[:, 1:2]
-        second_kept[slot] = second_pre
+        level = jnp.tanh(second_pre / shrink_width)
+        second_kept[slot] = level * level
         for copy in keep(step):
             copy.start()
-        return second_pre - shrink_width * jnp.tanh(second_pre / shrink_width)
+        return second_pre - shrink_width * level
 
     def leave(region):
         rows = pl.ds(pl.multiple_of(region * tokens, tokens), tokens)
@@ -919,10 +941,30 @@
         for copy in leave(region):
             copy.start()
 
+    tiles, count, tile = hidden_back.shape
+
+    def leave_back(k):
+        return pltpu.make_async_copy(hidden_back.at[k], hidden_back_hbm.at[k], back_sems.at[k])
+
+    def tick(place, step=0):
+        if place == "sent":
+            for copy in loads:
+                copy.wait()
+
+            def tile_step(k, carry):
+                here = pl.ds(pl.multiple_of(k * tile, tile), tile)
+                for first in range(0, count, 256):
+                    rows = slice(first, first + 256)
+                    hidden_back[k, rows, :] = dot_last(up_ref[rows, :], project_ref[here, :]).astype(low)
+                leave_back(k).start()
+                return carry
+
+            lax.fori_loop(0, tiles, tile_step, 0)
+
     tables = (to_modes, to_columns, ahead, behind)
-    filter_pass(
-        sizes, me, core, produce, middle, consume, tables, work, sems, lambda place, step=0: None
-    )
+    filter_pass(sizes, me, core, produce, middle, consume, tables, work, sems, tick)
+    for k in range(tiles):
+        leave_back(k).wait()
     for step in (steps - 2, steps - 1):
         for copy in keep(step):
             copy.wait()
@@ -1253,12 +1295,11 @@
             for copy in fetch(step + 1, 1 - slot):
                 copy.start()
 
-        level = jnp.tanh(pre_slots[slot] / shrink_width)
-        second = (shrunk_back * (level * level)).astype(low)
+        second = (shrunk_back * pre_slots[slot]).astype(low)
         ones = jnp.ones((8, second.shape[1]), low)
         offset_slope[...] += dot_last(ones, second)
         mixer_slope[...] += dot_last(act_slots[slot], second)
-        first = (dot(weights_ref[1], second) * gelu_slope(first_slots[slot])).astype(low)
+        first = (dot(weights_ref[1], second) * first_slots[slot]).astype(low)
         bias_slope[...] += dot_last(ones, first)
         kernel_slope[...] += dot_last(spectrum_slots[slot], first)
         return dot(weights_ref[0], first)
@@ -1488,7 +1529,7 @@
     )(*scalars, *operands)
 
 
-def forward_scratch(sizes, kept):
+def forward_scratch(sizes, kept, hidden, tile):
     regions, blocks, block_size, chips, cols, tokens = sizes
     dma = pltpu.SemaphoreType.DMA
     features = blocks * block_size
@@ -1498,6 +1539,11 @@
         dma((regions,)),
         dma((regions,)),
         dma((len(kept), 2)),
+        pltpu.VMEM((regions * tokens, features), low),
+        pltpu.VMEM((hidden, features), low),
+        pltpu.VMEM((hidden // tile, regions * tokens, tile), low),
+        dma((2,)),
+        dma((hidden // tile,)),
         *(pltpu.VMEM((2, *shape[1:]), kind) for shape, kind in kept),
     )
 
@@ -1553,6 +1599,144 @@
     )
 
 
+def finish_kernel(*refs):
+    (
+        project,
+        expand,
+        slope,
+        output,
+        gathered,
+        gathered_bias,
+        sums,
+        output_out,
+        slope_out,
+        gain,
+        shift,
+        kernel,
+        bias,
+        mixer,
+        offset,
+        scale,
+        center,
+        expand_out,
+        lift,
+        project_out,
+        returned,
+        project_low,
+        expand_low,
+        project_wide,
+        expand_wide,
+        slope_held,
+        output_held,
+        load_sems,
+        store_sems,
+        pass_sems,
+    ) = refs
+    parts = load_sems.shape[1]
+    whole = ((project, project_low, project_wide, project_out), (expand, expand_low, expand_wide, expand_out))
+
+    def rows_of(ref, part):
+        size = ref.shape[0] // parts
+        return ref.at[pl.ds(part * size, size)]
+
+    def load(k, part):
+        source, narrow, broad, target = whole[k]
+        return pltpu.make_async_copy(
+            rows_of(source, part), rows_of(narrow, part), load_sems.at[k, part]
+        )
+
+    def store(k, part):
+        source, narrow, broad, target = whole[k]
+        return pltpu.make_async_copy(
+            rows_of(broad, part), rows_of(target, part), store_sems.at[k, part]
+        )
+
+    for part in range(parts):
+        for k in range(2):
+            load(k, part).start()
+    passes = [
+        [
+            pltpu.make_async_copy(source, held, pass_sems.at[0, k]),
+            pltpu.make_async_copy(held, target, pass_sems.at[1, k]),
+        ]
+        for k, (source, held, target) in enumerate(
+            ((slope, slope_held, slope_out), (output, output_held, output_out))
+        )
+    ]
+    for copy in passes:
+        copy[0].start()
+    kernel[...] = gathered[0]
+    mixer[...] = gathered[1]
+    side = bias.shape[2]
+    for b in range(bias.shape[1]):
+        for i in range(2):
+            bias[i, b : b + 1, :] = gathered_bias[0, b, 0:1, i * side : (i + 1) * side]
+            offset[i, b : b + 1, :] = gathered_bias[1, b, 0:1, i * side : (i + 1) * side]
+    for k, ref in enumerate((gain, shift, scale, center, returned)):
+        ref[...] = sums[k : k + 1, :].reshape(ref.shape)
+    tile = lift.shape[0] // 6
+    for k in range(6):
+        lift[k * tile : (k + 1) * tile] = sums[5 + k : 6 + k, :tile].reshape(tile)
+    for copy in passes:
+        copy[0].wait()
+        copy[1].start()
+    for part in range(parts):
+        for k in range(2):
+            load(k, part).wait()
+            source, narrow, broad, target = whole[k]
+            rows_of(broad, part)[...] = rows_of(narrow, part)[...].astype(wide)
+            store(k, part).start()
+    for part in range(parts):
+        for k in range(2):
+            store(k, part).wait()
+    for copy in passes:
+        copy[1].wait()
+
+
+def call_finish(project, expand, slope, output, gathered, gathered_bias, sums):
+    hidden, features = project.shape
+    line = jax.ShapeDtypeStruct((features,), wide)
+    weight = jax.ShapeDtypeStruct(gathered.shape[1:], wide)
+    bias = jax.ShapeDtypeStruct(gathered.shape[1:4], wide)
+    shapes = [
+        jax.ShapeDtypeStruct(output.shape, low),
+        jax.ShapeDtypeStruct(slope.shape, wide),
+        line,
+        line,
+        weight,
+        bias,
+        weight,
+        bias,
+        line,
+        line,
+        jax.ShapeDtypeStruct(expand.shape, wide),
+        jax.ShapeDtypeStruct((hidden,), wide),
+        jax.ShapeDtypeStruct(project.shape, wide),
+        line,
+    ]
+    anywhere = pl.BlockSpec(memory_space=pl.ANY)
+    dma = pltpu.SemaphoreType.DMA
+    parts = 8
+    return pl.pallas_call(
+        finish_kernel,
+        out_shape=shapes,
+        in_specs=[anywhere] * 4 + [vmem] * 3,
+        out_specs=[anywhere if k in (0, 1, 10, 12) else vmem for k in range(len(shapes))],
+        scratch_shapes=[
+            pltpu.VMEM(project.shape, low),
+            pltpu.VMEM(expand.shape, low),
+            pltpu.VMEM(project.shape, wide),
+            pltpu.VMEM(expand.shape, wide),
+            pltpu.VMEM(slope.shape, wide),
+            pltpu.VMEM(output.shape, low),
+            dma((2, parts)),
+            dma((2, parts)),
+            dma((2, 2)),
+        ],
+        compiler_params=pltpu.CompilerParams(vmem_limit_bytes=60 * 1024 * 1024),
+    )(project, expand, slope, output, gathered, gathered_bias, sums)
+
+
 def dense_kernel(*refs):
     (
         second_ref,
@@ -1563,6 +1747,7 @@
         mixed_hbm,
         expand_hbm,
         project_hbm,
+        hidden_back_hbm,
         out_hbm,
         mixed_back_hbm,
         project_hbm_own,
@@ -1575,6 +1760,7 @@
         mixed_ref,
         expand_ref,
         project_ref,
+        hidden_back,
         out_ref,
         out_sum,
         back_sum,
@@ -1623,6 +1809,9 @@
         return [
             pltpu.make_async_copy(project_hbm.at[here], project_ref.at[k], weight_sems.at[0, k]),
             pltpu.make_async_copy(expand_hbm.at[:, here], expand_ref.at[k], weight_sems.at[1, k]),
+            pltpu.make_async_copy(
+                hidden_back_hbm.at[places[k]], hidden_back.at[k], weight_sems.at[2, k]
+            ),
         ]
 
     for k in range(2 * pairs):
@@ -1635,7 +1824,7 @@
         device = facing(spot, axis)[1]
         pl.semaphore_signal(barrier, inc=1, device_id=device, device_id_type=MESH)
     count = second_ref.shape[0]
-    piece = 512
+    piece = 1024
     vectors[...] = jnp.zeros_like(vectors)
 
     def start_step(part, carry):
@@ -1655,9 +1844,9 @@
         def piece_step(part, carry):
             rows = pl.ds(pl.multiple_of(part * piece, piece), piece)
             pre = dot(second_ref[rows, :], expand_ref[k]) + lift_row
-            back = dot_last(up_ref[rows, :], project_ref[k])
+            back = hidden_back[k, rows, :].astype(wide)
             curve = gelu_parts(pre)
-            bell = jnp.exp(-0.5 * pre * pre) * (1.0 / math.sqrt(2.0 * math.pi))
+            bell = gelu_bell(pre)
             hidden = (pre * curve).astype(low)
             hidden_tile[rows, :] = hidden
             pre_back = (back * (curve + pre * bell)).astype(low)
@@ -1754,6 +1943,7 @@
         return [
             pltpu.make_async_copy(project_ref.at[k], project_ref.at[k], weight_sems.at[0, k]),
             pltpu.make_async_copy(expand_ref.at[k], expand_ref.at[k], weight_sems.at[1, k]),
+            pltpu.make_async_copy(hidden_back.at[k], hidden_back.at[k], weight_sems.at[2, k]),
         ]
 
     lax.fori_loop(0, pairs, pair_step, 0)
@@ -1803,9 +1993,9 @@
             copy.wait()
 
 
-def call_dense(second_norm, upstream, scale, returned, lift, mixed, expand, project, cid):
+def call_dense(second_norm, upstream, scale, returned, lift, mixed, expand, project, hidden_back, cid):
     count, features = second_norm.shape
-    tile = 512
+    tile = hidden_back.shape[2]
     pairs = expand.shape[1] // tile // 2
     tall, broad = (tile, features), (features, tile)
     outs = (
@@ -1825,12 +2015,13 @@
     return pl.pallas_call(
         dense_kernel,
         out_shape=shapes,
-        in_specs=[vmem] * 5 + [anywhere] * 3,
+        in_specs=[vmem] * 5 + [anywhere] * 4,
         out_specs=[anywhere] * 4 + [vmem] * 5,
         scratch_shapes=[
             pltpu.VMEM((count, features), wide),
             pltpu.VMEM((2 * pairs, *broad), low),
             pltpu.VMEM((2 * pairs, *tall), low),
+            pltpu.VMEM(hidden_back.shape, low),
             pltpu.VMEM((count, features), low),
             pltpu.VMEM((count, features), wide),
             pltpu.VMEM((count, features), wide),
@@ -1844,7 +2035,7 @@
             pltpu.VMEM((tile // 8, features), low),
             pltpu.VMEM((features // 8, tile), low),
             dma((1,)),
-            dma((2, 2 * pairs)),
+            dma((3, 2 * pairs)),
             dma((2, count // 512)),
             dma((2,)),
             dma((pairs, 2)),
@@ -1855,7 +2046,7 @@
         compiler_params=pltpu.CompilerParams(
             collective_id=cid, has_side_effects=True, vmem_limit_bytes=60 * 1024 * 1024
         ),
-    )(second_norm, upstream, scale, returned, lift, mixed, expand, project)
+    )(second_norm, upstream, scale, returned, lift, mixed, expand, project, hidden_back)
 
 
 def shards(
@@ -1943,10 +2134,16 @@
     shape = (steps, side, 4 * 128)
     kept = ((shape, low), (shape, wide), (shape, low), (shape, wide))
     scalars = (region_sizes, region_starts)
-    mixed, second_norm, *stream = call_filter(
+    hidden, tile = dense_lift.shape[0], 512
+    mixed, second_norm, *stream, hidden_back = call_filter(
         forward_kernel,
         sizes,
-        (((count, features), wide), ((count, features), low), *kept),
+        (
+            ((count, features), wide),
+            ((count, features), low),
+            *kept,
+            ((hidden // tile, count, tile), low),
+        ),
         1,
         (
             flat_tokens,
@@ -1961,11 +2158,13 @@
             ahead,
             behind,
             eye,
+            upstream,
+            dense_project,
         ),
         scalars,
-        (),
-        range(6),
-        forward_scratch(sizes, kept),
+        (12, 13),
+        range(7),
+        forward_scratch(sizes, kept, hidden, tile),
     )
     output, mixed_back, *tiles, part_sums = call_dense(
         second_norm,
@@ -1976,6 +2175,7 @@
         mixed,
         dense_expand,
         dense_project,
+        hidden_back,
         3,
     )
     slope, project_sum, expand_sum, gathered, gathered_bias, sums = call_filter(
@@ -2009,22 +2209,16 @@
         range(3),
         backward_scratch(sizes, kept, tiles[0].shape[0], 3),
     )
-    biases = gathered_bias[:, :, 0].reshape(2, blocks, 2, block_size).swapaxes(1, 2)
-    return (
-        output.reshape(tokens.shape),
-        slope.reshape(tokens.shape),
-        sums[0],
-        sums[1],
-        gathered[0],
-        biases[0],
-        gathered[1],
-        biases[1],
-        sums[2],
-        sums[3],
-        expand_sum.astype(wide),
-        sums[5 : 5 + dense_lift.shape[0] // tiles[0].shape[0], : tiles[0].shape[0]].reshape(-1),
-        project_sum.astype(wide),
-        sums[4],
+    return tuple(
+        call_finish(
+            project_sum,
+            expand_sum,
+            slope.reshape(tokens.shape),
+            output.reshape(tokens.shape),
+            gathered,
+            gathered_bias,
+            sums,
+        )
     )
 
 

time: 317 us -> 309 us (0.975)
  Pallas kernels: 288 us -> 304 us
  other arithmetic: 13.6 us -> 1.68 us
  local copies, waits for them, and re-layouts: 14 us -> 2.44 us
    pallas_call x0 -> x1, Pallas kernels: none -> 15.6 us  [call_finish(): pl.pallas_call(finish_kernel, out_shape=shapes, in_specs=[anywhere] * 4 +...]
    convert_element_type x2 -> x0, other arithmetic: 11.9 us -> none  [the longest x1 7.43 us: shards(): expand_sum.astype(wide)]
    unnamed x10 -> x0, local copies, waits for them, and re-layouts: 4.13 us -> none
    squeeze x2 -> x0, local copies, waits for them, and re-layouts: 3.38 us -> none  [the longest x1 2.77 us: shards(): gathered[1]]
    slice x3 -> x0, local copies, waits for them, and re-layouts: 3.36 us -> none  [the longest x1 1.65 us: shards(): sums[4]]
where the time goes in v6:
time: 309 us
  Pallas kernels  304 us (98%)
    pallas_call x2, Pallas kernels, call_filter(): pl.pallas_call(functools.partial(body, sizes), out_shape=shapes, in_specs...  235 us
    pallas_call x1, Pallas kernels, call_dense(): pl.pallas_call(dense_kernel, out_shape=shapes, in_specs=[vmem] * 5 + [any...  53.2 us
    pallas_call x1, Pallas kernels, call_finish(): pl.pallas_call(finish_kernel, out_shape=shapes, in_specs=[anywhere] * 4 +...  15.6 us

profile of v6, /device:TPU:0, one launch (start us, length us, event | category | flops | bytes accessed | tf_op | source)
XLA Modules:
  0.0 309.0 jit_solution(16951704527146496388)
XLA Ops:
  0.7 0.7 fusion
  1.4 0.1 stack_reshape.6
  1.5 0.1 stack_reshape.7
  1.6 0.8 dynamic-slice_bitcast_fusion.1
  2.4 0.8 copy.39.refs_8_
  3.1 0.8 fusion.2
  3.9 0.1 maximum_bitcast_fusion
  4.0 0.1 maximum_bitcast_fusion.1
  4.1 0.7 pad_maximum_fusion.refs_7_.refs_5_
  4.8 100.2 %shard_map.326 = (f32[1024,768]{1,0:T(8,128)}, bf16[1024,768]{1,0:T(8,128)(2,1)}, bf16[8,192,512]{2,1,0:T(8,128)(2,1)}, f32[8,192,512]{2,1,0:T(8,128)}, bf16[8,1...) custom-call(s32[2,2]{1,0:T(2,128)} %refs_0_.3, s32[2]{0:T(128)} %refs_1_.3, ...), custom_call_target="tpu_custom_call" | custom-call | tf_op jit(solution)/shard_map/pallas_call | solution.py:1519
  105.1 53.2 %shard_map.327 = (bf16[1024,768]{1,0:T(8,128)(2,1)}, f32[1024,768]{1,0:T(8,128)}, bf16[512,768]{1,0:T(8,128)(2,1)}, bf16[768,512]{1,0:T(8,128)(2,1)}, bf16[32,76...) custom-call(bf16[1024,768]{1,0:T(8,128)(2,1)} %get-tuple-element.36., ...), custom_call_target="tpu_custom_call" | custom-call | tf_op jit(solution)/shard_map/pallas_call | solution.py:2015
  158.3 134.9 %shard_map.328 = (f32[1024,768]{1,0:T(8,128)}, bf16[3072,768]{1,0:T(8,128)(2,1)}, bf16[768,3072]{1,0:T(8,128)(2,1)}, f32[2,2,8,96,96]{4,3,2,1,0:T(8,128)}, f32[2,8,8,192]{3,2,1,0:T(8,128)}, /*index=5*/f32[16,768]{1,0:T(8,128)}) custom-call(s32[2,2]{1,0:T(2,128)} %refs_0_.3, s32[2]{0:T(128)} %refs_1_.3, bf16[1024,768]{1,0:T(8,128)(2,1)} %bitcast.19, ...), custom_call_target="tpu_custom_call" | custom-call | tf_op jit(solution)/shard_map/pallas_call | solution.py:1519
  293.2 15.6 %shard_map.329 = (bf16[2,8,64,768]{3,2,1,0:T(8,128)(2,1)}, f32[2,8,64,768]{3,2,1,0:T(8,128)}, f32[768]{0:T(1024)}, f32[768]{0:T(1024)}, f32[2,8,96,96]{3,2,1,0:T...) custom-call(bf16[3072,768]{1,0:T(8,128)(2,1)} %get-tuple-element.51., ...), custom_call_target="tpu_custom_call" | custom-call | tf_op jit(solution)/shard_map/pallas_call | solution.py:1720
  (1 shorter events, 0.0 us)

commit v7 on v6

--- a/solution.py
+++ b/solution.py
@@ -486,6 +486,13 @@
     return out
 
 
+def cross(value, mask, bits):
+    out = 0
+    for k in range(bits):
+        out = out + (value // (1 << k) + mask // (1 << k)) % 2 * (1 << k)
+    return out
+
+
 def greet(chips, cols):
     row = lax.axis_index("rows")
     core = row % 2
@@ -591,9 +598,27 @@
             send_piece(src, got.at[me], send_a.at[place], recv_a.at[me], target, me, core, cols)
     tick("sent")
 
+    middle_point = points // 2
+
+    def swap_half(k, first):
+        place = pl.ds(pl.multiple_of(first, middle_point), middle_point)
+        return pltpu.make_async_remote_copy(
+            src_ref=zonal.at[1 - core, place],
+            dst_ref=zonal_got.at[place],
+            send_sem=send_b.at[k],
+            recv_sem=recv_b.at[k],
+            device_id=chip_device(me, 1 - core, cols),
+            device_id_type=MESH,
+        )
+
+    swaps = [
+        swap_half(0, home * middle_point),
+        swap_half(1, (1 - home) * middle_point),
+    ]
+
     def zonal_step(index, carry):
         tick("arrival", index)
-        chip = (index + home * senders // regions) % senders
+        chip = cross(me // cols, index, senders.bit_length() - 1)
         for col in range(cols):
             await_piece(got.at[chip * cols + col], recv_a.at[chip * cols + col])
         for pair in range(pairs):
@@ -603,18 +628,15 @@
             y = dot(x, table_in[...]).astype(low)
             for part in range(2):
                 zonal[part, chip * pairs + pair] = y[:, part * lanes : (part + 1) * lanes]
+
+        @pl.when(index == senders // 2 - 1)
+        def _():
+            swaps[0].start()
+
         return carry
 
     lax.fori_loop(0, senders, zonal_step, 0)
-    swap = pltpu.make_async_remote_copy(
-        src_ref=zonal.at[1 - core],
-        dst_ref=zonal_got,
-        send_sem=send_b,
-        recv_sem=recv_b,
-        device_id=chip_device(me, 1 - core, cols),
-        device_id_type=MESH,
-    )
-    swap.start()
+    swaps[1].start()
     tick("zonal")
 
     def widen(source, first):
@@ -626,7 +648,8 @@
         lax.fori_loop(0, points, step, 0)
 
     widen(lambda point: zonal[core, point], core * points)
-    swap.wait()
+    for swap in swaps:
+        swap.wait()
     widen(lambda point: zonal_got[point], (1 - core) * points)
     modes = lanes // 4
 
@@ -702,7 +725,7 @@
     await_piece(sibling.at[1 - core], recv_c)
 
     def column_step(index, carry):
-        chip = (index + (home + 1) * senders // regions) % senders
+        chip = cross(me // cols, senders - 1 - index, senders.bit_length() - 1)
         for pair in range(pairs):
             point = chip * pairs + pair
             x = jnp.concatenate([sibling[0, point], sibling[1, point]], 1)
@@ -711,8 +734,8 @@
                 leaving[chip * cols + col, :, pair * lanes : (pair + 1) * lanes] = y[
                     :, col * lanes : (col + 1) * lanes
                 ]
-        for col in range(cols):
-            target = chip * cols + col
+        for turn in range(cols):
+            target = chip * cols + (me + turn + 1) % cols
             dst = coming.at[
                 me // blocks, pl.ds(pl.multiple_of(me % blocks * block_size, 32), block_size)
             ]
@@ -767,8 +790,8 @@
         pltpu.VMEM((regions, features, tokens), low),
         pltpu.SemaphoreType.DMA((chips,)),
         pltpu.SemaphoreType.DMA((chips,)),
-        pltpu.SemaphoreType.DMA,
-        pltpu.SemaphoreType.DMA,
+        pltpu.SemaphoreType.DMA((2,)),
+        pltpu.SemaphoreType.DMA((2,)),
         pltpu.SemaphoreType.DMA,
         pltpu.SemaphoreType.DMA,
         pltpu.SemaphoreType.DMA((chips,)),

time: 309 us -> 300 us (0.971)
  Pallas kernels: 304 us -> 295 us
    pallas_call x1, Pallas kernels: 53.2 us -> 47.7 us  [call_dense(): pl.pallas_call(dense_kernel, out_shape=shapes, in_specs=[vmem] * 5 + [any...]
    pallas_call x2, Pallas kernels: 235 us -> 231 us  [call_filter(): pl.pallas_call(functools.partial(body, sizes), out_shape=shapes, in_specs...]
where the time goes in v7:
time: 300 us
  Pallas kernels  295 us (98%)
    pallas_call x2, Pallas kernels, call_filter(): pl.pallas_call(functools.partial(body, sizes), out_shape=shapes, in_specs...  231 us
    pallas_call x1, Pallas kernels, call_dense(): pl.pallas_call(dense_kernel, out_shape=shapes, in_specs=[vmem] * 5 + [any...  47.7 us
    pallas_call x1, Pallas kernels, call_finish(): pl.pallas_call(finish_kernel, out_shape=shapes, in_specs=[anywhere] * 4 +...  15.6 us

profile of v7, /device:TPU:0, one launch (start us, length us, event | category | flops | bytes accessed | tf_op | source)
XLA Modules:
  0.0 299.5 jit_solution(814678792810574766)
XLA Ops:
  0.7 0.7 fusion
  1.4 0.1 stack_reshape.6
  1.5 0.1 stack_reshape.7
  1.6 0.8 dynamic-slice_bitcast_fusion.1
  2.4 0.8 copy.39.refs_8_
  3.1 0.8 fusion.2
  3.9 0.1 maximum_bitcast_fusion
  4.0 0.1 maximum_bitcast_fusion.1
  4.1 0.7 pad_maximum_fusion.refs_7_.refs_5_
  4.8 99.3 %shard_map.326 = (f32[1024,768]{1,0:T(8,128)}, bf16[1024,768]{1,0:T(8,128)(2,1)}, bf16[8,192,512]{2,1,0:T(8,128)(2,1)}, f32[8,192,512]{2,1,0:T(8,128)}, bf16[8,1...) custom-call(s32[2,2]{1,0:T(2,128)} %refs_0_.3, s32[2]{0:T(128)} %refs_1_.3, ...), custom_call_target="tpu_custom_call" | custom-call | tf_op jit(solution)/shard_map/pallas_call | solution.py:1542
  104.1 47.7 %shard_map.327 = (bf16[1024,768]{1,0:T(8,128)(2,1)}, f32[1024,768]{1,0:T(8,128)}, bf16[512,768]{1,0:T(8,128)(2,1)}, bf16[768,512]{1,0:T(8,128)(2,1)}, bf16[32,76...) custom-call(bf16[1024,768]{1,0:T(8,128)(2,1)} %get-tuple-element.36., ...), custom_call_target="tpu_custom_call" | custom-call | tf_op jit(solution)/shard_map/pallas_call | solution.py:2038
  151.8 131.9 %shard_map.328 = (f32[1024,768]{1,0:T(8,128)}, bf16[3072,768]{1,0:T(8,128)(2,1)}, bf16[768,3072]{1,0:T(8,128)(2,1)}, f32[2,2,8,96,96]{4,3,2,1,0:T(8,128)}, f32[2,8,8,192]{3,2,1,0:T(8,128)}, /*index=5*/f32[16,768]{1,0:T(8,128)}) custom-call(s32[2,2]{1,0:T(2,128)} %refs_0_.3, s32[2]{0:T(128)} %refs_1_.3, bf16[1024,768]{1,0:T(8,128)(2,1)} %bitcast.19, ...), custom_call_target="tpu_custom_call" | custom-call | tf_op jit(solution)/shard_map/pallas_call | solution.py:1542
  283.7 15.6 %shard_map.329 = (bf16[2,8,64,768]{3,2,1,0:T(8,128)(2,1)}, f32[2,8,64,768]{3,2,1,0:T(8,128)}, f32[768]{0:T(1024)}, f32[768]{0:T(1024)}, f32[2,8,96,96]{3,2,1,0:T...) custom-call(bf16[3072,768]{1,0:T(8,128)(2,1)} %get-tuple-element.51., ...), custom_call_target="tpu_custom_call" | custom-call | tf_op jit(solution)/shard_map/pallas_call | solution.py:1743
  (1 shorter events, 0.0 us)

commit v8 on v7

--- a/solution.py
+++ b/solution.py
@@ -621,13 +621,24 @@
         chip = cross(me // cols, index, senders.bit_length() - 1)
         for col in range(cols):
             await_piece(got.at[chip * cols + col], recv_a.at[chip * cols + col])
+        x = jnp.concatenate(
+            [
+                jnp.concatenate(
+                    [
+                        got[chip * cols + col, :, pair * lanes : (pair + 1) * lanes]
+                        for col in range(cols)
+                    ],
+                    1,
+                )
+                for pair in range(pairs)
+            ],
+            0,
+        )
+        y = dot(x, table_in[...]).astype(low)
         for pair in range(pairs):
-            x = jnp.concatenate(
-                [got[chip * cols + col, :, pair * lanes : (pair + 1) * lanes] for col in range(cols)], 1
-            )
-            y = dot(x, table_in[...]).astype(low)
+            rows = slice(pair * block_size, (pair + 1) * block_size)
             for part in range(2):
-                zonal[part, chip * pairs + pair] = y[:, part * lanes : (part + 1) * lanes]
+                zonal[part, chip * pairs + pair] = y[rows, part * lanes : (part + 1) * lanes]
 
         @pl.when(index == senders // 2 - 1)
         def _():
@@ -662,7 +673,7 @@
             flat[i, pl.ds(c, modes, stride=half), :] = y[i * modes : (i + 1) * modes]
         return carry
 
-    lax.fori_loop(0, half, turn_step, 0, unroll=4)
+    lax.fori_loop(0, half, turn_step, 0, unroll=8)
     tick("turned")
 
     def mode_step(step, carry):
@@ -692,7 +703,7 @@
             ]
         return carry
 
-    lax.fori_loop(0, half, return_step, 0, unroll=4)
+    lax.fori_loop(0, half, return_step, 0, unroll=8)
     tick("returned")
 
     def narrow(store, first):
@@ -726,13 +737,19 @@
 
     def column_step(index, carry):
         chip = cross(me // cols, senders - 1 - index, senders.bit_length() - 1)
+        x = jnp.concatenate(
+            [
+                jnp.concatenate([sibling[part, chip * pairs + pair] for part in range(2)], 1)
+                for pair in range(pairs)
+            ],
+            0,
+        )
+        y = dot(x, table_out[...]).astype(low)
         for pair in range(pairs):
-            point = chip * pairs + pair
-            x = jnp.concatenate([sibling[0, point], sibling[1, point]], 1)
-            y = dot(x, table_out[...]).astype(low)
+            rows = slice(pair * block_size, (pair + 1) * block_size)
             for col in range(cols):
                 leaving[chip * cols + col, :, pair * lanes : (pair + 1) * lanes] = y[
-                    :, col * lanes : (col + 1) * lanes
+                    rows, col * lanes : (col + 1) * lanes
                 ]
         for turn in range(cols):
             target = chip * cols + (me + turn + 1) % cols
@@ -888,7 +905,7 @@
     regions, blocks, block_size, chips, cols, tokens = sizes
     me, core = greet(chips, cols)
     sent, coming = work[0], work[-1]
-    piece = 128
+    piece = 256
     steps = kept_hbm[0].shape[0]
     cols_here = 128 // cols
     gain, shift, scale, center = (
@@ -1228,7 +1245,7 @@
     spot = place_of(lax.axis_index("rows"), lax.axis_index("cols"))
     block = me % blocks
     sent, coming = work[0], work[-1]
-    piece = 128
+    piece = 256
     cols_here = 128 // cols
     late[...] = jnp.zeros_like(late)
     vector_sum[...] = sums_ref[...]

time: 300 us -> 298 us (level)
  no operation moved by 1% of the time
where the time goes in v8:
time: 298 us
  Pallas kernels  293 us (98%)
    pallas_call x2, Pallas kernels, call_filter(): pl.pallas_call(functools.partial(body, sizes), out_shape=shapes, in_specs...  230 us
    pallas_call x1, Pallas kernels, call_dense(): pl.pallas_call(dense_kernel, out_shape=shapes, in_specs=[vmem] * 5 + [any...  47.6 us
    pallas_call x1, Pallas kernels, call_finish(): pl.pallas_call(finish_kernel, out_shape=shapes, in_specs=[anywhere] * 4 +...  15.6 us

profile of v8, /device:TPU:0, one launch (start us, length us, event | category | flops | bytes accessed | tf_op | source)
XLA Modules:
  0.0 298.0 jit_solution(6895925590675777512)
XLA Ops:
  0.7 0.7 fusion
  1.4 0.1 stack_reshape.6
  1.5 0.1 stack_reshape.7
  1.6 0.8 dynamic-slice_bitcast_fusion.1
  2.4 0.8 copy.39.refs_8_
  3.1 0.8 fusion.2
  3.9 0.1 maximum_bitcast_fusion
  4.0 0.1 maximum_bitcast_fusion.1
  4.1 0.7 pad_maximum_fusion.refs_7_.refs_5_
  4.8 98.1 %shard_map.326 = (f32[1024,768]{1,0:T(8,128)}, bf16[1024,768]{1,0:T(8,128)(2,1)}, bf16[8,192,512]{2,1,0:T(8,128)(2,1)}, f32[8,192,512]{2,1,0:T(8,128)}, bf16[8,1...) custom-call(s32[2,2]{1,0:T(2,128)} %refs_0_.3, s32[2]{0:T(128)} %refs_1_.3, ...), custom_call_target="tpu_custom_call" | custom-call | tf_op jit(solution)/shard_map/pallas_call | solution.py:1559
  102.9 47.6 %shard_map.327 = (bf16[1024,768]{1,0:T(8,128)(2,1)}, f32[1024,768]{1,0:T(8,128)}, bf16[512,768]{1,0:T(8,128)(2,1)}, bf16[768,512]{1,0:T(8,128)(2,1)}, bf16[32,76...) custom-call(bf16[1024,768]{1,0:T(8,128)(2,1)} %get-tuple-element.36., ...), custom_call_target="tpu_custom_call" | custom-call | tf_op jit(solution)/shard_map/pallas_call | solution.py:2055
  150.5 131.7 %shard_map.328 = (f32[1024,768]{1,0:T(8,128)}, bf16[3072,768]{1,0:T(8,128)(2,1)}, bf16[768,3072]{1,0:T(8,128)(2,1)}, f32[2,2,8,96,96]{4,3,2,1,0:T(8,128)}, f32[2,8,8,192]{3,2,1,0:T(8,128)}, /*index=5*/f32[16,768]{1,0:T(8,128)}) custom-call(s32[2,2]{1,0:T(2,128)} %refs_0_.3, s32[2]{0:T(128)} %refs_1_.3, bf16[1024,768]{1,0:T(8,128)(2,1)} %bitcast.19, ...), custom_call_target="tpu_custom_call" | custom-call | tf_op jit(solution)/shard_map/pallas_call | solution.py:1559
  282.2 15.6 %shard_map.329 = (bf16[2,8,64,768]{3,2,1,0:T(8,128)(2,1)}, f32[2,8,64,768]{3,2,1,0:T(8,128)}, f32[768]{0:T(1024)}, f32[768]{0:T(1024)}, f32[2,8,96,96]{3,2,1,0:T...) custom-call(bf16[3072,768]{1,0:T(8,128)(2,1)} %get-tuple-element.51., ...), custom_call_target="tpu_custom_call" | custom-call | tf_op jit(solution)/shard_map/pallas_call | solution.py:1760
  (1 shorter events, 0.0 us)
